TPU v7x, 256 devices: a whole 4x4x8 slice. The times are simulated.
256 devices in a mesh: lon: 16 (over x_lo, z), lat: 8 (over y, x_hi), ens: 2 (over core).
Axes of the slice: x: 4 (x_hi: 2, x_lo: 2; x = x_hi * 2 + x_lo), y: 4, z: 8, core: 2. Of those that a mesh axis runs over, the one named last changes fastest.
Arguments:
- inputs: bfloat16 [2, 2, 144, 384, 192], P('ens', None, 'lat', 'lon'), may hold values from -6 to 6
- cotangent: bfloat16 [2, 2, 144, 384, 192], P('ens', None, 'lat', 'lon'), may hold values from -6 to 6
- mask_ids: int32 [2, 144, 384], P(None, 'lat', 'lon'), may hold values from 0 to 3
- norm_gain: float32 [192], replicated, may hold values from 0.5 to 1.5
- project_in: bfloat16 [192, 576], replicated, may hold values from -0.4375 to 0.4375
- project_out: bfloat16 [192, 192], replicated, may hold values from -0.4375 to 0.4375
- bias_table: float32 [24, 6, 3312], replicated, may hold values from -4 to 265
Outputs:
- block_out: bfloat16 [2, 2, 144, 384, 192], P('ens', None, 'lat', 'lon')
- inputs_grad: bfloat16 [2, 2, 144, 384, 192], P('ens', None, 'lat', 'lon')
- project_in_grad: float32 [192, 576], replicated
- project_out_grad: float32 [192, 192], replicated
- gain_grad: float32 [192], replicated
- table_grad: float32 [24, 6, 3312], replicated
All inputs are finite; a program needn't handle non-finite values.
Results may differ from a plain program's by a relative error of at most 0.014.
Values may be sent and summed in bfloat16 or wider, within the bound.
No kernel may reach another device: no remote copies, remote signals or barrier semaphores. Data moves between devices by JAX's collectives and lax.ppermute only.
A program may use at most 128 MiB of HBM per device.

v0:
```python
import jax
import jax.numpy as jnp
from jax import lax
from jax.sharding import PartitionSpec as P

WL = 2
WLAT = 6
WLON = 12


EPS = 1e-05


def passed_along(x, axis, by):
    peers = lax.axis_size(axis)
    return lax.ppermute(x, axis, [(i, (i + by) % peers) for i in range(peers)])


def offset_table(width):
    position = jnp.arange(width, dtype=jnp.int32)
    delta = position[:, None] - position[None, :] + (width - 1)
    return (delta[None] == jnp.arange(2 * width - 1, dtype=jnp.int32)[:, None, None]).astype(
        jnp.float32
    )


def expand_bias(compact):
    lead = compact.shape[:-1]
    count = len(lead)
    shaped = compact.reshape(lead + (WL, WL, WLAT, WLAT, 2 * WLON - 1))
    full = jnp.einsum(
        "...abcdx,xef->...abcdef", shaped, offset_table(WLON), precision=lax.Precision.HIGHEST
    )
    order = tuple(range(count)) + (count, count + 2, count + 4, count + 1, count + 3, count + 5)
    points = WL * WLAT * WLON
    return full.transpose(order).reshape(lead + (points, points))


def compress_bias(full):
    lead = full.shape[:-2]
    count = len(lead)
    shaped = full.reshape(lead + (WL, WLAT, WLON, WL, WLAT, WLON))
    order = tuple(range(count)) + (count, count + 3, count + 1, count + 4, count + 2, count + 5)
    shaped = shaped.transpose(order)
    small = jnp.einsum(
        "...abcdef,xef->...abcdx", shaped, offset_table(WLON), precision=lax.Precision.HIGHEST
    )
    return small.reshape(lead + (-1,))


def to_windows(volume, win_depth, win_rows, win_cols):
    members, levels, lat_rows, lon_cols, channels = volume.shape
    shaped = volume.reshape(
        members,
        levels // win_depth,
        win_depth,
        lat_rows // win_rows,
        win_rows,
        lon_cols // win_cols,
        win_cols,
        channels,
    )
    shaped = shaped.transpose(0, 1, 3, 5, 2, 4, 6, 7)
    return shaped.reshape(
        members,
        levels // win_depth,
        lat_rows // win_rows,
        lon_cols // win_cols,
        win_depth * win_rows * win_cols,
        channels,
    )


def from_windows(window_set, win_depth, win_rows, win_cols):
    members, lev_win, lat_win, lon_win, points, channels = window_set.shape
    shaped = window_set.reshape(
        members, lev_win, lat_win, lon_win, win_depth, win_rows, win_cols, channels
    )
    shaped = shaped.transpose(0, 1, 4, 2, 5, 3, 6, 7)
    return shaped.reshape(
        members, lev_win * win_depth, lat_win * win_rows, lon_win * win_cols, channels
    )


def window_pass(seq_in, seq_cot, region, bias_win, project_in, project_out):
    f32 = jnp.float32
    bf16 = jnp.bfloat16
    num_win, points, channels = seq_in.shape
    head_num = bias_win.shape[1]
    head_dim = channels // head_num
    factor = head_dim ** (-0.5)
    triple = jnp.einsum("npc,cf->npf", seq_in, project_in, preferred_element_type=f32).astype(bf16)
    triple = triple.reshape(num_win, points, 3, head_num, head_dim)
    queries, key_vec, val_vec = (triple[:, :, 0], triple[:, :, 1], triple[:, :, 2])
    scores = (
        jnp.einsum("nqhd,nkhd->nhqk", queries, key_vec, preferred_element_type=f32) * factor
        + bias_win
    )
    allowed = (region[:, :, None] == region[:, None, :])[:, None]
    scores = jnp.where(allowed, scores, -jnp.inf)
    peak_val = jnp.max(scores, axis=-1, keepdims=True)
    raised = jnp.exp(scores - peak_val)
    prob_full = raised / jnp.sum(raised, axis=-1, keepdims=True)
    prob_low = prob_full.astype(bf16)
    mixed = jnp.einsum("nhqk,nkhd->nqhd", prob_low, val_vec, preferred_element_type=f32).astype(
        bf16
    )
    mixed = mixed.reshape(num_win, points, channels)
    attended = jnp.einsum("npc,cd->npd", mixed, project_out, preferred_element_type=f32).astype(
        bf16
    )
    out_grad = jnp.einsum("npc,npd->cd", mixed, seq_cot, preferred_element_type=f32)
    grad_mixed = jnp.einsum("npd,cd->npc", seq_cot, project_out, preferred_element_type=f32).astype(
        bf16
    )
    grad_mixed = grad_mixed.reshape(num_win, points, head_num, head_dim)
    grad_probs = jnp.einsum("nqhd,nkhd->nhqk", grad_mixed, val_vec, preferred_element_type=f32)
    grad_value = jnp.einsum(
        "nhqk,nqhd->nkhd", prob_low, grad_mixed, preferred_element_type=f32
    ).astype(bf16)
    grad_scores = prob_full * (grad_probs - jnp.sum(prob_full * grad_probs, axis=-1, keepdims=True))
    grad_low = grad_scores.astype(bf16)
    grad_query = (
        jnp.einsum("nhqk,nkhd->nqhd", grad_low, key_vec, preferred_element_type=f32) * factor
    ).astype(bf16)
    grad_key = (
        jnp.einsum("nhqk,nqhd->nkhd", grad_low, queries, preferred_element_type=f32) * factor
    ).astype(bf16)
    grad_triple = jnp.stack([grad_query, grad_key, grad_value], axis=2).reshape(
        num_win, points, 3 * channels
    )
    in_grad = jnp.einsum("npc,npf->cf", seq_in, grad_triple, preferred_element_type=f32)
    grad_seq = jnp.einsum(
        "npf,cf->npc", grad_triple, project_in, preferred_element_type=f32
    ).astype(jnp.bfloat16)
    return (attended, grad_seq, in_grad, out_grad, grad_scores)


def run_region(window_set, cot_set, regions, band_bias, project_in, project_out):
    members, lev_win, lat_win, lon_win, points, channels = window_set.shape
    num_win = members * lev_win * lat_win * lon_win
    grid_shape = (members, lev_win, lat_win, lon_win)
    tail = band_bias.shape[2:]
    region_rows = regions[None].reshape(num_win, points)
    bias_win = jnp.broadcast_to(band_bias[None, :, :, None], grid_shape + tail).reshape(
        (num_win,) + tail
    )
    attended, grad_seq, in_grad, out_grad, grad_scores = window_pass(
        window_set.reshape(num_win, points, channels),
        cot_set.reshape(num_win, points, channels),
        region_rows,
        bias_win,
        project_in,
        project_out,
    )
    row_sums = jnp.sum(grad_scores.reshape(grid_shape + tail), axis=(0, 3))
    return (
        attended.reshape(window_set.shape),
        grad_seq.reshape(window_set.shape),
        in_grad,
        out_grad,
        row_sums,
    )


def roll_in(field_one, field_two):
    half_lat = WLAT // 2
    half_lon = WLON // 2
    strip_pair = jnp.stack([field_one[:, :, :, :half_lon], field_two[:, :, :, :half_lon]])
    strip_pair = passed_along(strip_pair, "lon", -1)
    field_one = jnp.concatenate([field_one[:, :, :, half_lon:], strip_pair[0]], axis=3)
    field_two = jnp.concatenate([field_two[:, :, :, half_lon:], strip_pair[1]], axis=3)
    strip_pair = jnp.stack([field_one[:, :, :half_lat], field_two[:, :, :half_lat]])
    strip_pair = passed_along(strip_pair, "lat", -1)
    field_one = jnp.concatenate([field_one[:, :, half_lat:], strip_pair[0]], axis=2)
    field_two = jnp.concatenate([field_two[:, :, half_lat:], strip_pair[1]], axis=2)
    return (field_one, field_two)


def roll_out(field_one, field_two):
    half_lat = WLAT // 2
    half_lon = WLON // 2
    strip_pair = jnp.stack([field_one[:, :, -half_lat:], field_two[:, :, -half_lat:]])
    strip_pair = passed_along(strip_pair, "lat", 1)
    field_one = jnp.concatenate([strip_pair[0], field_one[:, :, :-half_lat]], axis=2)
    field_two = jnp.concatenate([strip_pair[1], field_two[:, :, :-half_lat]], axis=2)
    strip_pair = jnp.stack([field_one[:, :, :, -half_lon:], field_two[:, :, :, -half_lon:]])
    strip_pair = passed_along(strip_pair, "lon", 1)
    field_one = jnp.concatenate([strip_pair[0], field_one[:, :, :, :-half_lon]], axis=3)
    field_two = jnp.concatenate([strip_pair[1], field_two[:, :, :, :-half_lon]], axis=3)
    return (field_one, field_two)


def local(inputs, cotangent, mask_ids, norm_gain, project_in, project_out, bias_table):
    f32 = jnp.float32
    members, levels, lat_rows, lon_cols, channels = inputs.shape
    lev_win, lat_win, lon_win = (levels // WL, lat_rows // WLAT, lon_cols // WLON)
    half_lev, half_lat, half_lon = (WL // 2, WLAT // 2, WLON // 2)
    table_rows = bias_table.reshape(
        lev_win, bias_table.shape[0] // lev_win, bias_table.shape[1], bias_table.shape[2]
    )
    band_start = lax.axis_index("lat") * lat_win
    band_bias = expand_bias(lax.dynamic_slice_in_dim(table_rows, band_start, lat_win, 1))
    values = inputs.astype(f32)
    average = jnp.mean(values, axis=-1, keepdims=True)
    center = values - average
    inverse = lax.rsqrt(jnp.mean(center * center, axis=-1, keepdims=True) + EPS)
    normal_part = center * inverse
    normed = (normal_part * norm_gain).astype(jnp.bfloat16)
    lifted = jnp.roll(normed, -half_lev, axis=1)
    lifted_cot = jnp.roll(cotangent, -half_lev, axis=1)
    regions = to_windows(mask_ids[None, :, :, :, None], WL, WLAT, WLON)[0, :, :, :, :, 0]
    shifted, shifted_cot = roll_in(lifted, lifted_cot)
    attended, grad_seq, in_grad, out_grad, picked = run_region(
        to_windows(shifted, WL, WLAT, WLON),
        to_windows(shifted_cot, WL, WLAT, WLON),
        regions,
        band_bias,
        project_in,
        project_out,
    )
    local_grad = compress_bias(picked)
    layout_att = from_windows(attended, WL, WLAT, WLON)
    layout_grad = from_windows(grad_seq, WL, WLAT, WLON)
    back_att, back_grad = roll_out(layout_att, layout_grad)
    back_att = jnp.roll(back_att, half_lev, axis=1)
    back_grad = jnp.roll(back_grad, half_lev, axis=1)
    block_out = (values + back_att.astype(f32)).astype(jnp.bfloat16)
    grad_wide = back_grad.astype(f32)
    scaled = grad_wide * norm_gain
    gain_part = jnp.sum(grad_wide * normal_part, axis=(0, 1, 2, 3))
    grad_part = inverse * (
        scaled
        - jnp.mean(scaled, axis=-1, keepdims=True)
        - normal_part * jnp.mean(scaled * normal_part, axis=-1, keepdims=True)
    )
    inputs_grad = (cotangent.astype(f32) + grad_part).astype(jnp.bfloat16)
    placed = lax.dynamic_update_slice_in_dim(
        jnp.zeros(table_rows.shape, f32), local_grad, band_start, 1
    )
    in_total, out_total, gain_total, table_total = lax.psum(
        (in_grad, out_grad, gain_part, placed), ("lon", "lat", "ens")
    )
    table_total = table_total.reshape(bias_table.shape)
    return (block_out, inputs_grad, in_total, out_total, gain_total, table_total)


def solution(mesh):
    return jax.shard_map(
        local,
        mesh=mesh,
        in_specs=(
            P("ens", None, "lat", "lon", None),
            P("ens", None, "lat", "lon", None),
            P(None, "lat", "lon"),
            P(),
            P(),
            P(),
            P(),
        ),
        out_specs=(
            P("ens", None, "lat", "lon", None),
            P("ens", None, "lat", "lon", None),
            P(),
            P(),
            P(),
            P(),
        ),
        check_vma=False,
    )
```

profile of v0, /device:TPU:1, one launch (start us, length us, event | category | flops | bytes accessed | tf_op | source)
XLA Modules:
  0.0 487.7 jit_solution(5135713698320504451)
XLA Ops:
  13.1 2.6 multiply_convert_fusion
  18.7 7.5 %collective-permute-start = (bf16[2,1,2,18,6,192]{5,2,4,3,1,0:T(2,128)(2,1)}, bf16[2,1,2,18,6,192]{5,2,4,3,1,0:T(2,128)(2,1)}, u32[]{:S(2)}, u32[]{:S(2)}) collective-permute-start(bf16[2,1,2,18,6,192]{5,2,4,3,1,0:T(2,128)(2,1)} %pad_maximum_fusion.7), channel_id=1, source_target_pairs={{0,240},{16,0},{32,16},{48,32},{64,48},{80,64},{96,80},{112,96},{1... | collective-permute-start | bytes 497672 | tf_op jit(solution)/shard_map/ppermute | solution.py:16
  29.4 13.1 %convolution_bitcast_fusion = f32[1,3,6,2,6,12,2,6,12]{8,7,5,4,6,3,2,1,0:T(8,128)} fusion(f32[3,6,2,2,6,6,23,1]{6,5,4,3,2,1,0,7:T(8,128)S(1)} %reshape.245, s32[12,12]{1,0:T(8,128)S(1)} %subtract_add_fusion), kind=kOutput, calls=%fused_computation.3 | convolution fusion | flops 103019760 | bytes 1732032 | tf_op jit(solution)/shard_map/...abcdx,xef->...abcdef/dot_general | solution.py:31
  43.4 29.8 %copy.102 = f32[1,3,6,2,6,12,2,6,12]{5,4,3,8,7,6,2,1,0:T(8,128)} copy(f32[1,3,6,2,6,12,2,6,12]{8,7,5,4,6,3,2,1,0:T(8,128)} %convolution_bitcast_fusion) | data formatting | bytes 2985984 | tf_op jit(solution)/shard_map/broadcast_in_dim | solution.py:145
  73.2 14.9 %reshape.252 = f32[3,6,144,144]{2,3,1,0:T(8,128)} reshape(f32[1,3,6,2,6,12,2,6,12]{5,4,3,8,7,6,2,1,0:T(8,128)} %copy.102) | data formatting | bytes 2985984 | tf_op jit(solution)/shard_map/broadcast_in_dim | solution.py:145
  90.6 5.0 %collective-permute-start.1 = (bf16[2,1,2,3,24,192]{5,2,4,3,1,0:T(2,128)(2,1)S(1)}, bf16[2,1,2,3,24,192]{5,2,4,3,1,0:T(2,128)(2,1)S(1)}, u32[]{:S(2)}, u32[]{:S(2)}) collective-permute-start(bf16[2,1,2,3,24,192]{5,2,4,3,1,0:T(2,128)(2,1)S(1)} %pad_maximum_fusion.9), channel_id=1, source_target_pairs={{0,14},{2,0},{4,2},{6,4},{8,6},{10,8},{12,10},{14,12},{1,15},{3,1}... | collective-permute-start | bytes 331784 | tf_op jit(solution)/shard_map/ppermute | solution.py:16
  105.0 2.8 fusion.3
  107.8 3.8 fusion.69
  111.8 6.3 %fusion.26 = bf16[6,144,1,6,32]{1,4,3,0,2:T(8,128)(2,1)} fusion(bf16[6,144,6,32]{1,3,2,0:T(8,128)(2,1)} %bitcast.163, f32[6,6,144]{2,1,0:T(8,128)S(1)} %get-tuple-element.43, f32[6,6,144,144]{2,3,1,0:T(8,128)} %copy-done.3), kind=kOutput, calls=%fused_computation.32 | convolution fusion | flops 50186448 | bytes 3670272 | tf_op jit(solution)/shard_map/nhqk,nqhd->nkhd/dot_general | solution.py:118
  118.1 3.9 multiply_reduce_fusion
  123.8 2.3 fusion.29
  127.7 6.3 %fusion.14 = bf16[6,6,32,144]{3,2,1,0:T(8,128)(2,1)} fusion(bf16[6,144,3,6,32]{1,4,3,2,0:T(8,128)(2,1)S(1)} %bitcast.152, f32[6,6,144]{2,1,0:T(8,128)S(1)} %get-tuple-element.43, f32[6,6,144,144]{2,3,1,0:T(8,128)} %copy-done.3), kind=kOutput, calls=%fused_computation.25 | convolution fusion | flops 50186448 | bytes 11587584 | tf_op jit(solution)/shard_map/nhqk,nkhd->nqhd/dot_general | solution.py:105
  146.6 2.4 collective-permute-start.2
  149.0 4.7 reduce_sum.79
  153.8 3.7 copy.86
  157.4 14.1 %reshape.237 = f32[1,3,6,2,6,12,2,6,12]{8,7,6,5,4,3,2,1,0:T(8,128)} reshape(f32[3,6,144,144]{3,2,1,0:T(8,128)} %copy.86) | data formatting | bytes 2985984 | tf_op jit(solution)/shard_map/reshape | solution.py:42
  171.6 23.4 %fusion.5 = f32[3,6,2,2,6,6,23]{6,5,4,3,2,1,0:T(8,128)} fusion(s32[12,12]{1,0:T(8,128)S(1)} %subtract_add_fusion, f32[1,3,6,2,6,12,2,6,12]{8,7,6,5,4,3,2,1,0:T(8,128)} %reshape.237), kind=kOutput, calls=%fused_computation.12 | convolution fusion | flops 103019760 | bytes 1732032 | tf_op jit(solution)/shard_map/...abcdef,xef->...abcdx/dot_general | solution.py:45
  201.8 2.6 dynamic_update_slice.4
  211.1 5.1 %collective-permute-done.3 = bf16[2,1,2,18,6,192]{5,2,4,3,1,0:T(2,128)(2,1)} collective-permute-done((bf16[2,1,2,18,6,192]{5,2,4,3,1,0:T(2,128)(2,1)}, bf16[2,1,2,18,6,192]{5,2,4,3,1,0:T(2,128)(2,1)}, u32[]{:S(2)}, u32[]{:S(2)}) %collective-permute-start.3) | collective-permute-done | bytes 165920 | tf_op jit(solution)/shard_map/ppermute | solution.py:16
  219.6 3.5 fusion.45
  225.4 2.7 fusion.47
  229.8 77.7 %psum.30 = f32[192]{0:T(256)} all-reduce(f32[192]{0:T(256)S(1)} %get-tuple-element.18), channel_id=1, replica_groups=mesh['lon'=16,'lat'=8,'ens'=2] {'lon','lat','ens'}, use_global_device_ids=true, to_apply=%region_10.11 | all-reduce | flops 192 | bytes 1536 | tf_op jit(solution)/shard_map/psum | solution.py:241
  307.5 166.7 %all-reduce.3.cloned.1.call-done = (f32[192,576]{1,0:T(8,128)}, f32[192,192]{1,0:T(8,128)}, f32[24,6,3312]{2,0,1:T(8,128)}) async-done(((f32[192,576]{1,0:T(8,128)}, f32[192,192]{1,0:T(8,128)}, f32[24,6,3312]{2,0,1:T(8,128)}), (f32[192,576]{1,0:T(8,128)}, f32[192,192]{1,0:T(8,128)}, f32[24,6,3312]{2,0,1:T(8,128)})) %all-reduce.3.cloned.1.call-update) | async-done | bytes 2497552 | tf_op jit(solution)/shard_map/psum | solution.py:241
  477.7 2.9 copy.134
  (116 shorter events, 65.0 us)
Async XLA Ops:
  7.2 19.0 %copy-start = (f32[24,6,3312]{2,0,1:T(8,128)S(1)}, f32[24,6,3312]{2,0,1:T(8,128)}, u32[]{:S(2)}) copy-start(f32[24,6,3312]{2,0,1:T(8,128)} %param.13) | copy-start | bytes 5723140
  7.2 467.0 %all-reduce.3.cloned.1.call-start = ((), (), s32[]{:S(2)}) async-start(), calls=%async_computation | async-start | bytes 5210112 | tf_op jit(solution)/shard_map/psum | solution.py:241
  11.2 1.9 copy-start.9
  12.4 16.8 %copy-start.18 = (s32[2,18,24]{2,0,1:T(2,128)S(1)}, s32[2,18,24]{2,0,1:T(2,128)}, u32[]{:S(2)}) copy-start(s32[2,18,24]{2,0,1:T(2,128)} %param.9) | copy-start | bytes 10372
  18.7 70.3 %collective-permute-start = (bf16[2,1,2,18,6,192]{5,2,4,3,1,0:T(2,128)(2,1)}, bf16[2,1,2,18,6,192]{5,2,4,3,1,0:T(2,128)(2,1)}, u32[]{:S(2)}, u32[]{:S(2)}) collective-permute-start(bf16[2,1,2,18,6,192]{5,2,4,3,1,0:T(2,128)(2,1)} %pad_maximum_fusion.7), channel_id=1, source_target_pairs={{0,240},{16,0},{32,16},{48,32},{64,48},{80,64},{96,80},{112,96},{1... | collective-permute-start | bytes 497672 | tf_op jit(solution)/shard_map/ppermute | solution.py:16
  73.2 14.9 %copy-start.8 = (bf16[1,1,18,24,192]{4,1,3,2,0:T(2,128)(2,1)S(1)}, bf16[1,1,18,24,192]{4,1,3,2,0:T(2,128)(2,1)}, u32[]{:S(2)}) copy-start(bf16[1,1,18,24,192]{4,1,3,2,0:T(2,128)(2,1)} %copy-done.7) | copy-start | bytes 497668
  88.1 10.9 %copy-start.17 = (bf16[192,192]{1,0:T(8,128)(2,1)S(1)}, bf16[192,192]{1,0:T(8,128)(2,1)}, u32[]{:S(2)}) copy-start(bf16[192,192]{1,0:T(8,128)(2,1)} %param.12) | copy-start | bytes 221188
  90.3 11.1 %copy-start.14 = (bf16[192,576]{1,0:T(8,128)(2,1)S(1)}, bf16[192,576]{1,0:T(8,128)(2,1)}, u32[]{:S(2)}) copy-start(bf16[192,576]{1,0:T(8,128)(2,1)} %param.11) | copy-start | bytes 663556
  90.6 7.1 %collective-permute-start.1 = (bf16[2,1,2,3,24,192]{5,2,4,3,1,0:T(2,128)(2,1)S(1)}, bf16[2,1,2,3,24,192]{5,2,4,3,1,0:T(2,128)(2,1)S(1)}, u32[]{:S(2)}, u32[]{:S(2)}) collective-permute-start(bf16[2,1,2,3,24,192]{5,2,4,3,1,0:T(2,128)(2,1)S(1)} %pad_maximum_fusion.9), channel_id=1, source_target_pairs={{0,14},{2,0},{4,2},{6,4},{8,6},{10,8},{12,10},{14,12},{1,15},{3,1}... | collective-permute-start | bytes 331784 | tf_op jit(solution)/shard_map/ppermute | solution.py:16
  98.8 6.2 %copy-start.16 = (pred[6,144,144]{1,2,0:T(8,128)(4,1)S(1)}, pred[6,144,144]{1,2,0:T(8,128)(4,1)}, u32[]{:S(2)}) copy-start(pred[6,144,144]{1,2,0:T(8,128)(4,1)} %broadcast_compare_fusion) | copy-start | bytes 373252
  107.8 3.9 copy-start.3
  118.1 4.2 copy-start.4
  123.8 2.5 copy-start.2
  133.9 2.0 copy-start.15
  144.9 0.8 copy-start.12
  146.6 57.8 %collective-permute-start.2 = (bf16[2,1,2,3,24,192]{5,2,4,3,1,0:T(2,128)(2,1)}, bf16[2,1,2,3,24,192]{5,2,4,3,1,0:T(2,128)(2,1)}, u32[]{:S(2)}, u32[]{:S(2)}) collective-permute-start(bf16[2,1,2,3,24,192]{5,2,4,3,1,0:T(2,128)(2,1)} %pad_maximum_fusion.10), channel_id=1, source_target_pairs={{0,2},{2,4},{4,6},{6,8},{8,10},{10,12},{12,14},{14,0},{1,3},{3,5},... | collective-permute-start | bytes 331784 | tf_op jit(solution)/shard_map/ppermute | solution.py:16
  171.6 26.0 %copy-start.13 = (bf16[1,1,2,3,6,2,12,192]{7,2,6,5,4,3,1,0:T(2,128)(2,1)S(1)}, bf16[1,1,2,3,6,2,12,192]{7,2,6,5,4,3,1,0:T(2,128)(2,1)}, u32[]{:S(2)}) copy-start(bf16[1,1,2,3,6,2,12,192]{7,2,6,5,4,3,1,0:T(2,128)(2,1)} %copy-done.12) | copy-start | bytes 995332
  201.6 17.9 %copy-start.5 = (bf16[1,2,18,24,192]{4,3,2,1,0:T(8,128)(2,1)S(1)}, bf16[1,2,18,24,192]{4,3,2,1,0:T(8,128)(2,1)}, u32[]{:S(2)}) copy-start(bf16[1,2,18,24,192]{4,3,2,1,0:T(8,128)(2,1)} %param.7) | copy-start | bytes 995332
  201.6 17.9 %copy-start.10 = (f32[2,18,24]{0,2,1:T(8,128)S(1)}, f32[2,18,24]{0,2,1:T(8,128)}, u32[]{:S(2)}) copy-start(f32[2,18,24]{0,2,1:T(8,128)} %copy-done.9) | copy-start | bytes 10372
  201.6 17.9 %copy-start.19 = (f32[192]{0:T(256)S(1)}, f32[192]{0:T(256)}, u32[]{:S(2)}) copy-start(f32[192]{0:T(256)} %param.10) | copy-start | bytes 2308
  204.4 6.7 %copy-start.6 = (f32[24,6,3312]{2,0,1:T(8,128)}, f32[24,6,3312]{2,0,1:T(8,128)S(1)}, u32[]{:S(2)}) copy-start(f32[24,6,3312]{2,0,1:T(8,128)S(1)} %dynamic_update_slice.4) | copy-start | bytes 5723140
  208.8 7.4 %collective-permute-start.3 = (bf16[2,1,2,18,6,192]{5,2,4,3,1,0:T(2,128)(2,1)}, bf16[2,1,2,18,6,192]{5,2,4,3,1,0:T(2,128)(2,1)}, u32[]{:S(2)}, u32[]{:S(2)}) collective-permute-start(bf16[2,1,2,18,6,192]{5,2,4,3,1,0:T(2,128)(2,1)} %pad_maximum_fusion.8), channel_id=1, source_target_pairs={{0,16},{16,32},{32,48},{48,64},{64,80},{80,96},{96,112},{112,128},... | collective-permute-start | bytes 497672 | tf_op jit(solution)/shard_map/ppermute | solution.py:16
  211.1 14.4 %copy-start.11 = (bf16[1,2,18,24,192]{4,3,2,1,0:T(8,128)(2,1)S(1)}, bf16[1,2,18,24,192]{4,3,2,1,0:T(8,128)(2,1)}, u32[]{:S(2)}) copy-start(bf16[1,2,18,24,192]{4,3,2,1,0:T(8,128)(2,1)} %param.8) | copy-start | bytes 995332
  225.4 255.2 %copy-start.1 = (f32[24,6,3312]{2,0,1:T(8,128)S(1)}, f32[24,6,3312]{2,0,1:T(8,128)}, u32[]{:S(2)}) copy-start(f32[24,6,3312]{2,0,1:T(8,128)} %param.13) | copy-start | bytes 5723140
  (1 other events, 0.8 us)
Sparse Core Ops, SparseCore 0:
  211.2 262.9 all-reduce.2
where the time goes:
time: 494 us; the launch traced here: 488 us
  waiting for transfers between devices  173 us (35%)
  local copies, waits for them, and re-layouts  101 us (20%)
  blocking collectives  77.7 us (16%)
  matrix products  67.8 us (14%)
  other arithmetic  37.8 us (8%)
  starting transfers between devices  15.1 us (3%)
  between operations  14.8 us (3%)
    psum x1, waiting for transfers between devices, local(): lax.psum((in_grad, out_grad, gain_part, placed), ('lon', 'lat', 'ens'))  167 us
    psum x1, blocking collectives, local(): lax.psum((in_grad, out_grad, gain_part, placed), ('lon', 'lat', 'ens'))  77.7 us
    broadcast_in_dim x2, local copies, waits for them, and re-layouts, run_region(): jnp.broadcast_to(band_bias[None, :, :, None], grid_shape + tail)  44.7 us
    dot_general x1, matrix products, compress_bias(): jnp.einsum('...abcdef,xef->...abcdx', shaped, offset_table(WLON), precisi...  23.4 us
    ppermute x4, starting transfers between devices, passed_along(): return lax.ppermute(x, axis, [(i, (i + by) % peers) for i in range(peers)])  15.1 us
    reshape x1, local copies, waits for them, and re-layouts, compress_bias(): shaped = full.reshape(lead + (WL, WLAT, WLON, WL, WLAT, WLON))  14.1 us
    dot_general x1, matrix products, expand_bias(): jnp.einsum('...abcdx,xef->...abcdef', shaped, offset_table(WLON), precisi...  13.1 us
    unnamed x47, local copies, waits for them, and re-layouts  11 us
  transfers between devices with their start and end apart: 5, of which 3 were waited for; matrix products, arithmetic and copies ran while one was open for 28% of the time, Pallas kernels for 0%

commit v1 on v0

v1 whole, which is shorter than its diff:
```python
import functools

import jax
import jax.numpy as jnp
from jax import lax
from jax.experimental import pallas as pl
from jax.experimental.pallas import tpu as pltpu
from jax.sharding import PartitionSpec as P

WL, WLAT, WLON = 2, 6, 12
AB = WL * WLAT
POINTS = AB * WLON
SPAN = 2 * WLON - 1
EPS = 1e-05
F32, BF16, I32 = jnp.float32, jnp.bfloat16, jnp.int32
C, HEADS, HD = 192, 6, 32
FACTOR = HD ** (-0.5)
TAB = 3
ENTRIES = AB * AB * SPAN
LANE_BLOCKS = -(-ENTRIES // 128)
CHUNK = 64
G_ROWS = 40
T_ROWS = 16
SHARD = 176
VMEM = pltpu.CompilerParams(vmem_limit_bytes=56 * 2**20)


def dot(a, b, ca, cb):
    return lax.dot_general(a, b, (((ca,), (cb,)), ((), ())), preferred_element_type=F32)


def iota(shape, dim):
    return lax.broadcasted_iota(I32, shape, dim)


def segments():
    for ab_p in range(AB):
        a_p, b_p = divmod(ab_p, WLAT)
        for ab_r in range(AB):
            a_r, b_r = divmod(ab_r, WLAT)
            yield ab_p, ab_r, (((a_p * WL + a_r) * WLAT + b_p) * WLAT + b_r) * SPAN


def toeplitz(target, c):
    return (iota((384, POINTS), 0) == target + (WLON - 1 - c)).astype(BF16)


def expand_kernel(table_ref, target_ref, order_ref, bias_ref, rows_ref):
    rows_ref[...] = jnp.zeros_like(rows_ref)
    for t in range(TAB):
        for ab_p, ab_r, start in segments():
            rows_ref[t, ab_r * 8 : ab_r * 8 + HEADS, ab_p * SPAN : (ab_p + 1) * SPAN] = table_ref[
                t, :, start : start + SPAN
            ]
    order = order_ref[...]
    target = target_ref[...]
    pieces = []
    rest = [rows_ref[t] for t in range(TAB)]
    for _ in range(3):
        low = [r.astype(BF16) for r in rest]
        rest = [r - p.astype(F32) for r, p in zip(rest, low)]
        pieces.append(jnp.concatenate([dot(order, p, 1, 0).astype(BF16) for p in low], axis=0))
    for c in range(WLON):
        pick = toeplitz(target, c)
        full = dot(pieces[0], pick, 1, 0) + (dot(pieces[1], pick, 1, 0) + dot(pieces[2], pick, 1, 0))
        for th in range(TAB * HEADS):
            bias_ref[th, c * AB : (c + 1) * AB, :] = full[th * 16 : th * 16 + AB, :]


def main_kernel(
    ens_ref, x_ref, y_ref, lon_ref, lat_ref, cor_ref, region_ref, gain_ref, win_ref, win_t_ref, wout_ref,
    wout_t_ref, bias_ref, place_ref, target_ref, order_ref,
    out_ref, ig_ref, lon_out, lat_out, cor_out, keep_ref, send_ref,
    ext, grads, outer, gain_acc, dbias, blocks, rows, flat_t, flat, chunks,
):
    for k, ref in enumerate((x_ref, y_ref)):
        ext[k, :, 0:18, 0:24, :] = ref[...].astype(F32)
        ext[k, :, 0:18, 24:32, :] = lon_ref[k].astype(F32)
        ext[k, :, 18:21, 0:24, :] = lat_ref[k].astype(F32)
        ext[k, :, 18:21, 24:32, :] = cor_ref[k].astype(F32)
    grads[...] = jnp.zeros_like(grads)
    outer[...] = jnp.zeros_like(outer)
    gain_acc[...] = jnp.zeros_like(gain_acc)
    gain = gain_ref[...]
    place = place_ref[...]

    def row(v, carry):
        span = pl.ds(6 * v + 3, 6)
        xw = ext[0, :, span].reshape(384, C).astype(BF16)
        yw = ext[1, :, span].reshape(384, C).astype(BF16)
        out_w = jnp.zeros((384, C), F32)
        ig_w = jnp.zeros((384, C), F32)
        for w in range(2):
            pick = (iota((384, POINTS), 0) == place + WLON * w).astype(BF16)
            xt = dot(xw, pick, 0, 0)
            ct32 = dot(yw, pick, 0, 0)
            ct = ct32.astype(BF16)
            center = xt - jnp.mean(xt, axis=0, keepdims=True)
            inverse = lax.rsqrt(jnp.mean(center * center, axis=0, keepdims=True) + EPS)
            part = center * inverse
            normed = (part * gain).astype(BF16)
            triple = dot(win_t_ref[...], normed, 1, 0).astype(BF16)
            grad_mixed = dot(wout_ref[...], ct, 1, 0).astype(BF16)
            ids = region_ref[v, w]
            member = (iota((8, POINTS), 0) == ids).astype(BF16)
            barred = (dot(member, member, 0, 0) - 1.0) * 1e30
            mixed, g_q, g_k, g_v = [], [], [], []
            for h in range(HEADS):
                lo, hi = h * HD, (h + 1) * HD
                q, k, val = triple[lo:hi], triple[C + lo : C + hi], triple[2 * C + lo : 2 * C + hi]
                gm = grad_mixed[lo:hi]
                scores = dot(k, q, 0, 0) * FACTOR + (bias_ref[v * HEADS + h] + barred)
                raised = jnp.exp(scores - jnp.max(scores, axis=0, keepdims=True))
                prob = raised * (1.0 / jnp.sum(raised, axis=0, keepdims=True))
                low = prob.astype(BF16)
                mixed.append(dot(val, low, 1, 0))
                g_prob = dot(val, gm, 0, 0)
                g_v.append(dot(gm, low, 1, 1))
                g_score = prob * (g_prob - jnp.sum(prob * g_prob, axis=0, keepdims=True))
                if w == 0:
                    dbias[v * HEADS + h] = g_score
                else:
                    dbias[v * HEADS + h] += g_score
                g_low = g_score.astype(BF16)
                g_q.append(dot(k, g_low, 1, 0) * FACTOR)
                g_k.append(dot(q, g_low, 1, 1) * FACTOR)
            mixed = jnp.concatenate(mixed, axis=0).astype(BF16)
            attended = dot(wout_t_ref[...], mixed, 1, 0).astype(BF16)
            outer[...] += dot(mixed, ct, 1, 1)
            g_triple = jnp.concatenate(g_q + g_k + g_v, axis=0).astype(BF16)
            grads[:, : 3 * C] += dot(normed, g_triple, 1, 1)
            wide = dot(win_ref[...], g_triple, 1, 0).astype(BF16).astype(F32)
            block = (xt + attended.astype(F32)).astype(BF16)
            gain_acc[...] += wide * part
            scaled = wide * gain
            grad_part = inverse * (
                scaled
                - jnp.mean(scaled, axis=0, keepdims=True)
                - part * jnp.mean(scaled * part, axis=0, keepdims=True)
            )
            in_grad = (ct32 + grad_part).astype(BF16)
            out_w = out_w + dot(pick, block, 1, 1)
            ig_w = ig_w + dot(pick, in_grad, 1, 1)
        ext[0, :, span] = out_w.reshape(2, 6, 32, C)
        ext[1, :, span] = ig_w.reshape(2, 6, 32, C)
        return carry

    lax.fori_loop(0, TAB, row, 0)
    for k, ref in enumerate((out_ref, ig_ref)):
        ext[k, :, 0:3] = jnp.zeros((2, 3, 32, C), F32)
        ref[...] = ext[k, :, 0:18, 0:24, :].astype(BF16)
        lon_out[k] = ext[k, :, 0:18, 24:32, :].astype(BF16)
        lat_out[k] = ext[k, :, 18:21, 0:24, :].astype(BF16)
        cor_out[k] = ext[k, :, 18:21, 24:32, :].astype(BF16)

    blocks[...] = jnp.zeros_like(blocks)
    total = jnp.zeros((TAB * HEADS * 16, 384), F32)
    for c in range(WLON):
        for th in range(TAB * HEADS):
            blocks[th * 16 : th * 16 + AB, :] = dbias[th, c * AB : (c + 1) * AB, :]
        total = total + dot(blocks[...].astype(BF16), toeplitz(target_ref[...], c), 1, 1)
    flat_t[...] = jnp.zeros_like(flat_t)
    for t in range(TAB):
        rows[...] = dot(order_ref[...], total[t * 96 : (t + 1) * 96].astype(BF16), 0, 0)
        for ab_p, ab_r, start in segments():
            flat_t[t * 8 : t * 8 + 8, start : start + SPAN] = rows[
                ab_r * 8 : ab_r * 8 + 8, ab_p * SPAN : (ab_p + 1) * SPAN
            ]
    flat[...] = jnp.zeros_like(flat)
    for block in range(LANE_BLOCKS):
        for t in range(TAB):
            at = (block * TAB + t) * HEADS
            flat[at : at + HEADS, :] = flat_t[t * 8 : t * 8 + HEADS, block * 128 : (block + 1) * 128]

    chunks[...] = jnp.zeros_like(chunks)
    grads[:, 3 * C :] = outer[...]
    tile = 0
    for group in range(C // 8):
        for block in range(C * 4 // 128):
            chunk, slot = divmod(tile, G_ROWS // 8)
            chunks[chunk // 16, chunk % 16, slot * 8 : slot * 8 + 8, :] = grads[
                group * 8 : group * 8 + 8, block * 128 : (block + 1) * 128
            ]
            tile += 1
    for chunk in range(32):
        chunks[chunk // 16, chunk % 16, G_ROWS : G_ROWS + T_ROWS, :] = flat[chunk * T_ROWS : (chunk + 1) * T_ROWS]
    rest = gain_acc[...]
    gain_row = jnp.zeros((8, C), F32)
    for _ in range(3):
        low = rest.astype(BF16)
        rest = rest - low.astype(F32)
        gain_row = gain_row + dot(jnp.ones((8, POINTS), BF16), low, 1, 1)
    chunks[1, 13, 0:1, :] = gain_row[0:1, 0:128]
    chunks[1, 13, 1:2, 0:64] = gain_row[0:1, 128:192]
    me = ens_ref[0]
    keep_ref[...] = chunks[me]
    send_ref[...] = chunks[1 - me].astype(BF16)


def over_lon_kernel(got_ref, out_ref):
    total = jnp.sum(got_ref[...].astype(F32), axis=0).astype(BF16)
    for k in range(out_ref.shape[0]):
        out_ref[k] = total


def over_lat_kernel(got_ref, out_ref):
    got = got_ref[...].astype(F32)
    total = jnp.sum(got[:, : G_ROWS + 8], axis=0)
    shard = jnp.concatenate([total] + [got[k, G_ROWS : G_ROWS + T_ROWS] for k in range(8)], axis=0).astype(BF16)
    for k in range(out_ref.shape[0]):
        out_ref[k] = shard


def final_kernel(ens_ref, mine_ref, other_ref, order_ref, in_ref, outer_ref, gain_ref, table_ref, both, tables, grads, full):
    me = ens_ref[0]
    both[me] = mine_ref[...].astype(F32)
    both[1 - me] = other_ref[...].astype(F32)
    tile = 0
    for group in range(C // 8):
        for block in range(C * 4 // 128):
            chunk, slot = divmod(tile, G_ROWS // 8)
            grads[group * 8 : group * 8 + 8, block * 128 : (block + 1) * 128] = both[
                chunk // 16, chunk % 16, slot * 8 : slot * 8 + 8, :
            ]
            tile += 1
    in_ref[...] = grads[:, 0 : 3 * C]
    outer_ref[...] = grads[:, 3 * C :]
    gain_ref[0:1, 0:128] = both[1, 13, 0:1, :]
    gain_ref[0:1, 128:192] = both[1, 13, 1:2, 0:64]
    for lat in range(8):
        for chunk in range(32):
            tables[lat, chunk * T_ROWS : (chunk + 1) * T_ROWS, :] = both[
                chunk // 16, chunk % 16, G_ROWS + 8 + lat * T_ROWS : G_ROWS + 8 + (lat + 1) * T_ROWS, :
            ]
    count = TAB * HEADS
    for lat in range(8):
        for block in range(LANE_BLOCKS):
            full[lat * count : (lat + 1) * count, block * 128 : (block + 1) * 128] = tables[
                lat, block * count : (block + 1) * count, :
            ]
    ordered = dot(order_ref[...], full[...].astype(BF16), 1, 0)
    for h in range(HEADS):
        table_ref[h] = ordered[h * 24 : (h + 1) * 24, :ENTRIES]


def vmem(count):
    return [pl.BlockSpec(memory_space=pltpu.VMEM)] * count


SMEM = pl.BlockSpec(memory_space=pltpu.SMEM)


def struct(shape, dtype):
    return jax.ShapeDtypeStruct(shape, dtype)


def passed(x, axes, sizes, moves):
    total = [()]
    for size in sizes:
        total = [t + (i,) for t in total for i in range(size)]

    def number(index):
        n = 0
        for i, size in zip(index, sizes):
            n = n * size + i % size
        return n

    pairs = [(number(t), number(tuple(i + m for i, m in zip(t, moves)))) for t in total]
    return lax.ppermute(x, axes, pairs)


def halo(lon_strip, lat_strip, corner, by):
    n_lon, n_lat = lax.axis_size("lon"), lax.axis_size("lat")
    return (
        passed(lon_strip, "lon", (n_lon,), (by,)),
        passed(lat_strip, "lat", (n_lat,), (by,)),
        passed(corner, ("lon", "lat"), (n_lon, n_lat), (by, by)),
    )


def one_hot(index, width):
    return (index[:, None] == jnp.arange(width, dtype=I32)[None, :]).astype(BF16)


def local(inputs, cotangent, mask_ids, norm_gain, project_in, project_out, bias_table):
    x, y = inputs[0], cotangent[0]
    lat, ens = lax.axis_index("lat"), lax.axis_index("ens")
    pair = jnp.stack([x, y])
    strips = halo(pair[:, :, :, 0:8], pair[:, :, 0:3], pair[:, :, 0:3, 0:8], -1)

    p = jnp.arange(POINTS, dtype=I32)
    c_p, ab_p = p // AB, p % AB
    target = (ab_p * SPAN + c_p)[None]
    place = ((1 - ab_p // WLAT) * (WLAT * 32) + (ab_p % WLAT) * 32 + WLON // 2 + c_p)[None]
    n = jnp.arange(96, dtype=I32)
    order = one_hot(jnp.where(n % 16 < AB, (n % 16) * 8 + n // 16, -1), 96)
    table = lax.dynamic_slice_in_dim(bias_table, lat * TAB, TAB, 0)
    bias = pl.pallas_call(
        expand_kernel,
        out_shape=struct((TAB * HEADS, POINTS, POINTS), F32),
        in_specs=vmem(3),
        out_specs=vmem(1)[0],
        scratch_shapes=[pltpu.VMEM((TAB, 96, 384), F32)],
        compiler_params=VMEM,
    )(table, target, order)
    regions = mask_ids.reshape(WL, TAB, WLAT, 2, WLON).transpose(1, 3, 4, 0, 2).reshape(TAB, 2, 1, POINTS)
    me = ens.astype(I32).reshape(1)

    out, in_grad, lon_s, lat_s, cor_s, keep, send = pl.pallas_call(
        main_kernel,
        out_shape=(
            struct((2, 18, 24, C), BF16),
            struct((2, 18, 24, C), BF16),
            struct((2, 2, 18, 8, C), BF16),
            struct((2, 2, 3, 24, C), BF16),
            struct((2, 2, 3, 8, C), BF16),
            struct((16, CHUNK, 128), F32),
            struct((16, CHUNK, 128), BF16),
        ),
        in_specs=[SMEM] + vmem(15),
        out_specs=tuple(vmem(7)),
        scratch_shapes=[
            pltpu.VMEM((2, 2, 21, 32, C), F32),
            pltpu.VMEM((C, 4 * C), F32),
            pltpu.VMEM((C, C), F32),
            pltpu.VMEM((C, POINTS), F32),
            pltpu.VMEM((TAB * HEADS, POINTS, POINTS), F32),
            pltpu.VMEM((TAB * HEADS * 16, POINTS), F32),
            pltpu.VMEM((96, 384), F32),
            pltpu.VMEM((TAB * 8, LANE_BLOCKS * 128), F32),
            pltpu.VMEM((32 * T_ROWS, 128), F32),
            pltpu.VMEM((2, 16, CHUNK, 128), F32),
        ],
        compiler_params=VMEM,
    )(
        me, x, y, *strips, regions, norm_gain.reshape(C, 1), project_in, project_in.T, project_out, project_out.T,
        bias, place, target, order,
    )

    strips = halo(lon_s, lat_s, cor_s, 1)
    got = passed(send, "ens", (2,), (1,))
    part = (keep + got.astype(F32)).astype(BF16)
    part = lax.all_to_all(part, "lon", 0, 0, tiled=True)
    part = pl.pallas_call(
        over_lon_kernel,
        out_shape=struct((8, CHUNK, 128), BF16),
        in_specs=vmem(1),
        out_specs=vmem(1)[0],
        compiler_params=VMEM,
    )(part)
    part = lax.all_to_all(part, "lat", 0, 0, tiled=True)
    part = pl.pallas_call(
        over_lat_kernel,
        out_shape=struct((16, SHARD, 128), BF16),
        in_specs=vmem(1),
        out_specs=vmem(1)[0],
        compiler_params=VMEM,
    )(part)
    mine = lax.all_to_all(part, "lon", 0, 0, tiled=True)
    other = passed(mine, "ens", (2,), (1,))
    m = jnp.arange(144, dtype=I32)
    table_order = one_hot((m % 24) * HEADS + m // 24, 144)
    in_total, out_total, gain_total, table_total = pl.pallas_call(
        final_kernel,
        out_shape=(
            struct((C, 3 * C), F32),
            struct((C, C), F32),
            struct((1, C), F32),
            struct((HEADS, 24, ENTRIES), F32),
        ),
        in_specs=[SMEM] + vmem(3),
        out_specs=tuple(vmem(4)),
        scratch_shapes=[
            pltpu.VMEM((2, 16, SHARD, 128), F32),
            pltpu.VMEM((8, 32 * T_ROWS, 128), F32),
            pltpu.VMEM((C, 4 * C), F32),
            pltpu.VMEM((144, LANE_BLOCKS * 128), F32),
        ],
        compiler_params=VMEM,
    )(me, mine, other, table_order)

    both = jnp.stack([out, in_grad])
    lon_pad = jnp.pad(strips[0], ((0, 0), (0, 0), (0, 0), (0, 16), (0, 0)))
    lat_pad = jnp.pad(strips[1], ((0, 0), (0, 0), (0, 15), (0, 0), (0, 0)))
    cor_pad = jnp.pad(strips[2], ((0, 0), (0, 0), (0, 15), (0, 16), (0, 0)))
    both = both + lon_pad + lat_pad + cor_pad
    return (
        both[0][None],
        both[1][None],
        in_total,
        out_total,
        gain_total.reshape(C),
        table_total.transpose(1, 0, 2),
    )


def solution(mesh):
    return jax.shard_map(
        local,
        mesh=mesh,
        in_specs=(
            P("ens", None, "lat", "lon", None),
            P("ens", None, "lat", "lon", None),
            P(None, "lat", "lon"),
            P(),
            P(),
            P(),
            P(),
        ),
        out_specs=(
            P("ens", None, "lat", "lon", None),
            P("ens", None, "lat", "lon", None),
            P(),
            P(),
            P(),
            P(),
        ),
        check_vma=False,
    )
```

time: 494 us -> 136 us (0.28); the launches traced: 488 us -> 135 us
  waiting for transfers between devices: 173 us -> 12.3 us
  local copies, waits for them, and re-layouts: 101 us -> 9.84 us
  matrix products: 67.8 us -> 0 us
  Pallas kernels: 0 us -> 39.6 us
  other arithmetic: 37.8 us -> 3.33 us
  blocking collectives: 77.7 us -> 45.3 us
  between operations: 14.8 us -> 0.82 us
  starting transfers between devices: 15.1 us -> 24.1 us
    psum x1 -> x0, waiting for transfers between devices: 167 us -> none  [local(): lax.psum((in_grad, out_grad, gain_part, placed), ('lon', 'lat', 'ens'))]
    psum x1 -> x0, blocking collectives: 77.7 us -> none  [local(): lax.psum((in_grad, out_grad, gain_part, placed), ('lon', 'lat', 'ens'))]
    dot_general x14 -> x0, matrix products: 67.8 us -> none  [the longest x1 23.4 us: compress_bias(): jnp.einsum('...abcdef,xef->...abcdx', shaped, offset_table(WLON), precisi...]
    all_to_all x0 -> x3, blocking collectives: none -> 45.3 us  [the longest x1 21.7 us: local(): mine = lax.all_to_all(part, 'lon', 0, 0, tiled=True)]
    broadcast_in_dim x2 -> x0, local copies, waits for them, and re-layouts: 44.7 us -> none  [run_region(): jnp.broadcast_to(band_bias[None, :, :, None], grid_shape + tail)]
    pallas_call x0 -> x5, Pallas kernels: none -> 39.6 us  [the longest x1 26.3 us: local(): pl.pallas_call(main_kernel, out_shape=(struct((2, 18, 24, C), BF16), stru...]
    reshape x4, local copies, waits for them, and re-layouts: 17.3 us -> 1.77 us  [the longest x3 1 us: local(): mask_ids.reshape(WL, TAB, WLAT, 2, WLON).transpose(1, 3, 4, 0, 2)]
    reduce_sum x4 -> x0, other arithmetic: 12.2 us -> none  [the longest x1 4.74 us: run_region(): row_sums = jnp.sum(grad_scores.reshape(grid_shape + tail), axis=(0, 3))]
  transfers between devices with their start and end apart: 5 -> 8, of which waited for: 3 -> 3; matrix products, arithmetic and copies ran while one was open for 28% -> 6% of each run, Pallas kernels for 0% -> 5%
where the time goes in v1:
time: 136 us; the launch traced here: 135 us
  blocking collectives  45.3 us (33%)
  Pallas kernels  39.6 us (29%)
  starting transfers between devices  24.1 us (18%)
  waiting for transfers between devices  12.3 us (9%)
  local copies, waits for them, and re-layouts  9.84 us (7%)
  other arithmetic  3.33 us (2%)
    pallas_call x1, Pallas kernels, local(): pl.pallas_call(main_kernel, out_shape=(struct((2, 18, 24, C), BF16), stru...  26.3 us
    ppermute x8, starting transfers between devices, passed(): return lax.ppermute(x, axes, pairs)  24.1 us
    all_to_all x1, blocking collectives, local(): mine = lax.all_to_all(part, 'lon', 0, 0, tiled=True)  21.7 us
    all_to_all x1, blocking collectives, local(): part = lax.all_to_all(part, 'lon', 0, 0, tiled=True)  12.6 us
    ppermute x8, waiting for transfers between devices, passed(): return lax.ppermute(x, axes, pairs)  12.3 us
    all_to_all x1, blocking collectives, local(): part = lax.all_to_all(part, 'lat', 0, 0, tiled=True)  11 us
    pallas_call x1, Pallas kernels, local(): pl.pallas_call(expand_kernel, out_shape=struct((TAB * HEADS, POINTS, POIN...  6.32 us
    unnamed x34, local copies, waits for them, and re-layouts  5.29 us
  transfers between devices with their start and end apart: 8, of which 3 were waited for; matrix products, arithmetic and copies ran while one was open for 6% of the time, Pallas kernels for 5%

profile of v1, /device:TPU:1, one launch (start us, length us, event | category | flops | bytes accessed | tf_op | source)
XLA Modules:
  0.0 135.4 jit_solution(2286490355141332439)
XLA Ops:
  0.6 1.2 constant_dynamic-update-slice_fusion.1
  1.9 1.1 constant_dynamic-update-slice_fusion
  3.0 7.4 %collective-permute-start = (bf16[2,2,18,8,192]{4,3,2,1,0:T(8,128)(2,1)S(1)}, bf16[2,2,18,8,192]{4,3,2,1,0:T(8,128)(2,1)S(1)}, u32[]{:S(2)}, u32[]{:S(2)}) collective-permute-start(bf16[2,2,18,8,192]{4,3,2,1,0:T(8,128)(2,1)S(1)} %slice.20), channel_id=1, source_target_pairs={{0,240},{16,0},{32,16},{48,32},{64,48},{80,64},{96,80},{112,96},{1... | collective-permute-start | bytes 663560 | tf_op jit(solution)/shard_map/ppermute | solution.py:269
  10.4 5.0 %collective-permute-start.1 = (bf16[2,2,3,24,192]{4,3,2,1,0:T(8,128)(2,1)S(1)}, bf16[2,2,3,24,192]{4,3,2,1,0:T(8,128)(2,1)S(1)}, u32[]{:S(2)}, u32[]{:S(2)}) collective-permute-start(bf16[2,2,3,24,192]{4,3,2,1,0:T(8,128)(2,1)S(1)} %slice.21), channel_id=1, source_target_pairs={{0,14},{2,0},{4,2},{6,4},{8,6},{10,8},{12,10},{14,12},{1,15},{3,1}... | collective-permute-start | bytes 331784 | tf_op jit(solution)/shard_map/ppermute | solution.py:269
  18.8 0.9 copy.18
  22.3 6.3 %shard_map.118.bias_ref = f32[18,144,144]{2,1,0:T(8,128)} custom-call(f32[3,6,3312]{2,1,0:T(8,128)} %copy.23.table_ref, s32[1,144]{1,0:T(1,128)} %get-tuple-element.31.target_ref, bf16[96,96]{1,0:T(8,128)(2,1)} %fusion.3.order_ref), custom_call_target="tpu_custom_call" | custom-call | tf_op jit(solution)/shard_map/pallas_call | solution.py:298
  29.4 26.3 %shard_map.119 = (bf16[2,18,24,192]{3,2,1,0:T(8,128)(2,1)}, bf16[2,18,24,192]{3,2,1,0:T(8,128)(2,1)}, bf16[2,2,18,8,192]{4,3,2,1,0:T(8,128)(2,1)}, bf16[2,2,3,24...) custom-call(s32[1]{0:T(128)} %bitcast.ens_ref, ...), custom_call_target="tpu_custom_call" | custom-call | tf_op jit(solution)/shard_map/pallas_call | solution.py:309
  55.7 1.5 %collective-permute-start.6 = (bf16[16,64,128]{2,1,0:T(8,128)(2,1)}, bf16[16,64,128]{2,1,0:T(8,128)(2,1)S(1)}, u32[]{:S(2)}, u32[]{:S(2)}) collective-permute-start(bf16[16,64,128]{2,1,0:T(8,128)(2,1)} %get-tuple-element.23), channel_id=1, source_target_pairs={{0,1},{1,0},{2,3},{3,2},{4,5},{5,4},{6,7},{7,6},{8,9},{9,8},{10,11... | collective-permute-start | bytes 786440 | tf_op jit(solution)/shard_map/ppermute | solution.py:269
  57.2 1.4 %collective-permute-done.6 = bf16[16,64,128]{2,1,0:T(8,128)(2,1)S(1)} collective-permute-done((bf16[16,64,128]{2,1,0:T(8,128)(2,1)}, bf16[16,64,128]{2,1,0:T(8,128)(2,1)S(1)}, u32[]{:S(2)}, u32[]{:S(2)}) %collective-permute-start.6) | collective-permute-done | bytes 262176 | tf_op jit(solution)/shard_map/ppermute | solution.py:269
  58.6 1.1 add_convert_fusion
  59.7 12.6 %all_to_all.15.got_ref = bf16[16,64,128]{2,1,0:T(8,128)(2,1)} all-to-all(bf16[16,64,128]{2,1,0:T(8,128)(2,1)S(1)} %add_convert_fusion), channel_id=1, replica_groups=mesh['lon'=16,'lat'=8,'ens'=2] {'lon'}, dimensions={0} | all-to-all | bytes 524288 | tf_op jit(solution)/shard_map/all_to_all | solution.py:343
  72.4 1.6 %shard_map.120 = bf16[8,64,128]{2,1,0:T(8,128)(2,1)} custom-call(bf16[16,64,128]{2,1,0:T(8,128)(2,1)} %all_to_all.15.got_ref), custom_call_target="tpu_custom_call" | custom-call | tf_op jit(solution)/shard_map/pallas_call | solution.py:344
  74.0 11.0 %all_to_all.16.got_ref = bf16[8,64,128]{2,1,0:T(8,128)(2,1)} all-to-all(bf16[8,64,128]{2,1,0:T(8,128)(2,1)} %shard_map.120), channel_id=1, replica_groups=mesh['lon'=16,'lat'=8,'ens'=2] {'lat'}, dimensions={0} | all-to-all | bytes 262144 | tf_op jit(solution)/shard_map/all_to_all | solution.py:351
  85.1 1.8 %shard_map.121 = bf16[16,176,128]{2,1,0:T(8,128)(2,1)} custom-call(bf16[8,64,128]{2,1,0:T(8,128)(2,1)} %all_to_all.16.got_ref), custom_call_target="tpu_custom_call" | custom-call | tf_op jit(solution)/shard_map/pallas_call | solution.py:352
  86.9 21.7 %all_to_all.17.mine_ref = bf16[16,176,128]{2,1,0:T(8,128)(2,1)S(1)} all-to-all(bf16[16,176,128]{2,1,0:T(8,128)(2,1)} %shard_map.121), channel_id=1, replica_groups=mesh['lon'=16,'lat'=8,'ens'=2] {'lon'}, dimensions={0} | all-to-all | bytes 1441792 | tf_op jit(solution)/shard_map/all_to_all | solution.py:359
  108.6 5.1 %collective-permute-start.7 = (bf16[16,176,128]{2,1,0:T(8,128)(2,1)S(1)}, bf16[16,176,128]{2,1,0:T(8,128)(2,1)S(1)}, u32[]{:S(2)}, u32[]{:S(2)}) collective-permute-start(bf16[16,176,128]{2,1,0:T(8,128)(2,1)S(1)} %all_to_all.17.mine_ref), channel_id=1, source_target_pairs={{0,1},{1,0},{2,3},{3,2},{4,5},{5,4},{6,7},{7,6},{8,9},{9,8},{10,11... | collective-permute-start | bytes 2162696 | tf_op jit(solution)/shard_map/ppermute | solution.py:269
  113.7 1.8 %collective-permute-start.3 = (bf16[2,2,18,8,192]{4,3,2,1,0:T(8,128)(2,1)S(1)}, bf16[2,2,18,8,192]{4,3,2,1,0:T(8,128)(2,1)S(1)}, u32[]{:S(2)}, u32[]{:S(2)}) collective-permute-start(bf16[2,2,18,8,192]{4,3,2,1,0:T(8,128)(2,1)S(1)} %copy-done.12), channel_id=1, source_target_pairs={{0,16},{16,32},{32,48},{48,64},{64,80},{80,96},{96,112},{112,128},... | collective-permute-start | bytes 663560 | tf_op jit(solution)/shard_map/ppermute | solution.py:269
  115.5 1.4 %collective-permute-start.4 = (bf16[2,2,3,24,192]{4,3,2,1,0:T(8,128)(2,1)S(1)}, bf16[2,2,3,24,192]{4,3,2,1,0:T(8,128)(2,1)S(1)}, u32[]{:S(2)}, u32[]{:S(2)}) collective-permute-start(bf16[2,2,3,24,192]{4,3,2,1,0:T(8,128)(2,1)S(1)} %copy-done.13), channel_id=1, source_target_pairs={{0,2},{2,4},{4,6},{6,8},{8,10},{10,12},{12,14},{14,0},{1,3},{3,5},... | collective-permute-start | bytes 331784 | tf_op jit(solution)/shard_map/ppermute | solution.py:269
  116.8 1.3 collective-permute-start.5
  118.9 7.6 %collective-permute-done.5 = bf16[2,2,3,8,192]{4,3,2,1,0:T(8,128)(2,1)S(1)} collective-permute-done((bf16[2,2,3,8,192]{4,3,2,1,0:T(8,128)(2,1)S(1)}, bf16[2,2,3,8,192]{4,3,2,1,0:T(8,128)(2,1)S(1)}, u32[]{:S(2)}, u32[]{:S(2)}) %collective-permute-start.5) | collective-permute-done | bytes 36896 | tf_op jit(solution)/shard_map/ppermute | solution.py:269
  126.5 3.3 %collective-permute-done.4 = bf16[2,2,3,24,192]{4,3,2,1,0:T(8,128)(2,1)S(1)} collective-permute-done((bf16[2,2,3,24,192]{4,3,2,1,0:T(8,128)(2,1)S(1)}, bf16[2,2,3,24,192]{4,3,2,1,0:T(8,128)(2,1)S(1)}, u32[]{:S(2)}, u32[]{:S(2)}) %collective-permute-start.4) | collective-permute-done | bytes 110624 | tf_op jit(solution)/shard_map/ppermute | solution.py:269
  130.0 1.0 fusion.10
  131.0 0.9 copy-done.3
  131.9 3.5 %shard_map.122 = (f32[192,576]{1,0:T(8,128)}, f32[192,192]{1,0:T(8,128)}, f32[1,192]{1,0:T(1,128)}, f32[6,24,3312]{2,1,0:T(8,128)}) custom-call(s32[1]{0:T(128)} %bitcast.ens_ref, bf16[16,176,128]{2,1,0:T(8,128)(2,1)} %copy-done.1, bf16[16,176,128]{2,1,0:T(8,128)(2,1)} %copy-done.3, bf16[144,144]{1,0:T(8,128)(2,1)} %fusion.2.order_ref), custom_call_target="tpu_custom_call" | custom-call | tf_op jit(solution)/shard_map/pallas_call | solution.py:363
  (51 shorter events, 7.7 us)
Async XLA Ops:
  0.6 16.1 %copy-start = (f32[24,6,3312]{2,0,1:T(8,128)S(1)}, f32[24,6,3312]{2,0,1:T(8,128)}, u32[]{:S(2)}) copy-start(f32[24,6,3312]{2,0,1:T(8,128)} %param.13) | copy-start | bytes 5723140
  1.8 17.0 %copy-start.2 = (bf16[192,576]{1,0:T(8,128)(2,1)S(1)}, bf16[192,576]{1,0:T(8,128)(2,1)}, u32[]{:S(2)}) copy-start(bf16[192,576]{1,0:T(8,128)(2,1)} %win_ref.1) | copy-start | bytes 663556
  1.8 17.9 %copy-start.10 = (s32[2,18,24]{2,0,1:T(2,128)S(1)}, s32[2,18,24]{2,0,1:T(2,128)}, u32[]{:S(2)}) copy-start(s32[2,18,24]{2,0,1:T(2,128)} %param.9) | copy-start | bytes 10372
  2.9 17.8 %copy-start.6 = (bf16[192,192]{1,0:T(8,128)(2,1)S(1)}, bf16[192,192]{1,0:T(8,128)(2,1)}, u32[]{:S(2)}) copy-start(bf16[192,192]{1,0:T(8,128)(2,1)} %wout_ref.1) | copy-start | bytes 221188
  3.0 18.5 %copy-start.11 = (f32[192]{0:T(256)S(1)}, f32[192]{0:T(256)}, u32[]{:S(2)}) copy-start(f32[192]{0:T(256)} %param.10) | copy-start | bytes 2308
  3.0 25.6 %collective-permute-start = (bf16[2,2,18,8,192]{4,3,2,1,0:T(8,128)(2,1)S(1)}, bf16[2,2,18,8,192]{4,3,2,1,0:T(8,128)(2,1)S(1)}, u32[]{:S(2)}, u32[]{:S(2)}) collective-permute-start(bf16[2,2,18,8,192]{4,3,2,1,0:T(8,128)(2,1)S(1)} %slice.20), channel_id=1, source_target_pairs={{0,240},{16,0},{32,16},{48,32},{64,48},{80,64},{96,80},{112,96},{1... | collective-permute-start | bytes 663560 | tf_op jit(solution)/shard_map/ppermute | solution.py:269
  10.4 18.2 %collective-permute-start.1 = (bf16[2,2,3,24,192]{4,3,2,1,0:T(8,128)(2,1)S(1)}, bf16[2,2,3,24,192]{4,3,2,1,0:T(8,128)(2,1)S(1)}, u32[]{:S(2)}, u32[]{:S(2)}) collective-permute-start(bf16[2,2,3,24,192]{4,3,2,1,0:T(8,128)(2,1)S(1)} %slice.21), channel_id=1, source_target_pairs={{0,14},{2,0},{4,2},{6,4},{8,6},{10,8},{12,10},{14,12},{1,15},{3,1}... | collective-permute-start | bytes 331784 | tf_op jit(solution)/shard_map/ppermute | solution.py:269
  16.0 12.6 %collective-permute-start.2 = (bf16[2,2,3,8,192]{4,3,2,1,0:T(8,128)(2,1)}, bf16[2,2,3,8,192]{4,3,2,1,0:T(8,128)(2,1)S(1)}, u32[]{:S(2)}, u32[]{:S(2)}) collective-permute-start(bf16[2,2,3,8,192]{4,3,2,1,0:T(8,128)(2,1)} %slice.22), channel_id=1, source_target_pairs={{0,254},{2,240},{4,242},{6,244},{8,246},{10,248},{12,250},{14,252}... | collective-permute-start | bytes 110600 | tf_op jit(solution)/shard_map/ppermute | solution.py:269
  28.6 0.6 copy-start.9
  28.6 0.7 copy-start.8
  28.6 0.7 copy-start.7
  55.7 2.9 %collective-permute-start.6 = (bf16[16,64,128]{2,1,0:T(8,128)(2,1)}, bf16[16,64,128]{2,1,0:T(8,128)(2,1)S(1)}, u32[]{:S(2)}, u32[]{:S(2)}) collective-permute-start(bf16[16,64,128]{2,1,0:T(8,128)(2,1)} %get-tuple-element.23), channel_id=1, source_target_pairs={{0,1},{1,0},{2,3},{3,2},{4,5},{5,4},{6,7},{7,6},{8,9},{9,8},{10,11... | collective-permute-start | bytes 786440 | tf_op jit(solution)/shard_map/ppermute | solution.py:269
  59.7 54.0 %copy-start.12 = (bf16[2,2,18,8,192]{4,3,2,1,0:T(8,128)(2,1)S(1)}, bf16[2,2,18,8,192]{4,3,2,1,0:T(8,128)(2,1)}, u32[]{:S(2)}) copy-start(bf16[2,2,18,8,192]{4,3,2,1,0:T(8,128)(2,1)} %get-tuple-element.19) | copy-start | bytes 663556
  59.7 55.8 %copy-start.13 = (bf16[2,2,3,24,192]{4,3,2,1,0:T(8,128)(2,1)S(1)}, bf16[2,2,3,24,192]{4,3,2,1,0:T(8,128)(2,1)}, u32[]{:S(2)}) copy-start(bf16[2,2,3,24,192]{4,3,2,1,0:T(8,128)(2,1)} %get-tuple-element.20) | copy-start | bytes 331780
  59.7 57.1 %copy-start.14 = (bf16[2,2,3,8,192]{4,3,2,1,0:T(8,128)(2,1)S(1)}, bf16[2,2,3,8,192]{4,3,2,1,0:T(8,128)(2,1)}, u32[]{:S(2)}) copy-start(bf16[2,2,3,8,192]{4,3,2,1,0:T(8,128)(2,1)} %get-tuple-element.21) | copy-start | bytes 110596
  59.7 70.1 %copy-start.4 = (bf16[2,18,24,192]{3,2,1,0:T(8,128)(2,1)S(1)}, bf16[2,18,24,192]{3,2,1,0:T(8,128)(2,1)}, u32[]{:S(2)}) copy-start(bf16[2,18,24,192]{3,2,1,0:T(8,128)(2,1)} %get-tuple-element.17) | copy-start | bytes 995332
  59.7 70.1 %copy-start.5 = (bf16[2,18,24,192]{3,2,1,0:T(8,128)(2,1)S(1)}, bf16[2,18,24,192]{3,2,1,0:T(8,128)(2,1)}, u32[]{:S(2)}) copy-start(bf16[2,18,24,192]{3,2,1,0:T(8,128)(2,1)} %get-tuple-element.18) | copy-start | bytes 995332
  108.6 22.4 %copy-start.1 = (bf16[16,176,128]{2,1,0:T(8,128)(2,1)}, bf16[16,176,128]{2,1,0:T(8,128)(2,1)S(1)}, u32[]{:S(2)}) copy-start(bf16[16,176,128]{2,1,0:T(8,128)(2,1)S(1)} %all_to_all.17.mine_ref) | copy-start | bytes 2162692
  108.6 22.4 %collective-permute-start.7 = (bf16[16,176,128]{2,1,0:T(8,128)(2,1)S(1)}, bf16[16,176,128]{2,1,0:T(8,128)(2,1)S(1)}, u32[]{:S(2)}, u32[]{:S(2)}) collective-permute-start(bf16[16,176,128]{2,1,0:T(8,128)(2,1)S(1)} %all_to_all.17.mine_ref), channel_id=1, source_target_pairs={{0,1},{1,0},{2,3},{3,2},{4,5},{5,4},{6,7},{7,6},{8,9},{9,8},{10,11... | collective-permute-start | bytes 2162696 | tf_op jit(solution)/shard_map/ppermute | solution.py:269
  113.7 16.1 %collective-permute-start.3 = (bf16[2,2,18,8,192]{4,3,2,1,0:T(8,128)(2,1)S(1)}, bf16[2,2,18,8,192]{4,3,2,1,0:T(8,128)(2,1)S(1)}, u32[]{:S(2)}, u32[]{:S(2)}) collective-permute-start(bf16[2,2,18,8,192]{4,3,2,1,0:T(8,128)(2,1)S(1)} %copy-done.12), channel_id=1, source_target_pairs={{0,16},{16,32},{32,48},{48,64},{64,80},{80,96},{96,112},{112,128},... | collective-permute-start | bytes 663560 | tf_op jit(solution)/shard_map/ppermute | solution.py:269
  115.5 14.3 %collective-permute-start.4 = (bf16[2,2,3,24,192]{4,3,2,1,0:T(8,128)(2,1)S(1)}, bf16[2,2,3,24,192]{4,3,2,1,0:T(8,128)(2,1)S(1)}, u32[]{:S(2)}, u32[]{:S(2)}) collective-permute-start(bf16[2,2,3,24,192]{4,3,2,1,0:T(8,128)(2,1)S(1)} %copy-done.13), channel_id=1, source_target_pairs={{0,2},{2,4},{4,6},{6,8},{8,10},{10,12},{12,14},{14,0},{1,3},{3,5},... | collective-permute-start | bytes 331784 | tf_op jit(solution)/shard_map/ppermute | solution.py:269
  116.8 9.7 %collective-permute-start.5 = (bf16[2,2,3,8,192]{4,3,2,1,0:T(8,128)(2,1)S(1)}, bf16[2,2,3,8,192]{4,3,2,1,0:T(8,128)(2,1)S(1)}, u32[]{:S(2)}, u32[]{:S(2)}) collective-permute-start(bf16[2,2,3,8,192]{4,3,2,1,0:T(8,128)(2,1)S(1)} %copy-done.14), channel_id=1, source_target_pairs={{0,18},{2,20},{4,22},{6,24},{8,26},{10,28},{12,30},{14,16},{16,34}... | collective-permute-start | bytes 110600 | tf_op jit(solution)/shard_map/ppermute | solution.py:269
  131.0 0.9 copy-start.3

commit v2 on v1

--- a/solution.py
+++ b/solution.py
@@ -1,5 +1,3 @@
-import functools
-
 import jax
 import jax.numpy as jnp
 from jax import lax
@@ -22,7 +20,6 @@
 G_ROWS = 40
 T_ROWS = 16
 SHARD = 176
-VMEM = pltpu.CompilerParams(vmem_limit_bytes=56 * 2**20)
 
 
 def dot(a, b, ca, cb):
@@ -41,19 +38,44 @@
             yield ab_p, ab_r, (((a_p * WL + a_r) * WLAT + b_p) * WLAT + b_r) * SPAN
 
 
-def toeplitz(target, c):
-    return (iota((384, POINTS), 0) == target + (WLON - 1 - c)).astype(BF16)
-
-
-def expand_kernel(table_ref, target_ref, order_ref, bias_ref, rows_ref):
+def tokens():
+    p = iota((1, POINTS), 1)
+    c_p = (p * 21846) >> 18
+    return c_p, p - c_p * AB
+
+
+def toeplitz(c):
+    c_p, ab_p = tokens()
+    return (iota((384, POINTS), 0) == ab_p * SPAN + c_p + (WLON - 1 - c)).astype(BF16)
+
+
+def heads_first():
+    n = iota((96, 96), 0)
+    return ((iota((96, 96), 1) == (n & 15) * 8 + (n >> 4)) & ((n & 15) < AB)).astype(BF16)
+
+
+def strips_kernel(x_ref, y_ref, lon_ref, lat_ref, cor_ref):
+    for k, ref in enumerate((x_ref, y_ref)):
+        lon_ref[k] = ref[:, :, 0:8, :]
+        lat_ref[k] = ref[:, 0:3, :, :]
+        cor_ref[k] = ref[:, 0:3, 0:8, :]
+
+
+def shadow_kernel(
+    lat_ref, table_ref, gain_ref, win_ref, wout_ref, mask_ref,
+    bias_ref, win_t_ref, wout_t_ref, gain_out, region_ref, own_ref, rows_ref, ids_ref,
+):
+    first = lat_ref[0] * TAB
+    for t in range(TAB):
+        for h in range(HEADS):
+            own_ref[t, h : h + 1, :] = table_ref[h, pl.ds(first + t, 1), :]
     rows_ref[...] = jnp.zeros_like(rows_ref)
     for t in range(TAB):
         for ab_p, ab_r, start in segments():
-            rows_ref[t, ab_r * 8 : ab_r * 8 + HEADS, ab_p * SPAN : (ab_p + 1) * SPAN] = table_ref[
+            rows_ref[t, ab_r * 8 : ab_r * 8 + HEADS, ab_p * SPAN : (ab_p + 1) * SPAN] = own_ref[
                 t, :, start : start + SPAN
             ]
-    order = order_ref[...]
-    target = target_ref[...]
+    order = heads_first()
     pieces = []
     rest = [rows_ref[t] for t in range(TAB)]
     for _ in range(3):
@@ -61,15 +83,31 @@
         rest = [r - p.astype(F32) for r, p in zip(rest, low)]
         pieces.append(jnp.concatenate([dot(order, p, 1, 0).astype(BF16) for p in low], axis=0))
     for c in range(WLON):
-        pick = toeplitz(target, c)
+        pick = toeplitz(c)
         full = dot(pieces[0], pick, 1, 0) + (dot(pieces[1], pick, 1, 0) + dot(pieces[2], pick, 1, 0))
         for th in range(TAB * HEADS):
             bias_ref[th, c * AB : (c + 1) * AB, :] = full[th * 16 : th * 16 + AB, :]
+    win_t_ref[...] = win_ref[...].T
+    wout_t_ref[...] = wout_ref[...].T
+    column = jnp.broadcast_to(gain_ref[...], (8, C)).T
+    gain_out[...] = jnp.broadcast_to(column[:, 0:1], (C, POINTS))
+    ids_ref[...] = jnp.zeros_like(ids_ref)
+    c_p, ab_p = tokens()
+    for v in range(TAB):
+        for b in range(WLAT):
+            for a in range(WL):
+                at = a * WLAT + b
+                ids_ref[v, at : at + 1, 0:24] = mask_ref[v * WLAT + b, a : a + 1, :].astype(F32)
+        for w in range(2):
+            pick = (iota((128, POINTS), 0) == c_p + WLON * w).astype(BF16)
+            spread = dot(ids_ref[v].astype(BF16), pick, 1, 0)
+            own = jnp.where(iota((16, POINTS), 0) == ab_p, spread, 0.0)
+            region_ref[v, w] = jnp.sum(own, axis=0, keepdims=True)
 
 
 def main_kernel(
     ens_ref, x_ref, y_ref, lon_ref, lat_ref, cor_ref, region_ref, gain_ref, win_ref, win_t_ref, wout_ref,
-    wout_t_ref, bias_ref, place_ref, target_ref, order_ref,
+    wout_t_ref, bias_ref,
     out_ref, ig_ref, lon_out, lat_out, cor_out, keep_ref, send_ref,
     ext, grads, outer, gain_acc, dbias, blocks, rows, flat_t, flat, chunks,
 ):
@@ -82,7 +120,9 @@
     outer[...] = jnp.zeros_like(outer)
     gain_acc[...] = jnp.zeros_like(gain_acc)
     gain = gain_ref[...]
-    place = place_ref[...]
+    c_p, ab_p = tokens()
+    level = jnp.where(ab_p >= WLAT, 1, 0)
+    place = (1 - level) * (WLAT * 32) + (ab_p - level * WLAT) * 32 + WLON // 2 + c_p
 
     def row(v, carry):
         span = pl.ds(6 * v + 3, 6)
@@ -102,7 +142,7 @@
             triple = dot(win_t_ref[...], normed, 1, 0).astype(BF16)
             grad_mixed = dot(wout_ref[...], ct, 1, 0).astype(BF16)
             ids = region_ref[v, w]
-            member = (iota((8, POINTS), 0) == ids).astype(BF16)
+            member = (iota((8, POINTS), 0).astype(F32) == ids).astype(BF16)
             barred = (dot(member, member, 0, 0) - 1.0) * 1e30
             mixed, g_q, g_k, g_v = [], [], [], []
             for h in range(HEADS):
@@ -158,10 +198,10 @@
     for c in range(WLON):
         for th in range(TAB * HEADS):
             blocks[th * 16 : th * 16 + AB, :] = dbias[th, c * AB : (c + 1) * AB, :]
-        total = total + dot(blocks[...].astype(BF16), toeplitz(target_ref[...], c), 1, 1)
+        total = total + dot(blocks[...].astype(BF16), toeplitz(c), 1, 1)
     flat_t[...] = jnp.zeros_like(flat_t)
     for t in range(TAB):
-        rows[...] = dot(order_ref[...], total[t * 96 : (t + 1) * 96].astype(BF16), 0, 0)
+        rows[...] = dot(heads_first(), total[t * 96 : (t + 1) * 96].astype(BF16), 0, 0)
         for ab_p, ab_r, start in segments():
             flat_t[t * 8 : t * 8 + 8, start : start + SPAN] = rows[
                 ab_r * 8 : ab_r * 8 + 8, ab_p * SPAN : (ab_p + 1) * SPAN
@@ -197,6 +237,10 @@
     send_ref[...] = chunks[1 - me].astype(BF16)
 
 
+def over_ens_kernel(keep_ref, got_ref, out_ref):
+    out_ref[...] = (keep_ref[...] + got_ref[...].astype(F32)).astype(BF16)
+
+
 def over_lon_kernel(got_ref, out_ref):
     total = jnp.sum(got_ref[...].astype(F32), axis=0).astype(BF16)
     for k in range(out_ref.shape[0]):
@@ -211,7 +255,18 @@
         out_ref[k] = shard
 
 
-def final_kernel(ens_ref, mine_ref, other_ref, order_ref, in_ref, outer_ref, gain_ref, table_ref, both, tables, grads, full):
+def place_kernel(out_ref, grad_ref, lon_ref, lat_ref, cor_ref, out_whole, grad_whole):
+    for k, (ref, whole) in enumerate(((out_ref, out_whole), (grad_ref, grad_whole))):
+        left = ref[:, :, 0:8, :].astype(F32) + lon_ref[k].astype(F32)
+        whole[:, 3:, 0:8, :] = left[:, 3:].astype(BF16)
+        whole[:, 3:, 8:24, :] = ref[:, 3:, 8:24, :]
+        top = lat_ref[k].astype(F32)
+        corner = top[:, :, 0:8, :] + left[:, 0:3] + cor_ref[k].astype(F32)
+        whole[:, 0:3, 0:8, :] = corner.astype(BF16)
+        whole[:, 0:3, 8:24, :] = top[:, :, 8:24, :].astype(BF16)
+
+
+def final_kernel(ens_ref, mine_ref, other_ref, in_ref, outer_ref, gain_ref, table_ref, both, tables, grads, full):
     me = ens_ref[0]
     both[me] = mine_ref[...].astype(F32)
     both[1 - me] = other_ref[...].astype(F32)
@@ -238,20 +293,33 @@
             full[lat * count : (lat + 1) * count, block * 128 : (block + 1) * 128] = tables[
                 lat, block * count : (block + 1) * count, :
             ]
-    ordered = dot(order_ref[...], full[...].astype(BF16), 1, 0)
+    m = iota((144, 144), 0)
+    h24 = (m * 43691) >> 20
+    order = (iota((144, 144), 1) == (m - h24 * 24) * HEADS + h24).astype(BF16)
+    ordered = dot(order, full[...].astype(BF16), 1, 0)
     for h in range(HEADS):
         table_ref[h] = ordered[h * 24 : (h + 1) * 24, :ENTRIES]
 
 
-def vmem(count):
-    return [pl.BlockSpec(memory_space=pltpu.VMEM)] * count
-
-
 SMEM = pl.BlockSpec(memory_space=pltpu.SMEM)
-
-
-def struct(shape, dtype):
-    return jax.ShapeDtypeStruct(shape, dtype)
+WHOLE = pl.BlockSpec(memory_space=pltpu.VMEM)
+
+
+def call(kernel, outs, args, scratch=()):
+    specs = [SMEM if a.dtype == I32 and a.ndim == 1 else WHOLE for a in args]
+    shapes = tuple(pltpu.VMEM(*o) if len(o) == 2 else jax.ShapeDtypeStruct(*o[:2]) for o in outs)
+    return pl.pallas_call(
+        kernel,
+        out_shape=shapes,
+        in_specs=specs,
+        out_specs=tuple(WHOLE for _ in outs),
+        scratch_shapes=[pltpu.VMEM(*x) for x in scratch],
+        compiler_params=pltpu.CompilerParams(vmem_limit_bytes=56 * 2**20),
+    )(*args)
+
+
+def near(x):
+    return pltpu.with_memory_space_constraint(x, pltpu.VMEM)
 
 
 def passed(x, axes, sizes, moves):
@@ -278,115 +346,82 @@
     )
 
 
-def one_hot(index, width):
-    return (index[:, None] == jnp.arange(width, dtype=I32)[None, :]).astype(BF16)
-
-
 def local(inputs, cotangent, mask_ids, norm_gain, project_in, project_out, bias_table):
     x, y = inputs[0], cotangent[0]
-    lat, ens = lax.axis_index("lat"), lax.axis_index("ens")
-    pair = jnp.stack([x, y])
-    strips = halo(pair[:, :, :, 0:8], pair[:, :, 0:3], pair[:, :, 0:3, 0:8], -1)
-
-    p = jnp.arange(POINTS, dtype=I32)
-    c_p, ab_p = p // AB, p % AB
-    target = (ab_p * SPAN + c_p)[None]
-    place = ((1 - ab_p // WLAT) * (WLAT * 32) + (ab_p % WLAT) * 32 + WLON // 2 + c_p)[None]
-    n = jnp.arange(96, dtype=I32)
-    order = one_hot(jnp.where(n % 16 < AB, (n % 16) * 8 + n // 16, -1), 96)
-    table = lax.dynamic_slice_in_dim(bias_table, lat * TAB, TAB, 0)
-    bias = pl.pallas_call(
-        expand_kernel,
-        out_shape=struct((TAB * HEADS, POINTS, POINTS), F32),
-        in_specs=vmem(3),
-        out_specs=vmem(1)[0],
-        scratch_shapes=[pltpu.VMEM((TAB, 96, 384), F32)],
-        compiler_params=VMEM,
-    )(table, target, order)
-    regions = mask_ids.reshape(WL, TAB, WLAT, 2, WLON).transpose(1, 3, 4, 0, 2).reshape(TAB, 2, 1, POINTS)
-    me = ens.astype(I32).reshape(1)
-
-    out, in_grad, lon_s, lat_s, cor_s, keep, send = pl.pallas_call(
+    lat = lax.axis_index("lat").astype(I32).reshape(1)
+    me = lax.axis_index("ens").astype(I32).reshape(1)
+    strip_shapes = [((2, 2, 18, 8, C), BF16), ((2, 2, 3, 24, C), BF16), ((2, 2, 3, 8, C), BF16)]
+    strips = halo(*call(strips_kernel, strip_shapes, (x, y)), -1)
+    bias, win_t, wout_t, gain, regions = call(
+        shadow_kernel,
+        [
+            ((TAB * HEADS, POINTS, POINTS), F32),
+            ((3 * C, C), BF16),
+            ((C, C), BF16),
+            ((C, POINTS), F32),
+            ((TAB, 2, 1, POINTS), F32),
+        ],
+        (
+            lat, bias_table.transpose(1, 0, 2), norm_gain.reshape(1, C), project_in, project_out,
+            mask_ids.transpose(1, 0, 2),
+        ),
+        [((TAB, HEADS, ENTRIES), F32), ((TAB, 96, 384), F32), ((TAB, 16, 128), F32)],
+    )
+    out, in_grad, lon_s, lat_s, cor_s, keep, send = call(
         main_kernel,
-        out_shape=(
-            struct((2, 18, 24, C), BF16),
-            struct((2, 18, 24, C), BF16),
-            struct((2, 2, 18, 8, C), BF16),
-            struct((2, 2, 3, 24, C), BF16),
-            struct((2, 2, 3, 8, C), BF16),
-            struct((16, CHUNK, 128), F32),
-            struct((16, CHUNK, 128), BF16),
+        [((2, 18, 24, C), BF16)] * 2 + strip_shapes + [((16, CHUNK, 128), F32), ((16, CHUNK, 128), BF16)],
+        (
+            me, x, y, *map(near, strips), near(regions), near(gain), project_in, near(win_t), project_out,
+            near(wout_t), near(bias),
         ),
-        in_specs=[SMEM] + vmem(15),
-        out_specs=tuple(vmem(7)),
-        scratch_shapes=[
-            pltpu.VMEM((2, 2, 21, 32, C), F32),
-            pltpu.VMEM((C, 4 * C), F32),
-            pltpu.VMEM((C, C), F32),
-            pltpu.VMEM((C, POINTS), F32),
-            pltpu.VMEM((TAB * HEADS, POINTS, POINTS), F32),
-            pltpu.VMEM((TAB * HEADS * 16, POINTS), F32),
-            pltpu.VMEM((96, 384), F32),
-            pltpu.VMEM((TAB * 8, LANE_BLOCKS * 128), F32),
-            pltpu.VMEM((32 * T_ROWS, 128), F32),
-            pltpu.VMEM((2, 16, CHUNK, 128), F32),
+        [
+            ((2, 2, 21, 32, C), F32),
+            ((C, 4 * C), F32),
+            ((C, C), F32),
+            ((C, POINTS), F32),
+            ((TAB * HEADS, POINTS, POINTS), F32),
+            ((TAB * HEADS * 16, POINTS), F32),
+            ((96, 384), F32),
+            ((TAB * 8, LANE_BLOCKS * 128), F32),
+            ((32 * T_ROWS, 128), F32),
+            ((2, 16, CHUNK, 128), F32),
         ],
-        compiler_params=VMEM,
-    )(
-        me, x, y, *strips, regions, norm_gain.reshape(C, 1), project_in, project_in.T, project_out, project_out.T,
-        bias, place, target, order,
-    )
-
+    )
+
+    got = passed(send, "ens", (2,), (1,))
     strips = halo(lon_s, lat_s, cor_s, 1)
-    got = passed(send, "ens", (2,), (1,))
-    part = (keep + got.astype(F32)).astype(BF16)
+    (part,) = call(over_ens_kernel, [((16, CHUNK, 128), BF16)], (near(keep), near(got)))
     part = lax.all_to_all(part, "lon", 0, 0, tiled=True)
-    part = pl.pallas_call(
-        over_lon_kernel,
-        out_shape=struct((8, CHUNK, 128), BF16),
-        in_specs=vmem(1),
-        out_specs=vmem(1)[0],
-        compiler_params=VMEM,
-    )(part)
+    part, *strips = lax.optimization_barrier((part, *strips))
+    (part,) = call(over_lon_kernel, [((8, CHUNK, 128), BF16)], (near(part),))
     part = lax.all_to_all(part, "lat", 0, 0, tiled=True)
-    part = pl.pallas_call(
-        over_lat_kernel,
-        out_shape=struct((16, SHARD, 128), BF16),
-        in_specs=vmem(1),
-        out_specs=vmem(1)[0],
-        compiler_params=VMEM,
-    )(part)
+    (part,) = call(over_lat_kernel, [((16, SHARD, 128), BF16)], (near(part),))
     mine = lax.all_to_all(part, "lon", 0, 0, tiled=True)
     other = passed(mine, "ens", (2,), (1,))
-    m = jnp.arange(144, dtype=I32)
-    table_order = one_hot((m % 24) * HEADS + m // 24, 144)
-    in_total, out_total, gain_total, table_total = pl.pallas_call(
+    in_total, out_total, gain_total, table_total = call(
         final_kernel,
-        out_shape=(
-            struct((C, 3 * C), F32),
-            struct((C, C), F32),
-            struct((1, C), F32),
-            struct((HEADS, 24, ENTRIES), F32),
-        ),
-        in_specs=[SMEM] + vmem(3),
-        out_specs=tuple(vmem(4)),
-        scratch_shapes=[
-            pltpu.VMEM((2, 16, SHARD, 128), F32),
-            pltpu.VMEM((8, 32 * T_ROWS, 128), F32),
-            pltpu.VMEM((C, 4 * C), F32),
-            pltpu.VMEM((144, LANE_BLOCKS * 128), F32),
+        [
+            ((C, 3 * C), F32, None),
+            ((C, C), F32, None),
+            ((1, C), F32, None),
+            ((HEADS, 24, ENTRIES), F32, None),
         ],
-        compiler_params=VMEM,
-    )(me, mine, other, table_order)
-
-    both = jnp.stack([out, in_grad])
-    lon_pad = jnp.pad(strips[0], ((0, 0), (0, 0), (0, 0), (0, 16), (0, 0)))
-    lat_pad = jnp.pad(strips[1], ((0, 0), (0, 0), (0, 15), (0, 0), (0, 0)))
-    cor_pad = jnp.pad(strips[2], ((0, 0), (0, 0), (0, 15), (0, 16), (0, 0)))
-    both = both + lon_pad + lat_pad + cor_pad
+        (me, near(mine), near(other)),
+        [
+            ((2, 16, SHARD, 128), F32),
+            ((8, 32 * T_ROWS, 128), F32),
+            ((C, 4 * C), F32),
+            ((144, LANE_BLOCKS * 128), F32),
+        ],
+    )
+    out, in_grad = call(
+        place_kernel,
+        [((2, 18, 24, C), BF16, None)] * 2,
+        (near(out), near(in_grad), *map(near, strips)),
+    )
     return (
-        both[0][None],
-        both[1][None],
+        out[None],
+        in_grad[None],
         in_total,
         out_total,
         gain_total.reshape(C),

time: 136 us -> 113 us (0.83)
  blocking collectives: 45.3 us -> 31.2 us
  local copies, waits for them, and re-layouts: 9.84 us -> 0 us
  starting transfers between devices: 24.1 us -> 29.8 us
  Pallas kernels: 39.6 us -> 35.1 us
  waiting for transfers between devices: 12.3 us -> 15.8 us
  other arithmetic: 3.33 us -> 0 us
    all_to_all x1 -> x0, blocking collectives: 12.6 us -> none  [local(): part = lax.all_to_all(part, 'lon', 0, 0, tiled=True)]
    unnamed x34 -> x0, local copies, waits for them, and re-layouts: 5.29 us -> none
    pallas_call x5 -> x8, Pallas kernels: 39.6 us -> 35.1 us  [call(): pl.pallas_call(kernel, out_shape=shapes, in_specs=specs, out_specs=tuple(...]
    all_to_all x0 -> x1, starting transfers between devices: none -> 3.64 us  [local(): part = lax.all_to_all(part, 'lon', 0, 0, tiled=True)]
    ppermute x8, waiting for transfers between devices: 12.3 us -> 15.8 us  [passed(): return lax.ppermute(x, axes, pairs)]
    convert_element_type x3 -> x0, other arithmetic: 2.5 us -> none  [the longest x2 1.39 us: one_hot(): (index[:, None] == jnp.arange(width, dtype=I32)[None, :]).astype(BF16)]
    ppermute x8, starting transfers between devices: 24.1 us -> 26.1 us  [passed(): return lax.ppermute(x, axes, pairs)]
    reshape x4 -> x0, local copies, waits for them, and re-layouts: 1.77 us -> none  [the longest x3 1 us: local(): mask_ids.reshape(WL, TAB, WLAT, 2, WLON).transpose(1, 3, 4, 0, 2)]
  transfers between devices with their start and end apart: 8 -> 9, of which waited for: 3 -> 3; matrix products, arithmetic and copies ran while one was open for 6% -> 0% of each run, Pallas kernels for 5% -> 6%
where the time goes in v2:
time: 113 us
  Pallas kernels  35.1 us (31%)
  blocking collectives  31.2 us (28%)
  starting transfers between devices  29.8 us (26%)
  waiting for transfers between devices  15.8 us (14%)
    pallas_call x8, Pallas kernels, call(): pl.pallas_call(kernel, out_shape=shapes, in_specs=specs, out_specs=tuple(...  35.1 us
    ppermute x8, starting transfers between devices, passed(): return lax.ppermute(x, axes, pairs)  26.1 us
    all_to_all x1, blocking collectives, local(): mine = lax.all_to_all(part, 'lon', 0, 0, tiled=True)  21.2 us
    ppermute x8, waiting for transfers between devices, passed(): return lax.ppermute(x, axes, pairs)  15.8 us
    all_to_all x1, blocking collectives, local(): part = lax.all_to_all(part, 'lat', 0, 0, tiled=True)  9.96 us
    all_to_all x1, starting transfers between devices, local(): part = lax.all_to_all(part, 'lon', 0, 0, tiled=True)  3.64 us
  transfers between devices with their start and end apart: 9, of which 3 were waited for; matrix products, arithmetic and copies ran while one was open for 0% of the time, Pallas kernels for 6%

profile of v2, /device:TPU:1, one launch (start us, length us, event | category | flops | bytes accessed | tf_op | source)
XLA Modules:
  0.0 112.5 jit_solution(9322426354037301993)
XLA Ops:
  0.6 1.2 %shard_map.118 = (bf16[2,2,18,8,192]{4,3,2,1,0:T(8,128)(2,1)S(1)}, bf16[2,2,3,24,192]{4,3,2,1,0:T(8,128)(2,1)S(1)}, bf16[2,2,3,8,192]{4,3,2,1,0:T(8,128)(2,1)S(1)}) custom-call(bf16[2,18,24,192]{3,2,1,0:T(8,128)(2,1)} %bitcast.12, bf16[2,18,24,192]{3,2,1,0:T(8,128)(2,1)} %bitcast.14), custom_call_target="tpu_custom_call" | custom-call | tf_op jit(solution)/shard_map/pallas_call | solution.py:311
  1.8 7.4 %collective-permute-start = (bf16[2,2,18,8,192]{4,3,2,1,0:T(8,128)(2,1)S(1)}, bf16[2,2,18,8,192]{4,3,2,1,0:T(8,128)(2,1)S(1)}, u32[]{:S(2)}, u32[]{:S(2)}) collective-permute-start(bf16[2,2,18,8,192]{4,3,2,1,0:T(8,128)(2,1)S(1)} %get-tuple-element.31), channel_id=1, source_target_pairs={{0,240},{16,0},{32,16},{48,32},{64,48},{80,64},{96,80},{112,96},{1... | collective-permute-start | bytes 663560 | tf_op jit(solution)/shard_map/ppermute | solution.py:337
  9.2 4.9 %collective-permute-start.1 = (bf16[2,2,3,24,192]{4,3,2,1,0:T(8,128)(2,1)S(1)}, bf16[2,2,3,24,192]{4,3,2,1,0:T(8,128)(2,1)S(1)}, u32[]{:S(2)}, u32[]{:S(2)}) collective-permute-start(bf16[2,2,3,24,192]{4,3,2,1,0:T(8,128)(2,1)S(1)} %get-tuple-element.32), channel_id=1, source_target_pairs={{0,14},{2,0},{4,2},{6,4},{8,6},{10,8},{12,10},{14,12},{1,15},{3,1}... | collective-permute-start | bytes 331784 | tf_op jit(solution)/shard_map/ppermute | solution.py:337
  14.1 0.7 collective-permute-start.2
  14.8 5.7 %shard_map.119 = (f32[18,144,144]{2,1,0:T(8,128)S(1)}, bf16[576,192]{1,0:T(8,128)(2,1)S(1)}, bf16[192,192]{1,0:T(8,128)(2,1)S(1)}, f32[192,144]{1,0:T(8,128)S(1)}, f32[3,2,1,144]{3,2,1,0:T(1,128)S(1)}) custom-call(s32[1]{0:T(128)} %bitcast.3.lat_ref, f32[6,24,3312]{2,1,0:T(8,128)} %bitcast.11, f32[1,192]{1,0:T(1,128)} %bitcast.17, bf16[192,576]{1,0:T(8,128)(2,1)} %win_ref.3, ...), custom_call_target="tpu_custom_call" | custom-call | tf_op jit(solution)/shard_map/pallas_call | solution.py:311
  20.5 0.0 collective-permute-done.2.cor_ref
  20.5 0.0 collective-permute-done.1.lat_ref
  20.6 24.1 %shard_map.120 = (bf16[2,18,24,192]{3,2,1,0:T(8,128)(2,1)S(1)}, bf16[2,18,24,192]{3,2,1,0:T(8,128)(2,1)S(1)}, bf16[2,2,18,8,192]{4,3,2,1,0:T(8,128)(2,1)S(1)}, b...) custom-call(s32[1]{0:T(128)} %bitcast.ens_ref, ...), custom_call_target="tpu_custom_call" | custom-call | tf_op jit(solution)/shard_map/pallas_call | solution.py:311
  44.7 1.6 %collective-permute-start.3 = (bf16[16,64,128]{2,1,0:T(8,128)(2,1)S(1)}, bf16[16,64,128]{2,1,0:T(8,128)(2,1)S(1)}, u32[]{:S(2)}, u32[]{:S(2)}) collective-permute-start(bf16[16,64,128]{2,1,0:T(8,128)(2,1)S(1)} %get-tuple-element.42), channel_id=1, source_target_pairs={{0,1},{1,0},{2,3},{3,2},{4,5},{5,4},{6,7},{7,6},{8,9},{9,8},{10,11... | collective-permute-start | bytes 786440 | tf_op jit(solution)/shard_map/ppermute | solution.py:337
  46.3 1.2 %collective-permute-done.3.got_ref = bf16[16,64,128]{2,1,0:T(8,128)(2,1)S(1)} collective-permute-done((bf16[16,64,128]{2,1,0:T(8,128)(2,1)S(1)}, bf16[16,64,128]{2,1,0:T(8,128)(2,1)S(1)}, u32[]{:S(2)}, u32[]{:S(2)}) %collective-permute-start.3) | collective-permute-done | bytes 262176 | tf_op jit(solution)/shard_map/ppermute | solution.py:337
  47.4 0.7 shard_map.121
  48.2 3.6 %all-to-all-start = ((bf16[16,64,128]{2,1,0:T(8,128)(2,1)}), bf16[16,64,128]{2,1,0:T(8,128)(2,1)S(1)}, u32[]{:S(2)}, u32[]{:S(2)}) async-start(bf16[16,64,128]{2,1,0:T(8,128)(2,1)} %shard_map.121), calls=%async_computation | async-start | bytes 524288 | tf_op jit(solution)/shard_map/all_to_all | solution.py:394
  51.8 1.4 %collective-permute-start.4 = (bf16[2,2,18,8,192]{4,3,2,1,0:T(8,128)(2,1)S(1)}, bf16[2,2,18,8,192]{4,3,2,1,0:T(8,128)(2,1)S(1)}, u32[]{:S(2)}, u32[]{:S(2)}) collective-permute-start(bf16[2,2,18,8,192]{4,3,2,1,0:T(8,128)(2,1)S(1)} %get-tuple-element.43), channel_id=1, source_target_pairs={{0,16},{16,32},{32,48},{48,64},{64,80},{80,96},{96,112},{112,128},... | collective-permute-start | bytes 663560 | tf_op jit(solution)/shard_map/ppermute | solution.py:337
  53.2 3.5 %collective-permute-start.5 = (bf16[2,2,3,24,192]{4,3,2,1,0:T(8,128)(2,1)S(1)}, bf16[2,2,3,24,192]{4,3,2,1,0:T(8,128)(2,1)S(1)}, u32[]{:S(2)}, u32[]{:S(2)}) collective-permute-start(bf16[2,2,3,24,192]{4,3,2,1,0:T(8,128)(2,1)S(1)} %get-tuple-element.44), channel_id=1, source_target_pairs={{0,2},{2,4},{4,6},{6,8},{8,10},{10,12},{12,14},{14,0},{1,3},{3,5},... | collective-permute-start | bytes 331784 | tf_op jit(solution)/shard_map/ppermute | solution.py:337
  56.7 1.4 %collective-permute-start.6 = (bf16[2,2,3,8,192]{4,3,2,1,0:T(8,128)(2,1)S(1)}, bf16[2,2,3,8,192]{4,3,2,1,0:T(8,128)(2,1)S(1)}, u32[]{:S(2)}, u32[]{:S(2)}) collective-permute-start(bf16[2,2,3,8,192]{4,3,2,1,0:T(8,128)(2,1)S(1)} %get-tuple-element.45), channel_id=1, source_target_pairs={{0,18},{2,20},{4,22},{6,24},{8,26},{10,28},{12,30},{14,16},{16,34}... | collective-permute-start | bytes 110600 | tf_op jit(solution)/shard_map/ppermute | solution.py:337
  58.0 13.8 %collective-permute-done.6.cor_ref = bf16[2,2,3,8,192]{4,3,2,1,0:T(8,128)(2,1)S(1)} collective-permute-done((bf16[2,2,3,8,192]{4,3,2,1,0:T(8,128)(2,1)S(1)}, bf16[2,2,3,8,192]{4,3,2,1,0:T(8,128)(2,1)S(1)}, u32[]{:S(2)}, u32[]{:S(2)}) %collective-permute-start.6) | collective-permute-done | bytes 36896 | tf_op jit(solution)/shard_map/ppermute | solution.py:337
  71.8 0.0 collective-permute-done.5.lat_ref
  71.9 10.0 %all_to_all.15.got_ref = bf16[8,64,128]{2,1,0:T(8,128)(2,1)S(1)} all-to-all(bf16[8,64,128]{2,1,0:T(8,128)(2,1)S(1)} %shard_map.123), channel_id=1, replica_groups=mesh['lon'=16,'lat'=8,'ens'=2] {'lat'}, dimensions={0} | all-to-all | bytes 262144 | tf_op jit(solution)/shard_map/all_to_all | solution.py:397
  81.9 0.1 shard_map.124
  81.9 21.2 %all_to_all.16.mine_ref = bf16[16,176,128]{2,1,0:T(8,128)(2,1)S(1)} all-to-all(bf16[16,176,128]{2,1,0:T(8,128)(2,1)S(1)} %shard_map.124), channel_id=1, replica_groups=mesh['lon'=16,'lat'=8,'ens'=2] {'lon'}, dimensions={0} | all-to-all | bytes 1441792 | tf_op jit(solution)/shard_map/all_to_all | solution.py:399
  103.2 5.4 %collective-permute-start.7 = (bf16[16,176,128]{2,1,0:T(8,128)(2,1)S(1)}, bf16[16,176,128]{2,1,0:T(8,128)(2,1)S(1)}, u32[]{:S(2)}, u32[]{:S(2)}) collective-permute-start(bf16[16,176,128]{2,1,0:T(8,128)(2,1)S(1)} %all_to_all.16.mine_ref), channel_id=1, source_target_pairs={{0,1},{1,0},{2,3},{3,2},{4,5},{5,4},{6,7},{7,6},{8,9},{9,8},{10,11... | collective-permute-start | bytes 2162696 | tf_op jit(solution)/shard_map/ppermute | solution.py:337
  108.5 1.0 shard_map.122
  109.5 0.8 collective-permute-done.7.other_ref
  110.3 2.2 %shard_map.125 = (f32[192,576]{1,0:T(8,128)}, f32[192,192]{1,0:T(8,128)}, f32[1,192]{1,0:T(1,128)}, f32[6,24,3312]{2,1,0:T(8,128)}) custom-call(s32[1]{0:T(128)} %bitcast.ens_ref, bf16[16,176,128]{2,1,0:T(8,128)(2,1)S(1)} %all_to_all.16.mine_ref, bf16[16,176,128]{2,1,0:T(8,128)(2,1)S(1)} %collective-permute-done.7.other_ref), custom_call_target="tpu_custom_call" | custom-call | tf_op jit(solution)/shard_map/pallas_call | solution.py:311
  (4 shorter events, 0.1 us)
Async XLA Ops:
  1.8 18.7 %collective-permute-start = (bf16[2,2,18,8,192]{4,3,2,1,0:T(8,128)(2,1)S(1)}, bf16[2,2,18,8,192]{4,3,2,1,0:T(8,128)(2,1)S(1)}, u32[]{:S(2)}, u32[]{:S(2)}) collective-permute-start(bf16[2,2,18,8,192]{4,3,2,1,0:T(8,128)(2,1)S(1)} %get-tuple-element.31), channel_id=1, source_target_pairs={{0,240},{16,0},{32,16},{48,32},{64,48},{80,64},{96,80},{112,96},{1... | collective-permute-start | bytes 663560 | tf_op jit(solution)/shard_map/ppermute | solution.py:337
  9.2 11.3 %collective-permute-start.1 = (bf16[2,2,3,24,192]{4,3,2,1,0:T(8,128)(2,1)S(1)}, bf16[2,2,3,24,192]{4,3,2,1,0:T(8,128)(2,1)S(1)}, u32[]{:S(2)}, u32[]{:S(2)}) collective-permute-start(bf16[2,2,3,24,192]{4,3,2,1,0:T(8,128)(2,1)S(1)} %get-tuple-element.32), channel_id=1, source_target_pairs={{0,14},{2,0},{4,2},{6,4},{8,6},{10,8},{12,10},{14,12},{1,15},{3,1}... | collective-permute-start | bytes 331784 | tf_op jit(solution)/shard_map/ppermute | solution.py:337
  14.1 6.4 %collective-permute-start.2 = (bf16[2,2,3,8,192]{4,3,2,1,0:T(8,128)(2,1)S(1)}, bf16[2,2,3,8,192]{4,3,2,1,0:T(8,128)(2,1)S(1)}, u32[]{:S(2)}, u32[]{:S(2)}) collective-permute-start(bf16[2,2,3,8,192]{4,3,2,1,0:T(8,128)(2,1)S(1)} %get-tuple-element.33), channel_id=1, source_target_pairs={{0,254},{2,240},{4,242},{6,244},{8,246},{10,248},{12,250},{14,252}... | collective-permute-start | bytes 110600 | tf_op jit(solution)/shard_map/ppermute | solution.py:337
  44.7 2.8 %collective-permute-start.3 = (bf16[16,64,128]{2,1,0:T(8,128)(2,1)S(1)}, bf16[16,64,128]{2,1,0:T(8,128)(2,1)S(1)}, u32[]{:S(2)}, u32[]{:S(2)}) collective-permute-start(bf16[16,64,128]{2,1,0:T(8,128)(2,1)S(1)} %get-tuple-element.42), channel_id=1, source_target_pairs={{0,1},{1,0},{2,3},{3,2},{4,5},{5,4},{6,7},{7,6},{8,9},{9,8},{10,11... | collective-permute-start | bytes 786440 | tf_op jit(solution)/shard_map/ppermute | solution.py:337
  48.2 23.7 %all-to-all-start = ((bf16[16,64,128]{2,1,0:T(8,128)(2,1)}), bf16[16,64,128]{2,1,0:T(8,128)(2,1)S(1)}, u32[]{:S(2)}, u32[]{:S(2)}) async-start(bf16[16,64,128]{2,1,0:T(8,128)(2,1)} %shard_map.121), calls=%async_computation | async-start | bytes 524288 | tf_op jit(solution)/shard_map/all_to_all | solution.py:394
  51.8 20.0 %collective-permute-start.4 = (bf16[2,2,18,8,192]{4,3,2,1,0:T(8,128)(2,1)S(1)}, bf16[2,2,18,8,192]{4,3,2,1,0:T(8,128)(2,1)S(1)}, u32[]{:S(2)}, u32[]{:S(2)}) collective-permute-start(bf16[2,2,18,8,192]{4,3,2,1,0:T(8,128)(2,1)S(1)} %get-tuple-element.43), channel_id=1, source_target_pairs={{0,16},{16,32},{32,48},{48,64},{64,80},{80,96},{96,112},{112,128},... | collective-permute-start | bytes 663560 | tf_op jit(solution)/shard_map/ppermute | solution.py:337
  53.2 18.7 %collective-permute-start.5 = (bf16[2,2,3,24,192]{4,3,2,1,0:T(8,128)(2,1)S(1)}, bf16[2,2,3,24,192]{4,3,2,1,0:T(8,128)(2,1)S(1)}, u32[]{:S(2)}, u32[]{:S(2)}) collective-permute-start(bf16[2,2,3,24,192]{4,3,2,1,0:T(8,128)(2,1)S(1)} %get-tuple-element.44), channel_id=1, source_target_pairs={{0,2},{2,4},{4,6},{6,8},{8,10},{10,12},{12,14},{14,0},{1,3},{3,5},... | collective-permute-start | bytes 331784 | tf_op jit(solution)/shard_map/ppermute | solution.py:337
  56.7 15.2 %collective-permute-start.6 = (bf16[2,2,3,8,192]{4,3,2,1,0:T(8,128)(2,1)S(1)}, bf16[2,2,3,8,192]{4,3,2,1,0:T(8,128)(2,1)S(1)}, u32[]{:S(2)}, u32[]{:S(2)}) collective-permute-start(bf16[2,2,3,8,192]{4,3,2,1,0:T(8,128)(2,1)S(1)} %get-tuple-element.45), channel_id=1, source_target_pairs={{0,18},{2,20},{4,22},{6,24},{8,26},{10,28},{12,30},{14,16},{16,34}... | collective-permute-start | bytes 110600 | tf_op jit(solution)/shard_map/ppermute | solution.py:337
  103.2 7.2 %collective-permute-start.7 = (bf16[16,176,128]{2,1,0:T(8,128)(2,1)S(1)}, bf16[16,176,128]{2,1,0:T(8,128)(2,1)S(1)}, u32[]{:S(2)}, u32[]{:S(2)}) collective-permute-start(bf16[16,176,128]{2,1,0:T(8,128)(2,1)S(1)} %all_to_all.16.mine_ref), channel_id=1, source_target_pairs={{0,1},{1,0},{2,3},{3,2},{4,5},{5,4},{6,7},{7,6},{8,9},{9,8},{10,11... | collective-permute-start | bytes 2162696 | tf_op jit(solution)/shard_map/ppermute | solution.py:337

commit v3 on v2

--- a/solution.py
+++ b/solution.py
@@ -19,7 +19,7 @@
 CHUNK = 64
 G_ROWS = 40
 T_ROWS = 16
-SHARD = 176
+SHARD = 168
 
 
 def dot(a, b, ca, cb):
@@ -108,7 +108,7 @@
 def main_kernel(
     ens_ref, x_ref, y_ref, lon_ref, lat_ref, cor_ref, region_ref, gain_ref, win_ref, win_t_ref, wout_ref,
     wout_t_ref, bias_ref,
-    out_ref, ig_ref, lon_out, lat_out, cor_out, keep_ref, send_ref,
+    out_ref, ig_ref, lon_out, lat_out, keep_ref, send_ref,
     ext, grads, outer, gain_acc, dbias, blocks, rows, flat_t, flat, chunks,
 ):
     for k, ref in enumerate((x_ref, y_ref)):
@@ -120,78 +120,110 @@
     outer[...] = jnp.zeros_like(outer)
     gain_acc[...] = jnp.zeros_like(gain_acc)
     gain = gain_ref[...]
+    heads = [(iota((POINTS, C), 1) >> 5) == h for h in range(HEADS)]
     c_p, ab_p = tokens()
     level = jnp.where(ab_p >= WLAT, 1, 0)
     place = (1 - level) * (WLAT * 32) + (ab_p - level * WLAT) * 32 + WLON // 2 + c_p
 
-    def row(v, carry):
-        span = pl.ds(6 * v + 3, 6)
-        xw = ext[0, :, span].reshape(384, C).astype(BF16)
-        yw = ext[1, :, span].reshape(384, C).astype(BF16)
-        out_w = jnp.zeros((384, C), F32)
-        ig_w = jnp.zeros((384, C), F32)
-        for w in range(2):
-            pick = (iota((384, POINTS), 0) == place + WLON * w).astype(BF16)
-            xt = dot(xw, pick, 0, 0)
-            ct32 = dot(yw, pick, 0, 0)
-            ct = ct32.astype(BF16)
-            center = xt - jnp.mean(xt, axis=0, keepdims=True)
-            inverse = lax.rsqrt(jnp.mean(center * center, axis=0, keepdims=True) + EPS)
-            part = center * inverse
-            normed = (part * gain).astype(BF16)
-            triple = dot(win_t_ref[...], normed, 1, 0).astype(BF16)
-            grad_mixed = dot(wout_ref[...], ct, 1, 0).astype(BF16)
-            ids = region_ref[v, w]
-            member = (iota((8, POINTS), 0).astype(F32) == ids).astype(BF16)
-            barred = (dot(member, member, 0, 0) - 1.0) * 1e30
-            mixed, g_q, g_k, g_v = [], [], [], []
-            for h in range(HEADS):
-                lo, hi = h * HD, (h + 1) * HD
-                q, k, val = triple[lo:hi], triple[C + lo : C + hi], triple[2 * C + lo : 2 * C + hi]
-                gm = grad_mixed[lo:hi]
-                scores = dot(k, q, 0, 0) * FACTOR + (bias_ref[v * HEADS + h] + barred)
-                raised = jnp.exp(scores - jnp.max(scores, axis=0, keepdims=True))
-                prob = raised * (1.0 / jnp.sum(raised, axis=0, keepdims=True))
-                low = prob.astype(BF16)
-                mixed.append(dot(val, low, 1, 0))
-                g_prob = dot(val, gm, 0, 0)
-                g_v.append(dot(gm, low, 1, 1))
-                g_score = prob * (g_prob - jnp.sum(prob * g_prob, axis=0, keepdims=True))
-                if w == 0:
-                    dbias[v * HEADS + h] = g_score
-                else:
-                    dbias[v * HEADS + h] += g_score
-                g_low = g_score.astype(BF16)
-                g_q.append(dot(k, g_low, 1, 0) * FACTOR)
-                g_k.append(dot(q, g_low, 1, 1) * FACTOR)
-            mixed = jnp.concatenate(mixed, axis=0).astype(BF16)
-            attended = dot(wout_t_ref[...], mixed, 1, 0).astype(BF16)
-            outer[...] += dot(mixed, ct, 1, 1)
-            g_triple = jnp.concatenate(g_q + g_k + g_v, axis=0).astype(BF16)
-            grads[:, : 3 * C] += dot(normed, g_triple, 1, 1)
-            wide = dot(win_ref[...], g_triple, 1, 0).astype(BF16).astype(F32)
-            block = (xt + attended.astype(F32)).astype(BF16)
-            gain_acc[...] += wide * part
-            scaled = wide * gain
-            grad_part = inverse * (
-                scaled
-                - jnp.mean(scaled, axis=0, keepdims=True)
-                - part * jnp.mean(scaled * part, axis=0, keepdims=True)
-            )
-            in_grad = (ct32 + grad_part).astype(BF16)
-            out_w = out_w + dot(pick, block, 1, 1)
-            ig_w = ig_w + dot(pick, in_grad, 1, 1)
-        ext[0, :, span] = out_w.reshape(2, 6, 32, C)
-        ext[1, :, span] = ig_w.reshape(2, 6, 32, C)
-        return carry
-
-    lax.fori_loop(0, TAB, row, 0)
+    def window(v, w, x_rows, y_rows):
+        pick = (iota((384, POINTS), 0) == place + WLON * w).astype(BF16)
+        xt = dot(x_rows, pick, 1, 0)
+        ct32 = dot(y_rows, pick, 1, 0)
+        yield
+        ct = ct32.astype(BF16)
+        center = xt - jnp.mean(xt, axis=0, keepdims=True)
+        inverse = lax.rsqrt(jnp.mean(center * center, axis=0, keepdims=True) + EPS)
+        part = center * inverse
+        normed = (part * gain).astype(BF16)
+        yield
+        triple = dot(win_t_ref[...], normed, 1, 0).astype(BF16)
+        grad_mixed = dot(wout_ref[...], ct, 1, 0).astype(BF16)
+        yield
+        natural = dot(normed, win_ref[...], 0, 0).astype(BF16)
+        gm_n = dot(ct, wout_t_ref[...], 0, 0).astype(BF16)
+        ids = region_ref[v, w]
+        member = (iota((8, POINTS), 0).astype(F32) == ids).astype(BF16)
+        barred = (dot(member, member, 0, 0) - 1.0) * 1e30
+        yield
+        q_n, k_n, v_n = natural[:, :C], natural[:, C : 2 * C], natural[:, 2 * C :]
+        zero = jnp.zeros_like(k_n)
+        k_heads = jnp.concatenate([jnp.where(m, k_n, zero) for m in heads], axis=0)
+        v_heads = jnp.concatenate([jnp.where(m, v_n, zero) for m in heads], axis=0)
+        all_scores = dot(k_heads, triple[:C], 1, 0)
+        all_g_prob = dot(v_heads, grad_mixed, 1, 0)
+        yield
+        mixed, g_q, lows, g_lows = [], [], [], []
+        for h in range(HEADS):
+            lo, hi = h * HD, (h + 1) * HD
+            part_h = slice(h * POINTS, (h + 1) * POINTS)
+            scores = all_scores[part_h] * FACTOR + (bias_ref[v * HEADS + h] + barred)
+            raised = jnp.exp(scores - jnp.max(scores, axis=0, keepdims=True))
+            prob = raised * (1.0 / jnp.sum(raised, axis=0, keepdims=True))
+            low = prob.astype(BF16)
+            mixed.append(dot(triple[2 * C + lo : 2 * C + hi], low, 1, 0))
+            g_prob = all_g_prob[part_h]
+            g_score = prob * (g_prob - jnp.sum(prob * g_prob, axis=0, keepdims=True))
+            if w == 0:
+                dbias[v * HEADS + h] = g_score
+            else:
+                dbias[v * HEADS + h] += g_score
+            g_low = g_score.astype(BF16)
+            g_q.append(dot(triple[C + lo : C + hi], g_low, 1, 0) * FACTOR)
+            lows.append(low)
+            g_lows.append(g_low)
+            yield
+        all_g_v = dot(jnp.concatenate(lows, axis=0), gm_n, 1, 0)
+        all_g_k = dot(jnp.concatenate(g_lows, axis=0), q_n, 1, 0)
+        mixed = jnp.concatenate(mixed, axis=0).astype(BF16)
+        attended = dot(wout_t_ref[...], mixed, 1, 0).astype(BF16)
+        outer[...] += dot(mixed, ct, 1, 1)
+        yield
+        g_v, g_k = all_g_v[:POINTS], all_g_k[:POINTS]
+        for h in range(1, HEADS):
+            part_h = slice(h * POINTS, (h + 1) * POINTS)
+            g_v = jnp.where(heads[h], all_g_v[part_h], g_v)
+            g_k = jnp.where(heads[h], all_g_k[part_h], g_k)
+        g_q = jnp.concatenate(g_q, axis=0).astype(BF16)
+        g_k = (g_k * FACTOR).astype(BF16)
+        g_v = g_v.astype(BF16)
+        wide = dot(win_ref[:, :C], g_q, 1, 0)
+        wide = wide + dot(win_ref[:, C : 2 * C], g_k, 1, 1) + dot(win_ref[:, 2 * C :], g_v, 1, 1)
+        wide = wide.astype(BF16).astype(F32)
+        yield
+        grads[:, :C] += dot(normed, g_q, 1, 1)
+        grads[:, C : 2 * C] += dot(normed, g_k, 1, 0)
+        grads[:, 2 * C : 3 * C] += dot(normed, g_v, 1, 0)
+        block = (xt + attended.astype(F32)).astype(BF16)
+        gain_acc[...] += wide * part
+        scaled = wide * gain
+        grad_part = inverse * (
+            scaled
+            - jnp.mean(scaled, axis=0, keepdims=True)
+            - part * jnp.mean(scaled * part, axis=0, keepdims=True)
+        )
+        in_grad = (ct32 + grad_part).astype(BF16)
+        yield
+        yield dot(pick, block, 1, 1), dot(pick, in_grad, 1, 1)
+
+    def rows_of(k, v):
+        return ext[k, :, 6 * v + 3 : 6 * v + 9].reshape(384, C).astype(BF16).T
+
+    def group(chosen):
+        results = [None]
+        todo = [window(v, w, rows_of(0, v), rows_of(1, v)) for v in chosen for w in range(2)]
+        while results[0] is None:
+            results = [next(g) for g in todo]
+        for i, v in enumerate(chosen):
+            for k in range(2):
+                total = results[2 * i][k] + results[2 * i + 1][k]
+                ext[k, :, 6 * v + 3 : 6 * v + 9] = total.reshape(2, 6, 32, C)
+
+    group(range(TAB))
     for k, ref in enumerate((out_ref, ig_ref)):
         ext[k, :, 0:3] = jnp.zeros((2, 3, 32, C), F32)
         ref[...] = ext[k, :, 0:18, 0:24, :].astype(BF16)
-        lon_out[k] = ext[k, :, 0:18, 24:32, :].astype(BF16)
+        lon_out[k] = ext[k, :, 3:21, 24:32, :].astype(BF16)
         lat_out[k] = ext[k, :, 18:21, 0:24, :].astype(BF16)
-        cor_out[k] = ext[k, :, 18:21, 24:32, :].astype(BF16)
 
     blocks[...] = jnp.zeros_like(blocks)
     total = jnp.zeros((TAB * HEADS * 16, 384), F32)
@@ -247,23 +279,23 @@
         out_ref[k] = total
 
 
-def over_lat_kernel(got_ref, out_ref):
+def over_lat_kernel(got_ref, lon_ref, lat_ref, out_ref, lat_out):
+    lat_out[:, :, :, 8:24, :] = lat_ref[:, :, :, 8:24, :]
+    corner = lat_ref[:, :, :, 0:8, :].astype(F32) + lon_ref[:, :, 15:18].astype(F32)
+    lat_out[:, :, :, 0:8, :] = corner.astype(BF16)
     got = got_ref[...].astype(F32)
-    total = jnp.sum(got[:, : G_ROWS + 8], axis=0)
+    total = jnp.sum(got[:, :G_ROWS], axis=0)
     shard = jnp.concatenate([total] + [got[k, G_ROWS : G_ROWS + T_ROWS] for k in range(8)], axis=0).astype(BF16)
     for k in range(out_ref.shape[0]):
         out_ref[k] = shard
 
 
-def place_kernel(out_ref, grad_ref, lon_ref, lat_ref, cor_ref, out_whole, grad_whole):
+def place_kernel(out_ref, grad_ref, lon_ref, lat_ref, out_whole, grad_whole):
     for k, (ref, whole) in enumerate(((out_ref, out_whole), (grad_ref, grad_whole))):
-        left = ref[:, :, 0:8, :].astype(F32) + lon_ref[k].astype(F32)
-        whole[:, 3:, 0:8, :] = left[:, 3:].astype(BF16)
+        left = ref[:, 3:, 0:8, :].astype(F32) + lon_ref[k, :, 0:15].astype(F32)
+        whole[:, 3:, 0:8, :] = left.astype(BF16)
         whole[:, 3:, 8:24, :] = ref[:, 3:, 8:24, :]
-        top = lat_ref[k].astype(F32)
-        corner = top[:, :, 0:8, :] + left[:, 0:3] + cor_ref[k].astype(F32)
-        whole[:, 0:3, 0:8, :] = corner.astype(BF16)
-        whole[:, 0:3, 8:24, :] = top[:, :, 8:24, :].astype(BF16)
+        whole[:, 0:3] = lat_ref[k]
 
 
 def final_kernel(ens_ref, mine_ref, other_ref, in_ref, outer_ref, gain_ref, table_ref, both, tables, grads, full):
@@ -285,7 +317,7 @@
     for lat in range(8):
         for chunk in range(32):
             tables[lat, chunk * T_ROWS : (chunk + 1) * T_ROWS, :] = both[
-                chunk // 16, chunk % 16, G_ROWS + 8 + lat * T_ROWS : G_ROWS + 8 + (lat + 1) * T_ROWS, :
+                chunk // 16, chunk % 16, G_ROWS + lat * T_ROWS : G_ROWS + (lat + 1) * T_ROWS, :
             ]
     count = TAB * HEADS
     for lat in range(8):
@@ -346,13 +378,11 @@
     )
 
 
-def local(inputs, cotangent, mask_ids, norm_gain, project_in, project_out, bias_table):
-    x, y = inputs[0], cotangent[0]
-    lat = lax.axis_index("lat").astype(I32).reshape(1)
-    me = lax.axis_index("ens").astype(I32).reshape(1)
-    strip_shapes = [((2, 2, 18, 8, C), BF16), ((2, 2, 3, 24, C), BF16), ((2, 2, 3, 8, C), BF16)]
-    strips = halo(*call(strips_kernel, strip_shapes, (x, y)), -1)
-    bias, win_t, wout_t, gain, regions = call(
+STRIPS = [((2, 2, 18, 8, C), BF16), ((2, 2, 3, 24, C), BF16), ((2, 2, 3, 8, C), BF16)]
+
+
+def run_shadow(lat, bias_table, norm_gain, project_in, project_out, mask_ids):
+    return call(
         shadow_kernel,
         [
             ((TAB * HEADS, POINTS, POINTS), F32),
@@ -367,9 +397,12 @@
         ),
         [((TAB, HEADS, ENTRIES), F32), ((TAB, 96, 384), F32), ((TAB, 16, 128), F32)],
     )
-    out, in_grad, lon_s, lat_s, cor_s, keep, send = call(
+
+
+def run_main(me, x, y, strips, regions, gain, project_in, win_t, project_out, wout_t, bias):
+    return call(
         main_kernel,
-        [((2, 18, 24, C), BF16)] * 2 + strip_shapes + [((16, CHUNK, 128), F32), ((16, CHUNK, 128), BF16)],
+        [((2, 18, 24, C), BF16)] * 2 + STRIPS[:2] + [((16, CHUNK, 128), F32), ((16, CHUNK, 128), BF16)],
         (
             me, x, y, *map(near, strips), near(regions), near(gain), project_in, near(win_t), project_out,
             near(wout_t), near(bias),
@@ -388,15 +421,30 @@
         ],
     )
 
+
+def local(inputs, cotangent, mask_ids, norm_gain, project_in, project_out, bias_table):
+    x, y = inputs[0], cotangent[0]
+    lat = lax.axis_index("lat").astype(I32).reshape(1)
+    me = lax.axis_index("ens").astype(I32).reshape(1)
+    strips = halo(*call(strips_kernel, STRIPS, (x, y)), -1)
+    bias, win_t, wout_t, gain, regions = run_shadow(lat, bias_table, norm_gain, project_in, project_out, mask_ids)
+    out, in_grad, lon_s, lat_s, keep, send = run_main(
+        me, x, y, strips, regions, gain, project_in, win_t, project_out, wout_t, bias
+    )
     got = passed(send, "ens", (2,), (1,))
-    strips = halo(lon_s, lat_s, cor_s, 1)
     (part,) = call(over_ens_kernel, [((16, CHUNK, 128), BF16)], (near(keep), near(got)))
     part = lax.all_to_all(part, "lon", 0, 0, tiled=True)
-    part, *strips = lax.optimization_barrier((part, *strips))
     (part,) = call(over_lon_kernel, [((8, CHUNK, 128), BF16)], (near(part),))
+    lon_s = passed(lon_s, "lon", (lax.axis_size("lon"),), (1,))
     part = lax.all_to_all(part, "lat", 0, 0, tiled=True)
-    (part,) = call(over_lat_kernel, [((16, SHARD, 128), BF16)], (near(part),))
+    part, lat_s = call(
+        over_lat_kernel,
+        [((16, SHARD, 128), BF16), STRIPS[1]],
+        (near(part), near(lon_s), near(lat_s)),
+    )
+    lat_s = passed(lat_s, "lat", (lax.axis_size("lat"),), (1,))
     mine = lax.all_to_all(part, "lon", 0, 0, tiled=True)
+    mine, lat_s = lax.optimization_barrier((mine, lat_s))
     other = passed(mine, "ens", (2,), (1,))
     in_total, out_total, gain_total, table_total = call(
         final_kernel,
@@ -417,7 +465,7 @@
     out, in_grad = call(
         place_kernel,
         [((2, 18, 24, C), BF16, None)] * 2,
-        (near(out), near(in_grad), *map(near, strips)),
+        (near(out), near(in_grad), near(lon_s), near(lat_s)),
     )
     return (
         out[None],

time: 113 us -> 96.5 us (0.85)
  blocking collectives: 31.2 us -> 0 us
  waiting for transfers between devices: 15.8 us -> 29.9 us
  starting transfers between devices: 29.8 us -> 38.7 us
  Pallas kernels: 35.1 us -> 26.7 us
    all_to_all x2 -> x0, blocking collectives: 31.2 us -> none  [the longest x1 21.2 us: local(): mine = lax.all_to_all(part, 'lon', 0, 0, tiled=True)]
    all_to_all x0 -> x2, starting transfers between devices: none -> 12 us  [the longest x1 7.1 us: local(): part = lax.all_to_all(part, 'lat', 0, 0, tiled=True)]
    all_to_all x0 -> x2, waiting for transfers between devices: none -> 11.9 us  [the longest x1 7.05 us: local(): part = lax.all_to_all(part, 'lat', 0, 0, tiled=True)]
    pallas_call x8, Pallas kernels: 35.1 us -> 26.7 us  [call(): pl.pallas_call(kernel, out_shape=shapes, in_specs=specs, out_specs=tuple(...]
    all_to_all x1, waiting for transfers between devices: 0.01 us -> 7.48 us  [local(): part = lax.all_to_all(part, 'lon', 0, 0, tiled=True)]
    ppermute x8 -> x7, waiting for transfers between devices: 15.8 us -> 10.5 us  [passed(): return lax.ppermute(x, axes, pairs)]
    ppermute x8 -> x7, starting transfers between devices: 26.1 us -> 23.1 us  [passed(): return lax.ppermute(x, axes, pairs)]
  transfers between devices with their start and end apart: 9 -> 10, of which waited for: 3 -> 6; matrix products, arithmetic and copies ran while one was open for 0% -> 0% of each run, Pallas kernels for 6% -> 8%
where the time goes in v3:
time: 96.5 us; the launch traced here: 96 us
  starting transfers between devices  38.7 us (40%)
  waiting for transfers between devices  29.9 us (31%)
  Pallas kernels  26.7 us (28%)
    pallas_call x8, Pallas kernels, call(): pl.pallas_call(kernel, out_shape=shapes, in_specs=specs, out_specs=tuple(...  26.7 us
    ppermute x7, starting transfers between devices, passed(): return lax.ppermute(x, axes, pairs)  23.1 us
    ppermute x7, waiting for transfers between devices, passed(): return lax.ppermute(x, axes, pairs)  10.5 us
    all_to_all x1, waiting for transfers between devices, local(): part = lax.all_to_all(part, 'lon', 0, 0, tiled=True)  7.48 us
    all_to_all x1, starting transfers between devices, local(): part = lax.all_to_all(part, 'lat', 0, 0, tiled=True)  7.1 us
    all_to_all x1, waiting for transfers between devices, local(): part = lax.all_to_all(part, 'lat', 0, 0, tiled=True)  7.05 us
    all_to_all x1, waiting for transfers between devices, local(): mine = lax.all_to_all(part, 'lon', 0, 0, tiled=True)  4.89 us
    all_to_all x1, starting transfers between devices, local(): mine = lax.all_to_all(part, 'lon', 0, 0, tiled=True)  4.86 us
  transfers between devices with their start and end apart: 10, of which 6 were waited for; matrix products, arithmetic and copies ran while one was open for 0% of the time, Pallas kernels for 8%

profile of v3, /device:TPU:1, one launch (start us, length us, event | category | flops | bytes accessed | tf_op | source)
XLA Modules:
  0.0 96.0 jit_solution(9722595950803982110)
XLA Ops:
  0.6 1.2 %shard_map.118 = (bf16[2,2,18,8,192]{4,3,2,1,0:T(8,128)(2,1)S(1)}, bf16[2,2,3,24,192]{4,3,2,1,0:T(8,128)(2,1)S(1)}, bf16[2,2,3,8,192]{4,3,2,1,0:T(8,128)(2,1)S(1)}) custom-call(bf16[2,18,24,192]{3,2,1,0:T(8,128)(2,1)} %bitcast.12, bf16[2,18,24,192]{3,2,1,0:T(8,128)(2,1)} %bitcast.14), custom_call_target="tpu_custom_call" | custom-call | tf_op jit(solution)/shard_map/pallas_call | solution.py:343
  1.8 7.4 %collective-permute-start = (bf16[2,2,18,8,192]{4,3,2,1,0:T(8,128)(2,1)S(1)}, bf16[2,2,18,8,192]{4,3,2,1,0:T(8,128)(2,1)S(1)}, u32[]{:S(2)}, u32[]{:S(2)}) collective-permute-start(bf16[2,2,18,8,192]{4,3,2,1,0:T(8,128)(2,1)S(1)} %get-tuple-element.30), channel_id=1, source_target_pairs={{0,240},{16,0},{32,16},{48,32},{64,48},{80,64},{96,80},{112,96},{1... | collective-permute-start | bytes 663560 | tf_op jit(solution)/shard_map/ppermute | solution.py:369
  9.2 4.9 %collective-permute-start.1 = (bf16[2,2,3,24,192]{4,3,2,1,0:T(8,128)(2,1)S(1)}, bf16[2,2,3,24,192]{4,3,2,1,0:T(8,128)(2,1)S(1)}, u32[]{:S(2)}, u32[]{:S(2)}) collective-permute-start(bf16[2,2,3,24,192]{4,3,2,1,0:T(8,128)(2,1)S(1)} %get-tuple-element.31), channel_id=1, source_target_pairs={{0,14},{2,0},{4,2},{6,4},{8,6},{10,8},{12,10},{14,12},{1,15},{3,1}... | collective-permute-start | bytes 331784 | tf_op jit(solution)/shard_map/ppermute | solution.py:369
  14.1 0.7 collective-permute-start.2
  14.8 5.7 %shard_map.119 = (f32[18,144,144]{2,1,0:T(8,128)S(1)}, bf16[576,192]{1,0:T(8,128)(2,1)S(1)}, bf16[192,192]{1,0:T(8,128)(2,1)S(1)}, f32[192,144]{1,0:T(8,128)S(1)}, f32[3,2,1,144]{3,2,1,0:T(1,128)S(1)}) custom-call(s32[1]{0:T(128)} %bitcast.3.lat_ref, f32[6,24,3312]{2,1,0:T(8,128)} %bitcast.11, f32[1,192]{1,0:T(1,128)} %bitcast.17, bf16[192,576]{1,0:T(8,128)(2,1)} %win_ref.3, ...), custom_call_target="tpu_custom_call" | custom-call | tf_op jit(solution)/shard_map/pallas_call | solution.py:343
  20.6 14.3 %shard_map.120 = (bf16[2,18,24,192]{3,2,1,0:T(8,128)(2,1)S(1)}, bf16[2,18,24,192]{3,2,1,0:T(8,128)(2,1)S(1)}, bf16[2,2,18,8,192]{4,3,2,1,0:T(8,128)(2,1)S(1)}, b...) custom-call(s32[1]{0:T(128)} %bitcast.ens_ref, ...), custom_call_target="tpu_custom_call" | custom-call | tf_op jit(solution)/shard_map/pallas_call | solution.py:343
  34.8 1.6 %collective-permute-start.4 = (bf16[16,64,128]{2,1,0:T(8,128)(2,1)S(1)}, bf16[16,64,128]{2,1,0:T(8,128)(2,1)S(1)}, u32[]{:S(2)}, u32[]{:S(2)}) collective-permute-start(bf16[16,64,128]{2,1,0:T(8,128)(2,1)S(1)} %get-tuple-element.42), channel_id=1, source_target_pairs={{0,1},{1,0},{2,3},{3,2},{4,5},{5,4},{6,7},{7,6},{8,9},{9,8},{10,11... | collective-permute-start | bytes 786440 | tf_op jit(solution)/shard_map/ppermute | solution.py:369
  36.4 1.2 %collective-permute-done.4.got_ref = bf16[16,64,128]{2,1,0:T(8,128)(2,1)S(1)} collective-permute-done((bf16[16,64,128]{2,1,0:T(8,128)(2,1)S(1)}, bf16[16,64,128]{2,1,0:T(8,128)(2,1)S(1)}, u32[]{:S(2)}, u32[]{:S(2)}) %collective-permute-start.4) | collective-permute-done | bytes 262176 | tf_op jit(solution)/shard_map/ppermute | solution.py:369
  37.6 0.7 shard_map.121
  38.3 3.6 %all-to-all-start = ((bf16[16,64,128]{2,1,0:T(8,128)(2,1)}), bf16[16,64,128]{2,1,0:T(8,128)(2,1)S(1)}, u32[]{:S(2)}, u32[]{:S(2)}) async-start(bf16[16,64,128]{2,1,0:T(8,128)(2,1)} %shard_map.121), calls=%async_computation | async-start | bytes 524288 | tf_op jit(solution)/shard_map/all_to_all | solution.py:436
  42.0 1.4 %collective-permute-start.3 = (bf16[2,2,18,8,192]{4,3,2,1,0:T(8,128)(2,1)S(1)}, bf16[2,2,18,8,192]{4,3,2,1,0:T(8,128)(2,1)S(1)}, u32[]{:S(2)}, u32[]{:S(2)}) collective-permute-start(bf16[2,2,18,8,192]{4,3,2,1,0:T(8,128)(2,1)S(1)} %get-tuple-element.40), channel_id=1, source_target_pairs={{0,16},{16,32},{32,48},{48,64},{64,80},{80,96},{96,112},{112,128},... | collective-permute-start | bytes 663560 | tf_op jit(solution)/shard_map/ppermute | solution.py:369
  43.3 7.5 %all-to-all-done.got_ref = bf16[16,64,128]{2,1,0:T(8,128)(2,1)S(1)} async-done(((bf16[16,64,128]{2,1,0:T(8,128)(2,1)}), bf16[16,64,128]{2,1,0:T(8,128)(2,1)S(1)}, u32[]{:S(2)}, u32[]{:S(2)}) %all-to-all-start) | async-done | bytes 262176 | tf_op jit(solution)/shard_map/all_to_all | solution.py:436
  50.8 0.7 shard_map.122
  51.5 7.1 %all-to-all-start.1 = ((bf16[8,64,128]{2,1,0:T(8,128)(2,1)}), bf16[8,64,128]{2,1,0:T(8,128)(2,1)S(1)}, u32[]{:S(2)}, u32[]{:S(2)}) async-start(bf16[8,64,128]{2,1,0:T(8,128)(2,1)} %shard_map.122), calls=%async_computation.1 | async-start | bytes 262144 | tf_op jit(solution)/shard_map/all_to_all | solution.py:439
  58.6 7.0 %all-to-all-done.1.got_ref = bf16[8,64,128]{2,1,0:T(8,128)(2,1)S(1)} async-done(((bf16[8,64,128]{2,1,0:T(8,128)(2,1)}), bf16[8,64,128]{2,1,0:T(8,128)(2,1)S(1)}, u32[]{:S(2)}, u32[]{:S(2)}) %all-to-all-start.1) | async-done | bytes 131104 | tf_op jit(solution)/shard_map/all_to_all | solution.py:439
  65.7 0.9 shard_map.123
  66.6 4.9 %all-to-all-start.2 = ((bf16[16,168,128]{2,1,0:T(8,128)(2,1)}), bf16[16,168,128]{2,1,0:T(8,128)(2,1)S(1)}, u32[]{:S(2)}, u32[]{:S(2)}) async-start(bf16[16,168,128]{2,1,0:T(8,128)(2,1)} %get-tuple-element.44), calls=%async_computation.2 | async-start | bytes 1376256 | tf_op jit(solution)/shard_map/all_to_all | solution.py:446
  71.5 1.4 %collective-permute-start.5 = (bf16[2,2,3,24,192]{4,3,2,1,0:T(8,128)(2,1)S(1)}, bf16[2,2,3,24,192]{4,3,2,1,0:T(8,128)(2,1)S(1)}, u32[]{:S(2)}, u32[]{:S(2)}) collective-permute-start(bf16[2,2,3,24,192]{4,3,2,1,0:T(8,128)(2,1)S(1)} %get-tuple-element.45), channel_id=1, source_target_pairs={{0,2},{2,4},{4,6},{6,8},{8,10},{10,12},{12,14},{14,0},{1,3},{3,5},... | collective-permute-start | bytes 331784 | tf_op jit(solution)/shard_map/ppermute | solution.py:369
  72.9 8.6 %collective-permute-done.5.lat_ref = bf16[2,2,3,24,192]{4,3,2,1,0:T(8,128)(2,1)S(1)} collective-permute-done((bf16[2,2,3,24,192]{4,3,2,1,0:T(8,128)(2,1)S(1)}, bf16[2,2,3,24,192]{4,3,2,1,0:T(8,128)(2,1)S(1)}, u32[]{:S(2)}, u32[]{:S(2)}) %collective-permute-start.5) | collective-permute-done | bytes 110624 | tf_op jit(solution)/shard_map/ppermute | solution.py:369
  81.5 4.9 %all-to-all-done.2.mine_ref = bf16[16,168,128]{2,1,0:T(8,128)(2,1)S(1)} async-done(((bf16[16,168,128]{2,1,0:T(8,128)(2,1)}), bf16[16,168,128]{2,1,0:T(8,128)(2,1)S(1)}, u32[]{:S(2)}, u32[]{:S(2)}) %all-to-all-start.2) | async-done | bytes 688160 | tf_op jit(solution)/shard_map/all_to_all | solution.py:446
  86.4 5.7 %collective-permute-start.6 = (bf16[16,168,128]{2,1,0:T(8,128)(2,1)S(1)}, bf16[16,168,128]{2,1,0:T(8,128)(2,1)S(1)}, u32[]{:S(2)}, u32[]{:S(2)}) collective-permute-start(bf16[16,168,128]{2,1,0:T(8,128)(2,1)S(1)} %all-to-all-done.2.mine_ref), channel_id=1, source_target_pairs={{0,1},{1,0},{2,3},{3,2},{4,5},{5,4},{6,7},{7,6},{8,9},{9,8},{10,11... | collective-permute-start | bytes 2064392 | tf_op jit(solution)/shard_map/ppermute | solution.py:369
  92.1 1.0 %shard_map.124 = (bf16[2,18,24,192]{3,2,1,0:T(8,128)(2,1)}, bf16[2,18,24,192]{3,2,1,0:T(8,128)(2,1)}) custom-call(bf16[2,18,24,192]{3,2,1,0:T(8,128)(2,1)S(1)} %get-tuple-element.38.out_ref, bf16[2,18,24,192]{3,2,1,0:T(8,128)(2,1)S(1)} %get-tuple-element.39.grad_ref, bf16[2,2,18,8,192]{4,3,2,1,0:T(8,128)(2,1)S(1)} %collective-permute-done.3.lon_ref, ...), custom_call_target="tpu_custom_call" | custom-call | tf_op jit(solution)/shard_map/pallas_call | solution.py:343
  93.1 0.8 collective-permute-done.6.other_ref
  93.8 2.2 %shard_map.125 = (f32[192,576]{1,0:T(8,128)}, f32[192,192]{1,0:T(8,128)}, f32[1,192]{1,0:T(1,128)}, f32[6,24,3312]{2,1,0:T(8,128)}) custom-call(s32[1]{0:T(128)} %bitcast.ens_ref, bf16[16,168,128]{2,1,0:T(8,128)(2,1)S(1)} %all-to-all-done.2.mine_ref, bf16[16,168,128]{2,1,0:T(8,128)(2,1)S(1)} %collective-permute-done.6.other_ref), custom_call_target="tpu_custom_call" | custom-call | tf_op jit(solution)/shard_map/pallas_call | solution.py:343
  (4 shorter events, 0.0 us)
Async XLA Ops:
  1.8 18.7 %collective-permute-start = (bf16[2,2,18,8,192]{4,3,2,1,0:T(8,128)(2,1)S(1)}, bf16[2,2,18,8,192]{4,3,2,1,0:T(8,128)(2,1)S(1)}, u32[]{:S(2)}, u32[]{:S(2)}) collective-permute-start(bf16[2,2,18,8,192]{4,3,2,1,0:T(8,128)(2,1)S(1)} %get-tuple-element.30), channel_id=1, source_target_pairs={{0,240},{16,0},{32,16},{48,32},{64,48},{80,64},{96,80},{112,96},{1... | collective-permute-start | bytes 663560 | tf_op jit(solution)/shard_map/ppermute | solution.py:369
  9.2 11.3 %collective-permute-start.1 = (bf16[2,2,3,24,192]{4,3,2,1,0:T(8,128)(2,1)S(1)}, bf16[2,2,3,24,192]{4,3,2,1,0:T(8,128)(2,1)S(1)}, u32[]{:S(2)}, u32[]{:S(2)}) collective-permute-start(bf16[2,2,3,24,192]{4,3,2,1,0:T(8,128)(2,1)S(1)} %get-tuple-element.31), channel_id=1, source_target_pairs={{0,14},{2,0},{4,2},{6,4},{8,6},{10,8},{12,10},{14,12},{1,15},{3,1}... | collective-permute-start | bytes 331784 | tf_op jit(solution)/shard_map/ppermute | solution.py:369
  14.1 6.4 %collective-permute-start.2 = (bf16[2,2,3,8,192]{4,3,2,1,0:T(8,128)(2,1)S(1)}, bf16[2,2,3,8,192]{4,3,2,1,0:T(8,128)(2,1)S(1)}, u32[]{:S(2)}, u32[]{:S(2)}) collective-permute-start(bf16[2,2,3,8,192]{4,3,2,1,0:T(8,128)(2,1)S(1)} %get-tuple-element.32), channel_id=1, source_target_pairs={{0,254},{2,240},{4,242},{6,244},{8,246},{10,248},{12,250},{14,252}... | collective-permute-start | bytes 110600 | tf_op jit(solution)/shard_map/ppermute | solution.py:369
  34.8 2.8 %collective-permute-start.4 = (bf16[16,64,128]{2,1,0:T(8,128)(2,1)S(1)}, bf16[16,64,128]{2,1,0:T(8,128)(2,1)S(1)}, u32[]{:S(2)}, u32[]{:S(2)}) collective-permute-start(bf16[16,64,128]{2,1,0:T(8,128)(2,1)S(1)} %get-tuple-element.42), channel_id=1, source_target_pairs={{0,1},{1,0},{2,3},{3,2},{4,5},{5,4},{6,7},{7,6},{8,9},{9,8},{10,11... | collective-permute-start | bytes 786440 | tf_op jit(solution)/shard_map/ppermute | solution.py:369
  38.3 12.5 %all-to-all-start = ((bf16[16,64,128]{2,1,0:T(8,128)(2,1)}), bf16[16,64,128]{2,1,0:T(8,128)(2,1)S(1)}, u32[]{:S(2)}, u32[]{:S(2)}) async-start(bf16[16,64,128]{2,1,0:T(8,128)(2,1)} %shard_map.121), calls=%async_computation | async-start | bytes 524288 | tf_op jit(solution)/shard_map/all_to_all | solution.py:436
  42.0 16.7 %collective-permute-start.3 = (bf16[2,2,18,8,192]{4,3,2,1,0:T(8,128)(2,1)S(1)}, bf16[2,2,18,8,192]{4,3,2,1,0:T(8,128)(2,1)S(1)}, u32[]{:S(2)}, u32[]{:S(2)}) collective-permute-start(bf16[2,2,18,8,192]{4,3,2,1,0:T(8,128)(2,1)S(1)} %get-tuple-element.40), channel_id=1, source_target_pairs={{0,16},{16,32},{32,48},{48,64},{64,80},{80,96},{96,112},{112,128},... | collective-permute-start | bytes 663560 | tf_op jit(solution)/shard_map/ppermute | solution.py:369
  51.5 14.2 %all-to-all-start.1 = ((bf16[8,64,128]{2,1,0:T(8,128)(2,1)}), bf16[8,64,128]{2,1,0:T(8,128)(2,1)S(1)}, u32[]{:S(2)}, u32[]{:S(2)}) async-start(bf16[8,64,128]{2,1,0:T(8,128)(2,1)} %shard_map.122), calls=%async_computation.1 | async-start | bytes 262144 | tf_op jit(solution)/shard_map/all_to_all | solution.py:439
  66.6 19.8 %all-to-all-start.2 = ((bf16[16,168,128]{2,1,0:T(8,128)(2,1)}), bf16[16,168,128]{2,1,0:T(8,128)(2,1)S(1)}, u32[]{:S(2)}, u32[]{:S(2)}) async-start(bf16[16,168,128]{2,1,0:T(8,128)(2,1)} %get-tuple-element.44), calls=%async_computation.2 | async-start | bytes 1376256 | tf_op jit(solution)/shard_map/all_to_all | solution.py:446
  71.5 10.0 %collective-permute-start.5 = (bf16[2,2,3,24,192]{4,3,2,1,0:T(8,128)(2,1)S(1)}, bf16[2,2,3,24,192]{4,3,2,1,0:T(8,128)(2,1)S(1)}, u32[]{:S(2)}, u32[]{:S(2)}) collective-permute-start(bf16[2,2,3,24,192]{4,3,2,1,0:T(8,128)(2,1)S(1)} %get-tuple-element.45), channel_id=1, source_target_pairs={{0,2},{2,4},{4,6},{6,8},{8,10},{10,12},{12,14},{14,0},{1,3},{3,5},... | collective-permute-start | bytes 331784 | tf_op jit(solution)/shard_map/ppermute | solution.py:369
  86.4 7.5 %collective-permute-start.6 = (bf16[16,168,128]{2,1,0:T(8,128)(2,1)S(1)}, bf16[16,168,128]{2,1,0:T(8,128)(2,1)S(1)}, u32[]{:S(2)}, u32[]{:S(2)}) collective-permute-start(bf16[16,168,128]{2,1,0:T(8,128)(2,1)S(1)} %all-to-all-done.2.mine_ref), channel_id=1, source_target_pairs={{0,1},{1,0},{2,3},{3,2},{4,5},{5,4},{6,7},{7,6},{8,9},{9,8},{10,11... | collective-permute-start | bytes 2064392 | tf_op jit(solution)/shard_map/ppermute | solution.py:369

commit v4 on v3

--- a/solution.py
+++ b/solution.py
@@ -76,17 +76,20 @@
                 t, :, start : start + SPAN
             ]
     order = heads_first()
-    pieces = []
+    m = iota((1, 384), 1)
+    x = (m * 21846) >> 18
+    swap = (iota((384, 384), 0) == (m - x * AB) * SPAN + x).astype(BF16)
+    full = 0.0
     rest = [rows_ref[t] for t in range(TAB)]
     for _ in range(3):
         low = [r.astype(BF16) for r in rest]
         rest = [r - p.astype(F32) for r, p in zip(rest, low)]
-        pieces.append(jnp.concatenate([dot(order, p, 1, 0).astype(BF16) for p in low], axis=0))
+        full = full + dot(jnp.concatenate([dot(order, p, 1, 0).astype(BF16) for p in low], axis=0), swap, 1, 0)
     for c in range(WLON):
-        pick = toeplitz(c)
-        full = dot(pieces[0], pick, 1, 0) + (dot(pieces[1], pick, 1, 0) + dot(pieces[2], pick, 1, 0))
+        start = (WLON - 1 - c) * AB
+        part = full[:, start : start + POINTS]
         for th in range(TAB * HEADS):
-            bias_ref[th, c * AB : (c + 1) * AB, :] = full[th * 16 : th * 16 + AB, :]
+            bias_ref[th, c * AB : (c + 1) * AB, :] = part[th * 16 : th * 16 + AB, :]
     win_t_ref[...] = win_ref[...].T
     wout_t_ref[...] = wout_ref[...].T
     column = jnp.broadcast_to(gain_ref[...], (8, C)).T
@@ -105,20 +108,9 @@
             region_ref[v, w] = jnp.sum(own, axis=0, keepdims=True)
 
 
-def main_kernel(
-    ens_ref, x_ref, y_ref, lon_ref, lat_ref, cor_ref, region_ref, gain_ref, win_ref, win_t_ref, wout_ref,
-    wout_t_ref, bias_ref,
-    out_ref, ig_ref, lon_out, lat_out, keep_ref, send_ref,
-    ext, grads, outer, gain_acc, dbias, blocks, rows, flat_t, flat, chunks,
-):
-    for k, ref in enumerate((x_ref, y_ref)):
-        ext[k, :, 0:18, 0:24, :] = ref[...].astype(F32)
-        ext[k, :, 0:18, 24:32, :] = lon_ref[k].astype(F32)
-        ext[k, :, 18:21, 0:24, :] = lat_ref[k].astype(F32)
-        ext[k, :, 18:21, 24:32, :] = cor_ref[k].astype(F32)
-    grads[...] = jnp.zeros_like(grads)
-    outer[...] = jnp.zeros_like(outer)
-    gain_acc[...] = jnp.zeros_like(gain_acc)
+def windows(weights, sums, save):
+    region_ref, gain_ref, win_ref, win_t_ref, wout_ref, wout_t_ref, bias_ref = weights
+    grads, outer, gain_acc = sums
     gain = gain_ref[...]
     heads = [(iota((POINTS, C), 1) >> 5) == h for h in range(HEADS)]
     c_p, ab_p = tokens()
@@ -163,10 +155,7 @@
             mixed.append(dot(triple[2 * C + lo : 2 * C + hi], low, 1, 0))
             g_prob = all_g_prob[part_h]
             g_score = prob * (g_prob - jnp.sum(prob * g_prob, axis=0, keepdims=True))
-            if w == 0:
-                dbias[v * HEADS + h] = g_score
-            else:
-                dbias[v * HEADS + h] += g_score
+            save(v, w, h, g_score)
             g_low = g_score.astype(BF16)
             g_q.append(dot(triple[C + lo : C + hi], g_low, 1, 0) * FACTOR)
             lows.append(low)
@@ -205,20 +194,72 @@
         yield
         yield dot(pick, block, 1, 1), dot(pick, in_grad, 1, 1)
 
+    return window
+
+
+def interleaved(window, ext, chosen):
     def rows_of(k, v):
         return ext[k, :, 6 * v + 3 : 6 * v + 9].reshape(384, C).astype(BF16).T
 
-    def group(chosen):
-        results = [None]
-        todo = [window(v, w, rows_of(0, v), rows_of(1, v)) for v in chosen for w in range(2)]
-        while results[0] is None:
-            results = [next(g) for g in todo]
-        for i, v in enumerate(chosen):
-            for k in range(2):
-                total = results[2 * i][k] + results[2 * i + 1][k]
-                ext[k, :, 6 * v + 3 : 6 * v + 9] = total.reshape(2, 6, 32, C)
-
-    group(range(TAB))
+    results = [None]
+    todo = [window(v, w, rows_of(0, v), rows_of(1, v)) for v, w in chosen]
+    while results[0] is None:
+        results = [next(g) for g in todo]
+    return dict(zip(chosen, results))
+
+
+def inner_kernel(
+    x_ref, y_ref, region_ref, gain_ref, win_ref, win_t_ref, wout_ref, wout_t_ref, bias_ref,
+    rows_ref, grads, outer, gain_acc, dbias, ext,
+):
+    for k, ref in enumerate((x_ref, y_ref)):
+        ext[k, :, :, 0:24, :] = ref[:, 0:15].astype(F32)
+        ext[k, :, :, 24:32, :] = jnp.zeros((2, 15, 8, C), F32)
+    for ref in (grads, outer, gain_acc):
+        ref[...] = jnp.zeros_like(ref)
+
+    def save(v, w, h, g_score):
+        dbias[v * HEADS + h] = g_score
+
+    weights = (region_ref, gain_ref, win_ref, win_t_ref, wout_ref, wout_t_ref, bias_ref)
+    got = interleaved(windows(weights, (grads, outer, gain_acc), save), ext, [(0, 0), (1, 0)])
+    for v in range(2):
+        for k in range(2):
+            rows_ref[k, v] = got[v, 0][k]
+
+
+def main_kernel(
+    ens_ref, x_ref, y_ref, lon_ref, lat_ref, cor_ref, region_ref, gain_ref, win_ref, win_t_ref, wout_ref,
+    wout_t_ref, bias_ref, rows_in, grads_in, outer_in, gain_in, dbias_in,
+    out_ref, ig_ref, lon_out, lat_out, keep_ref, send_ref,
+    ext, grads, outer, gain_acc, dbias, blocks, rows, flat_t, flat, chunks,
+):
+    for k, ref in enumerate((x_ref, y_ref)):
+        ext[k, :, 0:18, 0:24, :] = ref[...].astype(F32)
+        ext[k, :, 0:18, 24:32, :] = lon_ref[k].astype(F32)
+        ext[k, :, 18:21, 0:24, :] = lat_ref[k].astype(F32)
+        ext[k, :, 18:21, 24:32, :] = cor_ref[k].astype(F32)
+    grads[:, : 3 * C] = grads_in[...]
+    outer[...] = outer_in[...]
+    gain_acc[...] = gain_in[...]
+
+    def save(v, w, h, g_score):
+        at = v * HEADS + h
+        if v < 2:
+            dbias[at] = dbias_in[at] + g_score
+        elif w == 0:
+            dbias[at] = g_score
+        else:
+            dbias[at] += g_score
+
+    weights = (region_ref, gain_ref, win_ref, win_t_ref, wout_ref, wout_t_ref, bias_ref)
+    got = interleaved(
+        windows(weights, (grads, outer, gain_acc), save), ext, [(0, 1), (1, 1), (2, 0), (2, 1)]
+    )
+    for v in range(TAB):
+        for k in range(2):
+            first = rows_in[k, v] if v < 2 else got[v, 0][k]
+            ext[k, :, 6 * v + 3 : 6 * v + 9] = (first + got[v, 1][k]).reshape(2, 6, 32, C)
     for k, ref in enumerate((out_ref, ig_ref)):
         ext[k, :, 0:3] = jnp.zeros((2, 3, 32, C), F32)
         ref[...] = ext[k, :, 0:18, 0:24, :].astype(BF16)
@@ -337,7 +378,7 @@
 WHOLE = pl.BlockSpec(memory_space=pltpu.VMEM)
 
 
-def call(kernel, outs, args, scratch=()):
+def call(kernel, outs, args, scratch=(), room=24):
     specs = [SMEM if a.dtype == I32 and a.ndim == 1 else WHOLE for a in args]
     shapes = tuple(pltpu.VMEM(*o) if len(o) == 2 else jax.ShapeDtypeStruct(*o[:2]) for o in outs)
     return pl.pallas_call(
@@ -346,7 +387,7 @@
         in_specs=specs,
         out_specs=tuple(WHOLE for _ in outs),
         scratch_shapes=[pltpu.VMEM(*x) for x in scratch],
-        compiler_params=pltpu.CompilerParams(vmem_limit_bytes=56 * 2**20),
+        compiler_params=pltpu.CompilerParams(vmem_limit_bytes=room * 2**20),
     )(*args)
 
 
@@ -396,17 +437,28 @@
             mask_ids.transpose(1, 0, 2),
         ),
         [((TAB, HEADS, ENTRIES), F32), ((TAB, 96, 384), F32), ((TAB, 16, 128), F32)],
-    )
+        56,
+    )
+
+
+SUMS = [
+    ((2, 2, 384, C), F32),
+    ((C, 3 * C), F32),
+    ((C, C), F32),
+    ((C, POINTS), F32),
+    ((2 * HEADS, POINTS, POINTS), F32),
+]
 
 
 def run_main(me, x, y, strips, regions, gain, project_in, win_t, project_out, wout_t, bias):
+    weights = (
+        near(regions), near(gain), project_in, near(win_t), project_out, near(wout_t), near(bias),
+    )
+    inner = call(inner_kernel, SUMS, (x, y, *weights), [((2, 2, 15, 32, C), F32)], 50)
     return call(
         main_kernel,
         [((2, 18, 24, C), BF16)] * 2 + STRIPS[:2] + [((16, CHUNK, 128), F32), ((16, CHUNK, 128), BF16)],
-        (
-            me, x, y, *map(near, strips), near(regions), near(gain), project_in, near(win_t), project_out,
-            near(wout_t), near(bias),
-        ),
+        (me, x, y, *map(near, strips), *weights, *map(near, inner)),
         [
             ((2, 2, 21, 32, C), F32),
             ((C, 4 * C), F32),
@@ -419,6 +471,7 @@
             ((32 * T_ROWS, 128), F32),
             ((2, 16, CHUNK, 128), F32),
         ],
+        46,
     )
 
 
@@ -426,7 +479,7 @@
     x, y = inputs[0], cotangent[0]
     lat = lax.axis_index("lat").astype(I32).reshape(1)
     me = lax.axis_index("ens").astype(I32).reshape(1)
-    strips = halo(*call(strips_kernel, STRIPS, (x, y)), -1)
+    strips = halo(*call(strips_kernel, STRIPS, (x, y), (), 56), -1)
     bias, win_t, wout_t, gain, regions = run_shadow(lat, bias_table, norm_gain, project_in, project_out, mask_ids)
     out, in_grad, lon_s, lat_s, keep, send = run_main(
         me, x, y, strips, regions, gain, project_in, win_t, project_out, wout_t, bias

time: 96.5 us -> 93.7 us (0.971)
  starting transfers between devices: 38.7 us -> 34.4 us
  waiting for transfers between devices: 29.9 us -> 31 us
    all_to_all x1, starting transfers between devices: 7.1 us -> 3.37 us  [local(): part = lax.all_to_all(part, 'lat', 0, 0, tiled=True)]
    ppermute x7, waiting for transfers between devices: 10.5 us -> 13.4 us  [passed(): return lax.ppermute(x, axes, pairs)]
    all_to_all x1, waiting for transfers between devices: 7.05 us -> 4.27 us  [local(): part = lax.all_to_all(part, 'lat', 0, 0, tiled=True)]
    pallas_call x8 -> x9, Pallas kernels: 26.7 us -> 27.2 us  [call(): pl.pallas_call(kernel, out_shape=shapes, in_specs=specs, out_specs=tuple(...]
  transfers between devices with their start and end apart: 10 -> 10, of which waited for: 6 -> 7; matrix products, arithmetic and copies ran while one was open for 0% -> 0% of each run, Pallas kernels for 8% -> 12%
where the time goes in v4:
time: 93.7 us; the launch traced here: 93.2 us
  starting transfers between devices  34.4 us (37%)
  waiting for transfers between devices  31 us (33%)
  Pallas kernels  27.2 us (29%)
    pallas_call x9, Pallas kernels, call(): pl.pallas_call(kernel, out_shape=shapes, in_specs=specs, out_specs=tuple(...  27.2 us
    ppermute x7, starting transfers between devices, passed(): return lax.ppermute(x, axes, pairs)  22.3 us
    ppermute x7, waiting for transfers between devices, passed(): return lax.ppermute(x, axes, pairs)  13.4 us
    all_to_all x1, waiting for transfers between devices, local(): part = lax.all_to_all(part, 'lon', 0, 0, tiled=True)  7.95 us
    all_to_all x1, waiting for transfers between devices, local(): mine = lax.all_to_all(part, 'lon', 0, 0, tiled=True)  5.37 us
    all_to_all x1, starting transfers between devices, local(): mine = lax.all_to_all(part, 'lon', 0, 0, tiled=True)  5.19 us
    all_to_all x1, waiting for transfers between devices, local(): part = lax.all_to_all(part, 'lat', 0, 0, tiled=True)  4.27 us
    all_to_all x1, starting transfers between devices, local(): part = lax.all_to_all(part, 'lon', 0, 0, tiled=True)  3.53 us
  transfers between devices with their start and end apart: 10, of which 7 were waited for; matrix products, arithmetic and copies ran while one was open for 0% of the time, Pallas kernels for 12%

profile of v4, /device:TPU:1, one launch (start us, length us, event | category | flops | bytes accessed | tf_op | source)
XLA Modules:
  0.0 93.2 jit_solution(2805524941738088859)
XLA Ops:
  0.6 1.2 %shard_map.118 = (bf16[2,2,18,8,192]{4,3,2,1,0:T(8,128)(2,1)S(1)}, bf16[2,2,3,24,192]{4,3,2,1,0:T(8,128)(2,1)S(1)}, bf16[2,2,3,8,192]{4,3,2,1,0:T(8,128)(2,1)S(1)}) custom-call(bf16[2,18,24,192]{3,2,1,0:T(8,128)(2,1)} %bitcast.11, bf16[2,18,24,192]{3,2,1,0:T(8,128)(2,1)} %bitcast.14), custom_call_target="tpu_custom_call" | custom-call | tf_op jit(solution)/shard_map/pallas_call | solution.py:384
  1.8 7.4 %collective-permute-start = (bf16[2,2,18,8,192]{4,3,2,1,0:T(8,128)(2,1)S(1)}, bf16[2,2,18,8,192]{4,3,2,1,0:T(8,128)(2,1)S(1)}, u32[]{:S(2)}, u32[]{:S(2)}) collective-permute-start(bf16[2,2,18,8,192]{4,3,2,1,0:T(8,128)(2,1)S(1)} %get-tuple-element.35), channel_id=1, source_target_pairs={{0,240},{16,0},{32,16},{48,32},{64,48},{80,64},{96,80},{112,96},{1... | collective-permute-start | bytes 663560 | tf_op jit(solution)/shard_map/ppermute | solution.py:410
  9.2 4.9 %collective-permute-start.1 = (bf16[2,2,3,24,192]{4,3,2,1,0:T(8,128)(2,1)S(1)}, bf16[2,2,3,24,192]{4,3,2,1,0:T(8,128)(2,1)S(1)}, u32[]{:S(2)}, u32[]{:S(2)}) collective-permute-start(bf16[2,2,3,24,192]{4,3,2,1,0:T(8,128)(2,1)S(1)} %get-tuple-element.36), channel_id=1, source_target_pairs={{0,14},{2,0},{4,2},{6,4},{8,6},{10,8},{12,10},{14,12},{1,15},{3,1}... | collective-permute-start | bytes 331784 | tf_op jit(solution)/shard_map/ppermute | solution.py:410
  14.8 4.2 %shard_map.119 = (f32[18,144,144]{2,1,0:T(8,128)S(1)}, bf16[576,192]{1,0:T(8,128)(2,1)S(1)}, bf16[192,192]{1,0:T(8,128)(2,1)S(1)}, f32[192,144]{1,0:T(8,128)S(1)}, f32[3,2,1,144]{3,2,1,0:T(1,128)S(1)}) custom-call(s32[1]{0:T(128)} %bitcast.3.lat_ref, f32[6,24,3312]{2,1,0:T(8,128)} %bitcast.17, f32[1,192]{1,0:T(1,128)} %bitcast.19, bf16[192,576]{1,0:T(8,128)(2,1)} %win_ref.5, ...), custom_call_target="tpu_custom_call" | custom-call | tf_op jit(solution)/shard_map/pallas_call | solution.py:384
  19.0 5.0 %shard_map.120 = (f32[2,2,384,192]{3,2,1,0:T(8,128)S(1)}, f32[192,576]{1,0:T(8,128)S(1)}, f32[192,192]{1,0:T(8,128)S(1)}, f32[192,144]{1,0:T(8,128)S(1)}, f32[12,144,144]{2,1,0:T(8,128)S(1)}) custom-call(bf16[2,18,24,192]{3,2,1,0:T(8,128)(2,1)} %bitcast.12, bf16[2,18,24,192]{3,2,1,0:T(8,128)(2,1)} %bitcast.15, ...), custom_call_target="tpu_custom_call" | custom-call | tf_op jit(solution)/shard_map/pallas_call | solution.py:384
  24.1 11.2 %shard_map.121 = (bf16[2,18,24,192]{3,2,1,0:T(8,128)(2,1)S(1)}, bf16[2,18,24,192]{3,2,1,0:T(8,128)(2,1)S(1)}, bf16[2,2,18,8,192]{4,3,2,1,0:T(8,128)(2,1)S(1)}, b...) custom-call(s32[1]{0:T(128)} %bitcast.ens_ref, ...), custom_call_target="tpu_custom_call" | custom-call | tf_op jit(solution)/shard_map/pallas_call | solution.py:384
  35.3 1.6 %collective-permute-start.4 = (bf16[16,64,128]{2,1,0:T(8,128)(2,1)S(1)}, bf16[16,64,128]{2,1,0:T(8,128)(2,1)S(1)}, u32[]{:S(2)}, u32[]{:S(2)}) collective-permute-start(bf16[16,64,128]{2,1,0:T(8,128)(2,1)S(1)} %get-tuple-element.52), channel_id=1, source_target_pairs={{0,1},{1,0},{2,3},{3,2},{4,5},{5,4},{6,7},{7,6},{8,9},{9,8},{10,11... | collective-permute-start | bytes 786440 | tf_op jit(solution)/shard_map/ppermute | solution.py:410
  36.9 1.2 %collective-permute-done.4.got_ref = bf16[16,64,128]{2,1,0:T(8,128)(2,1)S(1)} collective-permute-done((bf16[16,64,128]{2,1,0:T(8,128)(2,1)S(1)}, bf16[16,64,128]{2,1,0:T(8,128)(2,1)S(1)}, u32[]{:S(2)}, u32[]{:S(2)}) %collective-permute-start.4) | collective-permute-done | bytes 262176 | tf_op jit(solution)/shard_map/ppermute | solution.py:410
  38.0 0.8 shard_map.122
  38.8 3.5 %all-to-all-start = ((bf16[16,64,128]{2,1,0:T(8,128)(2,1)}), bf16[16,64,128]{2,1,0:T(8,128)(2,1)S(1)}, u32[]{:S(2)}, u32[]{:S(2)}) async-start(bf16[16,64,128]{2,1,0:T(8,128)(2,1)} %shard_map.122), calls=%async_computation | async-start | bytes 524288 | tf_op jit(solution)/shard_map/all_to_all | solution.py:489
  42.3 1.2 %collective-permute-start.3 = (bf16[2,2,18,8,192]{4,3,2,1,0:T(8,128)(2,1)S(1)}, bf16[2,2,18,8,192]{4,3,2,1,0:T(8,128)(2,1)S(1)}, u32[]{:S(2)}, u32[]{:S(2)}) collective-permute-start(bf16[2,2,18,8,192]{4,3,2,1,0:T(8,128)(2,1)S(1)} %get-tuple-element.50), channel_id=1, source_target_pairs={{0,16},{16,32},{32,48},{48,64},{64,80},{80,96},{96,112},{112,128},... | collective-permute-start | bytes 663560 | tf_op jit(solution)/shard_map/ppermute | solution.py:410
  43.6 7.9 %all-to-all-done.got_ref = bf16[16,64,128]{2,1,0:T(8,128)(2,1)S(1)} async-done(((bf16[16,64,128]{2,1,0:T(8,128)(2,1)}), bf16[16,64,128]{2,1,0:T(8,128)(2,1)S(1)}, u32[]{:S(2)}, u32[]{:S(2)}) %all-to-all-start) | async-done | bytes 262176 | tf_op jit(solution)/shard_map/all_to_all | solution.py:489
  52.2 3.4 %all-to-all-start.1 = ((bf16[8,64,128]{2,1,0:T(8,128)(2,1)}), bf16[8,64,128]{2,1,0:T(8,128)(2,1)S(1)}, u32[]{:S(2)}, u32[]{:S(2)}) async-start(bf16[8,64,128]{2,1,0:T(8,128)(2,1)} %shard_map.123), calls=%async_computation.1 | async-start | bytes 262144 | tf_op jit(solution)/shard_map/all_to_all | solution.py:492
  55.6 2.8 %collective-permute-done.3.lon_ref = bf16[2,2,18,8,192]{4,3,2,1,0:T(8,128)(2,1)S(1)} collective-permute-done((bf16[2,2,18,8,192]{4,3,2,1,0:T(8,128)(2,1)S(1)}, bf16[2,2,18,8,192]{4,3,2,1,0:T(8,128)(2,1)S(1)}, u32[]{:S(2)}, u32[]{:S(2)}) %collective-permute-start.3) | collective-permute-done | bytes 221216 | tf_op jit(solution)/shard_map/ppermute | solution.py:410
  58.4 4.3 %all-to-all-done.1.got_ref = bf16[8,64,128]{2,1,0:T(8,128)(2,1)S(1)} async-done(((bf16[8,64,128]{2,1,0:T(8,128)(2,1)}), bf16[8,64,128]{2,1,0:T(8,128)(2,1)S(1)}, u32[]{:S(2)}, u32[]{:S(2)}) %all-to-all-start.1) | async-done | bytes 131104 | tf_op jit(solution)/shard_map/all_to_all | solution.py:492
  62.7 0.9 %shard_map.124 = (bf16[16,168,128]{2,1,0:T(8,128)(2,1)}, bf16[2,2,3,24,192]{4,3,2,1,0:T(8,128)(2,1)S(1)}) custom-call(bf16[8,64,128]{2,1,0:T(8,128)(2,1)S(1)} %all-to-all-done.1.got_ref, bf16[2,2,18,8,192]{4,3,2,1,0:T(8,128)(2,1)S(1)} %collective-permute-done.3.lon_ref, bf16[2,2,3,24,192]{4,3,2,1,0:T(8,128)(2,1)S(1)} %get-tuple-element.53.lat_ref), custom_call_target="tpu_custom_call" | custom-call | tf_op jit(solution)/shard_map/pallas_call | solution.py:384
  63.6 5.2 %all-to-all-start.2 = ((bf16[16,168,128]{2,1,0:T(8,128)(2,1)}), bf16[16,168,128]{2,1,0:T(8,128)(2,1)S(1)}, u32[]{:S(2)}, u32[]{:S(2)}) async-start(bf16[16,168,128]{2,1,0:T(8,128)(2,1)} %get-tuple-element.54), calls=%async_computation.2 | async-start | bytes 1376256 | tf_op jit(solution)/shard_map/all_to_all | solution.py:499
  68.8 1.2 %collective-permute-start.5 = (bf16[2,2,3,24,192]{4,3,2,1,0:T(8,128)(2,1)S(1)}, bf16[2,2,3,24,192]{4,3,2,1,0:T(8,128)(2,1)S(1)}, u32[]{:S(2)}, u32[]{:S(2)}) collective-permute-start(bf16[2,2,3,24,192]{4,3,2,1,0:T(8,128)(2,1)S(1)} %get-tuple-element.55), channel_id=1, source_target_pairs={{0,2},{2,4},{4,6},{6,8},{8,10},{10,12},{12,14},{14,0},{1,3},{3,5},... | collective-permute-start | bytes 331784 | tf_op jit(solution)/shard_map/ppermute | solution.py:410
  70.0 8.7 %collective-permute-done.5.lat_ref = bf16[2,2,3,24,192]{4,3,2,1,0:T(8,128)(2,1)S(1)} collective-permute-done((bf16[2,2,3,24,192]{4,3,2,1,0:T(8,128)(2,1)S(1)}, bf16[2,2,3,24,192]{4,3,2,1,0:T(8,128)(2,1)S(1)}, u32[]{:S(2)}, u32[]{:S(2)}) %collective-permute-start.5) | collective-permute-done | bytes 110624 | tf_op jit(solution)/shard_map/ppermute | solution.py:410
  78.7 5.4 %all-to-all-done.2.mine_ref = bf16[16,168,128]{2,1,0:T(8,128)(2,1)S(1)} async-done(((bf16[16,168,128]{2,1,0:T(8,128)(2,1)}), bf16[16,168,128]{2,1,0:T(8,128)(2,1)S(1)}, u32[]{:S(2)}, u32[]{:S(2)}) %all-to-all-start.2) | async-done | bytes 688160 | tf_op jit(solution)/shard_map/all_to_all | solution.py:499
  84.0 5.3 %collective-permute-start.6 = (bf16[16,168,128]{2,1,0:T(8,128)(2,1)S(1)}, bf16[16,168,128]{2,1,0:T(8,128)(2,1)S(1)}, u32[]{:S(2)}, u32[]{:S(2)}) collective-permute-start(bf16[16,168,128]{2,1,0:T(8,128)(2,1)S(1)} %all-to-all-done.2.mine_ref), channel_id=1, source_target_pairs={{0,1},{1,0},{2,3},{3,2},{4,5},{5,4},{6,7},{7,6},{8,9},{9,8},{10,11... | collective-permute-start | bytes 2064392 | tf_op jit(solution)/shard_map/ppermute | solution.py:410
  89.3 1.0 %shard_map.125 = (bf16[2,18,24,192]{3,2,1,0:T(8,128)(2,1)}, bf16[2,18,24,192]{3,2,1,0:T(8,128)(2,1)}) custom-call(bf16[2,18,24,192]{3,2,1,0:T(8,128)(2,1)S(1)} %get-tuple-element.48.out_ref, bf16[2,18,24,192]{3,2,1,0:T(8,128)(2,1)S(1)} %get-tuple-element.49.grad_ref, bf16[2,2,18,8,192]{4,3,2,1,0:T(8,128)(2,1)S(1)} %collective-permute-done.3.lon_ref, ...), custom_call_target="tpu_custom_call" | custom-call | tf_op jit(solution)/shard_map/pallas_call | solution.py:384
  90.3 0.8 collective-permute-done.6.other_ref
  91.1 2.2 %shard_map.126 = (f32[192,576]{1,0:T(8,128)}, f32[192,192]{1,0:T(8,128)}, f32[1,192]{1,0:T(1,128)}, f32[6,24,3312]{2,1,0:T(8,128)}) custom-call(s32[1]{0:T(128)} %bitcast.ens_ref, bf16[16,168,128]{2,1,0:T(8,128)(2,1)S(1)} %all-to-all-done.2.mine_ref, bf16[16,168,128]{2,1,0:T(8,128)(2,1)S(1)} %collective-permute-done.6.other_ref), custom_call_target="tpu_custom_call" | custom-call | tf_op jit(solution)/shard_map/pallas_call | solution.py:384
  (5 shorter events, 1.4 us)
Async XLA Ops:
  1.8 22.2 %collective-permute-start = (bf16[2,2,18,8,192]{4,3,2,1,0:T(8,128)(2,1)S(1)}, bf16[2,2,18,8,192]{4,3,2,1,0:T(8,128)(2,1)S(1)}, u32[]{:S(2)}, u32[]{:S(2)}) collective-permute-start(bf16[2,2,18,8,192]{4,3,2,1,0:T(8,128)(2,1)S(1)} %get-tuple-element.35), channel_id=1, source_target_pairs={{0,240},{16,0},{32,16},{48,32},{64,48},{80,64},{96,80},{112,96},{1... | collective-permute-start | bytes 663560 | tf_op jit(solution)/shard_map/ppermute | solution.py:410
  9.2 14.8 %collective-permute-start.1 = (bf16[2,2,3,24,192]{4,3,2,1,0:T(8,128)(2,1)S(1)}, bf16[2,2,3,24,192]{4,3,2,1,0:T(8,128)(2,1)S(1)}, u32[]{:S(2)}, u32[]{:S(2)}) collective-permute-start(bf16[2,2,3,24,192]{4,3,2,1,0:T(8,128)(2,1)S(1)} %get-tuple-element.36), channel_id=1, source_target_pairs={{0,14},{2,0},{4,2},{6,4},{8,6},{10,8},{12,10},{14,12},{1,15},{3,1}... | collective-permute-start | bytes 331784 | tf_op jit(solution)/shard_map/ppermute | solution.py:410
  14.1 9.9 %collective-permute-start.2 = (bf16[2,2,3,8,192]{4,3,2,1,0:T(8,128)(2,1)S(1)}, bf16[2,2,3,8,192]{4,3,2,1,0:T(8,128)(2,1)S(1)}, u32[]{:S(2)}, u32[]{:S(2)}) collective-permute-start(bf16[2,2,3,8,192]{4,3,2,1,0:T(8,128)(2,1)S(1)} %get-tuple-element.37), channel_id=1, source_target_pairs={{0,254},{2,240},{4,242},{6,244},{8,246},{10,248},{12,250},{14,252}... | collective-permute-start | bytes 110600 | tf_op jit(solution)/shard_map/ppermute | solution.py:410
  35.3 2.8 %collective-permute-start.4 = (bf16[16,64,128]{2,1,0:T(8,128)(2,1)S(1)}, bf16[16,64,128]{2,1,0:T(8,128)(2,1)S(1)}, u32[]{:S(2)}, u32[]{:S(2)}) collective-permute-start(bf16[16,64,128]{2,1,0:T(8,128)(2,1)S(1)} %get-tuple-element.52), channel_id=1, source_target_pairs={{0,1},{1,0},{2,3},{3,2},{4,5},{5,4},{6,7},{7,6},{8,9},{9,8},{10,11... | collective-permute-start | bytes 786440 | tf_op jit(solution)/shard_map/ppermute | solution.py:410
  38.8 12.7 %all-to-all-start = ((bf16[16,64,128]{2,1,0:T(8,128)(2,1)}), bf16[16,64,128]{2,1,0:T(8,128)(2,1)S(1)}, u32[]{:S(2)}, u32[]{:S(2)}) async-start(bf16[16,64,128]{2,1,0:T(8,128)(2,1)} %shard_map.122), calls=%async_computation | async-start | bytes 524288 | tf_op jit(solution)/shard_map/all_to_all | solution.py:489
  42.3 16.0 %collective-permute-start.3 = (bf16[2,2,18,8,192]{4,3,2,1,0:T(8,128)(2,1)S(1)}, bf16[2,2,18,8,192]{4,3,2,1,0:T(8,128)(2,1)S(1)}, u32[]{:S(2)}, u32[]{:S(2)}) collective-permute-start(bf16[2,2,18,8,192]{4,3,2,1,0:T(8,128)(2,1)S(1)} %get-tuple-element.50), channel_id=1, source_target_pairs={{0,16},{16,32},{32,48},{48,64},{64,80},{80,96},{96,112},{112,128},... | collective-permute-start | bytes 663560 | tf_op jit(solution)/shard_map/ppermute | solution.py:410
  52.2 10.4 %all-to-all-start.1 = ((bf16[8,64,128]{2,1,0:T(8,128)(2,1)}), bf16[8,64,128]{2,1,0:T(8,128)(2,1)S(1)}, u32[]{:S(2)}, u32[]{:S(2)}) async-start(bf16[8,64,128]{2,1,0:T(8,128)(2,1)} %shard_map.123), calls=%async_computation.1 | async-start | bytes 262144 | tf_op jit(solution)/shard_map/all_to_all | solution.py:492
  63.6 20.4 %all-to-all-start.2 = ((bf16[16,168,128]{2,1,0:T(8,128)(2,1)}), bf16[16,168,128]{2,1,0:T(8,128)(2,1)S(1)}, u32[]{:S(2)}, u32[]{:S(2)}) async-start(bf16[16,168,128]{2,1,0:T(8,128)(2,1)} %get-tuple-element.54), calls=%async_computation.2 | async-start | bytes 1376256 | tf_op jit(solution)/shard_map/all_to_all | solution.py:499
  68.8 9.9 %collective-permute-start.5 = (bf16[2,2,3,24,192]{4,3,2,1,0:T(8,128)(2,1)S(1)}, bf16[2,2,3,24,192]{4,3,2,1,0:T(8,128)(2,1)S(1)}, u32[]{:S(2)}, u32[]{:S(2)}) collective-permute-start(bf16[2,2,3,24,192]{4,3,2,1,0:T(8,128)(2,1)S(1)} %get-tuple-element.55), channel_id=1, source_target_pairs={{0,2},{2,4},{4,6},{6,8},{8,10},{10,12},{12,14},{14,0},{1,3},{3,5},... | collective-permute-start | bytes 331784 | tf_op jit(solution)/shard_map/ppermute | solution.py:410
  84.0 7.0 %collective-permute-start.6 = (bf16[16,168,128]{2,1,0:T(8,128)(2,1)S(1)}, bf16[16,168,128]{2,1,0:T(8,128)(2,1)S(1)}, u32[]{:S(2)}, u32[]{:S(2)}) collective-permute-start(bf16[16,168,128]{2,1,0:T(8,128)(2,1)S(1)} %all-to-all-done.2.mine_ref), channel_id=1, source_target_pairs={{0,1},{1,0},{2,3},{3,2},{4,5},{5,4},{6,7},{7,6},{8,9},{9,8},{10,11... | collective-permute-start | bytes 2064392 | tf_op jit(solution)/shard_map/ppermute | solution.py:410

commit v5 on v4

--- a/solution.py
+++ b/solution.py
@@ -54,17 +54,18 @@
     return ((iota((96, 96), 1) == (n & 15) * 8 + (n >> 4)) & ((n & 15) < AB)).astype(BF16)
 
 
-def strips_kernel(x_ref, y_ref, lon_ref, lat_ref, cor_ref):
-    for k, ref in enumerate((x_ref, y_ref)):
-        lon_ref[k] = ref[:, :, 0:8, :]
-        lat_ref[k] = ref[:, 0:3, :, :]
-        cor_ref[k] = ref[:, 0:3, 0:8, :]
-
-
-def shadow_kernel(
-    lat_ref, table_ref, gain_ref, win_ref, wout_ref, mask_ref,
-    bias_ref, win_t_ref, wout_t_ref, gain_out, region_ref, own_ref, rows_ref, ids_ref,
+def prepare_kernel(
+    lat_ref, x_ref, y_ref, table_ref, gain_ref, win_ref, wout_ref, mask_ref,
+    lon_out, lat_out, cor_out, x_out, y_out, bias_ref, win_out, win_t_ref, wout_out, wout_t_ref, gain_out, region_ref,
+    own_ref, rows_ref, ids_ref,
 ):
+    for k, (ref, copy) in enumerate(((x_ref, x_out), (y_ref, y_out))):
+        lon_out[k] = ref[:, :, 0:8, :]
+        lat_out[k] = ref[:, 0:3, :, :]
+        cor_out[k] = ref[:, 0:3, 0:8, :]
+        copy[...] = ref[...]
+    win_out[...] = win_ref[...]
+    wout_out[...] = wout_ref[...]
     first = lat_ref[0] * TAB
     for t in range(TAB):
         for h in range(HEADS):
@@ -422,22 +423,27 @@
 STRIPS = [((2, 2, 18, 8, C), BF16), ((2, 2, 3, 24, C), BF16), ((2, 2, 3, 8, C), BF16)]
 
 
-def run_shadow(lat, bias_table, norm_gain, project_in, project_out, mask_ids):
+def run_prepare(lat, x, y, bias_table, norm_gain, project_in, project_out, mask_ids):
     return call(
-        shadow_kernel,
+        prepare_kernel,
         [
+            *STRIPS,
+            ((2, 18, 24, C), BF16),
+            ((2, 18, 24, C), BF16),
             ((TAB * HEADS, POINTS, POINTS), F32),
+            ((C, 3 * C), BF16),
             ((3 * C, C), BF16),
+            ((C, C), BF16),
             ((C, C), BF16),
             ((C, POINTS), F32),
             ((TAB, 2, 1, POINTS), F32),
         ],
         (
-            lat, bias_table.transpose(1, 0, 2), norm_gain.reshape(1, C), project_in, project_out,
+            lat, x, y, bias_table.transpose(1, 0, 2), norm_gain.reshape(1, C), project_in, project_out,
             mask_ids.transpose(1, 0, 2),
         ),
         [((TAB, HEADS, ENTRIES), F32), ((TAB, 96, 384), F32), ((TAB, 16, 128), F32)],
-        56,
+        50,
     )
 
 
@@ -450,10 +456,8 @@
 ]
 
 
-def run_main(me, x, y, strips, regions, gain, project_in, win_t, project_out, wout_t, bias):
-    weights = (
-        near(regions), near(gain), project_in, near(win_t), project_out, near(wout_t), near(bias),
-    )
+def run_main(me, x, y, strips, weights):
+    x, y, *weights = map(near, (x, y, *weights))
     inner = call(inner_kernel, SUMS, (x, y, *weights), [((2, 2, 15, 32, C), F32)], 50)
     return call(
         main_kernel,
@@ -479,10 +483,12 @@
     x, y = inputs[0], cotangent[0]
     lat = lax.axis_index("lat").astype(I32).reshape(1)
     me = lax.axis_index("ens").astype(I32).reshape(1)
-    strips = halo(*call(strips_kernel, STRIPS, (x, y), (), 56), -1)
-    bias, win_t, wout_t, gain, regions = run_shadow(lat, bias_table, norm_gain, project_in, project_out, mask_ids)
+    lon_s, lat_s, cor_s, x, y, bias, win, win_t, wout, wout_t, gain, regions = run_prepare(
+        lat, x, y, bias_table, norm_gain, project_in, project_out, mask_ids
+    )
+    strips = halo(lon_s, lat_s, cor_s, -1)
     out, in_grad, lon_s, lat_s, keep, send = run_main(
-        me, x, y, strips, regions, gain, project_in, win_t, project_out, wout_t, bias
+        me, x, y, strips, (regions, gain, win, win_t, wout, wout_t, bias)
     )
     got = passed(send, "ens", (2,), (1,))
     (part,) = call(over_ens_kernel, [((16, CHUNK, 128), BF16)], (near(keep), near(got)))

time: 93.7 us -> 104 us (1.11)
  local copies, waits for them, and re-layouts: 0 us -> 10.9 us
  Pallas kernels: 27.2 us -> 25.6 us
  starting transfers between devices: 34.4 us -> 35.7 us
    unnamed x0 -> x36, local copies, waits for them, and re-layouts: none -> 10.9 us
    pallas_call x9 -> x8, Pallas kernels: 27.2 us -> 25.6 us  [call(): pl.pallas_call(kernel, out_shape=shapes, in_specs=specs, out_specs=tuple(...]
    ppermute x7, waiting for transfers between devices: 13.4 us -> 12.2 us  [passed(): return lax.ppermute(x, axes, pairs)]
    all_to_all x1, waiting for transfers between devices: 4.27 us -> 5.39 us  [local(): part = lax.all_to_all(part, 'lat', 0, 0, tiled=True)]
    all_to_all x1, starting transfers between devices: 3.37 us -> 4.47 us  [local(): part = lax.all_to_all(part, 'lat', 0, 0, tiled=True)]
  transfers between devices with their start and end apart: 10 -> 10, of which waited for: 7 -> 7; matrix products, arithmetic and copies ran while one was open for 0% -> 0% of each run, Pallas kernels for 12% -> 5%
where the time goes in v5:
time: 104 us; the launch traced here: 103 us
  starting transfers between devices  35.7 us (34%)
  waiting for transfers between devices  30.4 us (29%)
  Pallas kernels  25.6 us (25%)
  local copies, waits for them, and re-layouts  10.9 us (10%)
    pallas_call x8, Pallas kernels, call(): pl.pallas_call(kernel, out_shape=shapes, in_specs=specs, out_specs=tuple(...  25.6 us
    ppermute x7, starting transfers between devices, passed(): return lax.ppermute(x, axes, pairs)  22.8 us
    ppermute x7, waiting for transfers between devices, passed(): return lax.ppermute(x, axes, pairs)  12.2 us
    unnamed x36, local copies, waits for them, and re-layouts  10.9 us
    all_to_all x1, waiting for transfers between devices, local(): part = lax.all_to_all(part, 'lon', 0, 0, tiled=True)  7.95 us
    all_to_all x1, waiting for transfers between devices, local(): part = lax.all_to_all(part, 'lat', 0, 0, tiled=True)  5.39 us
    all_to_all x1, waiting for transfers between devices, local(): mine = lax.all_to_all(part, 'lon', 0, 0, tiled=True)  4.89 us
    all_to_all x1, starting transfers between devices, local(): mine = lax.all_to_all(part, 'lon', 0, 0, tiled=True)  4.86 us
  transfers between devices with their start and end apart: 10, of which 7 were waited for; matrix products, arithmetic and copies ran while one was open for 0% of the time, Pallas kernels for 5%

profile of v5, /device:TPU:1, one launch (start us, length us, event | category | flops | bytes accessed | tf_op | source)
XLA Modules:
  0.0 103.3 jit_solution(2881391153198387145)
XLA Ops:
  0.6 5.3 %shard_map.118 = (bf16[2,2,18,8,192]{4,3,2,1,0:T(8,128)(2,1)}, bf16[2,2,3,24,192]{4,3,2,1,0:T(8,128)(2,1)}, bf16[2,2,3,8,192]{4,3,2,1,0:T(8,128)(2,1)}, bf16[2,1...) custom-call(s32[1]{0:T(128)} %bitcast.1.lat_ref, ...), custom_call_target="tpu_custom_call" | custom-call | tf_op jit(solution)/shard_map/pallas_call | solution.py:385
  9.3 7.3 %collective-permute-start = (bf16[2,2,18,8,192]{4,3,2,1,0:T(8,128)(2,1)}, bf16[2,2,18,8,192]{4,3,2,1,0:T(8,128)(2,1)}, u32[]{:S(2)}, u32[]{:S(2)}) collective-permute-start(bf16[2,2,18,8,192]{4,3,2,1,0:T(8,128)(2,1)} %get-tuple-element.41), channel_id=1, source_target_pairs={{0,240},{16,0},{32,16},{48,32},{64,48},{80,64},{96,80},{112,96},{1... | collective-permute-start | bytes 663560 | tf_op jit(solution)/shard_map/ppermute | solution.py:411
  16.7 4.9 %collective-permute-start.1 = (bf16[2,2,3,24,192]{4,3,2,1,0:T(8,128)(2,1)}, bf16[2,2,3,24,192]{4,3,2,1,0:T(8,128)(2,1)}, u32[]{:S(2)}, u32[]{:S(2)}) collective-permute-start(bf16[2,2,3,24,192]{4,3,2,1,0:T(8,128)(2,1)} %get-tuple-element.42), channel_id=1, source_target_pairs={{0,14},{2,0},{4,2},{6,4},{8,6},{10,8},{12,10},{14,12},{1,15},{3,1}... | collective-permute-start | bytes 331784 | tf_op jit(solution)/shard_map/ppermute | solution.py:411
  22.3 1.0 copy-done.1
  23.2 0.9 copy-done.3
  24.2 0.9 copy-done.6
  26.9 3.8 %shard_map.119 = (f32[2,2,384,192]{3,2,1,0:T(8,128)S(1)}, f32[192,576]{1,0:T(8,128)S(1)}, f32[192,192]{1,0:T(8,128)S(1)}, f32[192,144]{1,0:T(8,128)S(1)}, f32[12,144,144]{2,1,0:T(8,128)S(1)}) custom-call(bf16[2,18,24,192]{3,2,1,0:T(8,128)(2,1)S(1)} %get-tuple-element.39.x_ref, bf16[2,18,24,192]{3,2,1,0:T(8,128)(2,1)S(1)} %get-tuple-element.40.y_ref, ...), custom_call_target="tpu_custom_call" | custom-call | tf_op jit(solution)/shard_map/pallas_call | solution.py:385
  30.7 10.9 %shard_map.120 = (bf16[2,18,24,192]{3,2,1,0:T(8,128)(2,1)S(1)}, bf16[2,18,24,192]{3,2,1,0:T(8,128)(2,1)S(1)}, bf16[2,2,18,8,192]{4,3,2,1,0:T(8,128)(2,1)S(1)}, b...) custom-call(s32[1]{0:T(128)} %bitcast.ens_ref, ...), custom_call_target="tpu_custom_call" | custom-call | tf_op jit(solution)/shard_map/pallas_call | solution.py:385
  44.5 1.5 %collective-permute-start.4 = (bf16[16,64,128]{2,1,0:T(8,128)(2,1)S(1)}, bf16[16,64,128]{2,1,0:T(8,128)(2,1)S(1)}, u32[]{:S(2)}, u32[]{:S(2)}) collective-permute-start(bf16[16,64,128]{2,1,0:T(8,128)(2,1)S(1)} %get-tuple-element.60), channel_id=1, source_target_pairs={{0,1},{1,0},{2,3},{3,2},{4,5},{5,4},{6,7},{7,6},{8,9},{9,8},{10,11... | collective-permute-start | bytes 786440 | tf_op jit(solution)/shard_map/ppermute | solution.py:411
  46.0 1.2 %collective-permute-done.4.got_ref = bf16[16,64,128]{2,1,0:T(8,128)(2,1)S(1)} collective-permute-done((bf16[16,64,128]{2,1,0:T(8,128)(2,1)S(1)}, bf16[16,64,128]{2,1,0:T(8,128)(2,1)S(1)}, u32[]{:S(2)}, u32[]{:S(2)}) %collective-permute-start.4) | collective-permute-done | bytes 262176 | tf_op jit(solution)/shard_map/ppermute | solution.py:411
  48.0 3.5 %all-to-all-start = ((bf16[16,64,128]{2,1,0:T(8,128)(2,1)}), bf16[16,64,128]{2,1,0:T(8,128)(2,1)S(1)}, u32[]{:S(2)}, u32[]{:S(2)}) async-start(bf16[16,64,128]{2,1,0:T(8,128)(2,1)} %shard_map.121), calls=%async_computation | async-start | bytes 524288 | tf_op jit(solution)/shard_map/all_to_all | solution.py:495
  51.5 1.2 %collective-permute-start.3 = (bf16[2,2,18,8,192]{4,3,2,1,0:T(8,128)(2,1)}, bf16[2,2,18,8,192]{4,3,2,1,0:T(8,128)(2,1)S(1)}, u32[]{:S(2)}, u32[]{:S(2)}) collective-permute-start(bf16[2,2,18,8,192]{4,3,2,1,0:T(8,128)(2,1)} %copy-done.17), channel_id=1, source_target_pairs={{0,16},{16,32},{32,48},{48,64},{64,80},{80,96},{96,112},{112,128},... | collective-permute-start | bytes 663560 | tf_op jit(solution)/shard_map/ppermute | solution.py:411
  52.7 7.9 %all-to-all-done.got_ref = bf16[16,64,128]{2,1,0:T(8,128)(2,1)S(1)} async-done(((bf16[16,64,128]{2,1,0:T(8,128)(2,1)}), bf16[16,64,128]{2,1,0:T(8,128)(2,1)S(1)}, u32[]{:S(2)}, u32[]{:S(2)}) %all-to-all-start) | async-done | bytes 262176 | tf_op jit(solution)/shard_map/all_to_all | solution.py:495
  61.4 4.5 %all-to-all-start.1 = ((bf16[8,64,128]{2,1,0:T(8,128)(2,1)}), bf16[8,64,128]{2,1,0:T(8,128)(2,1)S(1)}, u32[]{:S(2)}, u32[]{:S(2)}) async-start(bf16[8,64,128]{2,1,0:T(8,128)(2,1)} %shard_map.122), calls=%async_computation.1 | async-start | bytes 262144 | tf_op jit(solution)/shard_map/all_to_all | solution.py:498
  65.9 1.7 %collective-permute-done.3.lon_ref = bf16[2,2,18,8,192]{4,3,2,1,0:T(8,128)(2,1)S(1)} collective-permute-done((bf16[2,2,18,8,192]{4,3,2,1,0:T(8,128)(2,1)}, bf16[2,2,18,8,192]{4,3,2,1,0:T(8,128)(2,1)S(1)}, u32[]{:S(2)}, u32[]{:S(2)}) %collective-permute-start.3) | collective-permute-done | bytes 221216 | tf_op jit(solution)/shard_map/ppermute | solution.py:411
  67.5 5.4 %all-to-all-done.1.got_ref = bf16[8,64,128]{2,1,0:T(8,128)(2,1)S(1)} async-done(((bf16[8,64,128]{2,1,0:T(8,128)(2,1)}), bf16[8,64,128]{2,1,0:T(8,128)(2,1)S(1)}, u32[]{:S(2)}, u32[]{:S(2)}) %all-to-all-start.1) | async-done | bytes 131104 | tf_op jit(solution)/shard_map/all_to_all | solution.py:498
  72.9 0.9 shard_map.123
  73.9 4.9 %all-to-all-start.2 = ((bf16[16,168,128]{2,1,0:T(8,128)(2,1)}), bf16[16,168,128]{2,1,0:T(8,128)(2,1)S(1)}, u32[]{:S(2)}, u32[]{:S(2)}) async-start(bf16[16,168,128]{2,1,0:T(8,128)(2,1)} %get-tuple-element.62), calls=%async_computation.2 | async-start | bytes 1376256 | tf_op jit(solution)/shard_map/all_to_all | solution.py:505
  78.7 1.4 %collective-permute-start.5 = (bf16[2,2,3,24,192]{4,3,2,1,0:T(8,128)(2,1)S(1)}, bf16[2,2,3,24,192]{4,3,2,1,0:T(8,128)(2,1)S(1)}, u32[]{:S(2)}, u32[]{:S(2)}) collective-permute-start(bf16[2,2,3,24,192]{4,3,2,1,0:T(8,128)(2,1)S(1)} %get-tuple-element.63), channel_id=1, source_target_pairs={{0,2},{2,4},{4,6},{6,8},{8,10},{10,12},{12,14},{14,0},{1,3},{3,5},... | collective-permute-start | bytes 331784 | tf_op jit(solution)/shard_map/ppermute | solution.py:411
  80.2 8.6 %collective-permute-done.5.lat_ref = bf16[2,2,3,24,192]{4,3,2,1,0:T(8,128)(2,1)S(1)} collective-permute-done((bf16[2,2,3,24,192]{4,3,2,1,0:T(8,128)(2,1)S(1)}, bf16[2,2,3,24,192]{4,3,2,1,0:T(8,128)(2,1)S(1)}, u32[]{:S(2)}, u32[]{:S(2)}) %collective-permute-start.5) | collective-permute-done | bytes 110624 | tf_op jit(solution)/shard_map/ppermute | solution.py:411
  88.7 4.9 %all-to-all-done.2.mine_ref = bf16[16,168,128]{2,1,0:T(8,128)(2,1)S(1)} async-done(((bf16[16,168,128]{2,1,0:T(8,128)(2,1)}), bf16[16,168,128]{2,1,0:T(8,128)(2,1)S(1)}, u32[]{:S(2)}, u32[]{:S(2)}) %all-to-all-start.2) | async-done | bytes 688160 | tf_op jit(solution)/shard_map/all_to_all | solution.py:505
  93.6 5.7 %collective-permute-start.6 = (bf16[16,168,128]{2,1,0:T(8,128)(2,1)S(1)}, bf16[16,168,128]{2,1,0:T(8,128)(2,1)S(1)}, u32[]{:S(2)}, u32[]{:S(2)}) collective-permute-start(bf16[16,168,128]{2,1,0:T(8,128)(2,1)S(1)} %all-to-all-done.2.mine_ref), channel_id=1, source_target_pairs={{0,1},{1,0},{2,3},{3,2},{4,5},{5,4},{6,7},{7,6},{8,9},{9,8},{10,11... | collective-permute-start | bytes 2064392 | tf_op jit(solution)/shard_map/ppermute | solution.py:411
  99.3 1.0 shard_map.124
  101.1 2.2 %shard_map.125 = (f32[192,576]{1,0:T(8,128)}, f32[192,192]{1,0:T(8,128)}, f32[1,192]{1,0:T(1,128)}, f32[6,24,3312]{2,1,0:T(8,128)}) custom-call(s32[1]{0:T(128)} %bitcast.ens_ref, bf16[16,168,128]{2,1,0:T(8,128)(2,1)S(1)} %all-to-all-done.2.mine_ref, bf16[16,168,128]{2,1,0:T(8,128)(2,1)S(1)} %collective-permute-done.6.other_ref), custom_call_target="tpu_custom_call" | custom-call | tf_op jit(solution)/shard_map/pallas_call | solution.py:385
  (40 shorter events, 11.0 us)
Async XLA Ops:
  6.0 0.7 copy-start
  6.7 0.7 copy-start.2
  9.3 21.3 %collective-permute-start = (bf16[2,2,18,8,192]{4,3,2,1,0:T(8,128)(2,1)}, bf16[2,2,18,8,192]{4,3,2,1,0:T(8,128)(2,1)}, u32[]{:S(2)}, u32[]{:S(2)}) collective-permute-start(bf16[2,2,18,8,192]{4,3,2,1,0:T(8,128)(2,1)} %get-tuple-element.41), channel_id=1, source_target_pairs={{0,240},{16,0},{32,16},{48,32},{64,48},{80,64},{96,80},{112,96},{1... | collective-permute-start | bytes 663560 | tf_op jit(solution)/shard_map/ppermute | solution.py:411
  16.7 14.0 %collective-permute-start.1 = (bf16[2,2,3,24,192]{4,3,2,1,0:T(8,128)(2,1)}, bf16[2,2,3,24,192]{4,3,2,1,0:T(8,128)(2,1)}, u32[]{:S(2)}, u32[]{:S(2)}) collective-permute-start(bf16[2,2,3,24,192]{4,3,2,1,0:T(8,128)(2,1)} %get-tuple-element.42), channel_id=1, source_target_pairs={{0,14},{2,0},{4,2},{6,4},{8,6},{10,8},{12,10},{14,12},{1,15},{3,1}... | collective-permute-start | bytes 331784 | tf_op jit(solution)/shard_map/ppermute | solution.py:411
  21.6 9.1 %collective-permute-start.2 = (bf16[2,2,3,8,192]{4,3,2,1,0:T(8,128)(2,1)}, bf16[2,2,3,8,192]{4,3,2,1,0:T(8,128)(2,1)}, u32[]{:S(2)}, u32[]{:S(2)}) collective-permute-start(bf16[2,2,3,8,192]{4,3,2,1,0:T(8,128)(2,1)} %get-tuple-element.43), channel_id=1, source_target_pairs={{0,254},{2,240},{4,242},{6,244},{8,246},{10,248},{12,250},{14,252}... | collective-permute-start | bytes 110600 | tf_op jit(solution)/shard_map/ppermute | solution.py:411
  22.2 1.0 copy-start.1
  23.2 0.9 copy-start.3
  24.2 0.9 copy-start.6
  25.1 0.9 copy-start.12
  26.0 0.9 copy-start.14
  26.9 3.8 %copy-start.4 = (bf16[192,576]{1,0:T(8,128)(2,1)S(1)}, bf16[192,576]{1,0:T(8,128)(2,1)}, u32[]{:S(2)}) copy-start(bf16[192,576]{1,0:T(8,128)(2,1)} %copy-done.2) | copy-start | bytes 663556
  41.6 0.8 copy-start.7
  42.4 0.8 copy-start.9
  43.8 0.7 copy-start.17
  44.5 28.4 %copy-start.16 = (bf16[2,2,3,24,192]{4,3,2,1,0:T(8,128)(2,1)S(1)}, bf16[2,2,3,24,192]{4,3,2,1,0:T(8,128)(2,1)}, u32[]{:S(2)}) copy-start(bf16[2,2,3,24,192]{4,3,2,1,0:T(8,128)(2,1)} %copy-done.15) | copy-start | bytes 331780
  44.5 2.7 %collective-permute-start.4 = (bf16[16,64,128]{2,1,0:T(8,128)(2,1)S(1)}, bf16[16,64,128]{2,1,0:T(8,128)(2,1)S(1)}, u32[]{:S(2)}, u32[]{:S(2)}) collective-permute-start(bf16[16,64,128]{2,1,0:T(8,128)(2,1)S(1)} %get-tuple-element.60), channel_id=1, source_target_pairs={{0,1},{1,0},{2,3},{3,2},{4,5},{5,4},{6,7},{7,6},{8,9},{9,8},{10,11... | collective-permute-start | bytes 786440 | tf_op jit(solution)/shard_map/ppermute | solution.py:411
  47.2 52.1 %copy-start.8 = (bf16[2,18,24,192]{3,2,1,0:T(8,128)(2,1)S(1)}, bf16[2,18,24,192]{3,2,1,0:T(8,128)(2,1)}, u32[]{:S(2)}) copy-start(bf16[2,18,24,192]{3,2,1,0:T(8,128)(2,1)} %copy-done.7) | copy-start | bytes 995332
  47.2 52.1 %copy-start.10 = (bf16[2,18,24,192]{3,2,1,0:T(8,128)(2,1)S(1)}, bf16[2,18,24,192]{3,2,1,0:T(8,128)(2,1)}, u32[]{:S(2)}) copy-start(bf16[2,18,24,192]{3,2,1,0:T(8,128)(2,1)} %copy-done.9) | copy-start | bytes 995332
  48.0 12.7 %all-to-all-start = ((bf16[16,64,128]{2,1,0:T(8,128)(2,1)}), bf16[16,64,128]{2,1,0:T(8,128)(2,1)S(1)}, u32[]{:S(2)}, u32[]{:S(2)}) async-start(bf16[16,64,128]{2,1,0:T(8,128)(2,1)} %shard_map.121), calls=%async_computation | async-start | bytes 524288 | tf_op jit(solution)/shard_map/all_to_all | solution.py:495
  51.5 16.0 %collective-permute-start.3 = (bf16[2,2,18,8,192]{4,3,2,1,0:T(8,128)(2,1)}, bf16[2,2,18,8,192]{4,3,2,1,0:T(8,128)(2,1)S(1)}, u32[]{:S(2)}, u32[]{:S(2)}) collective-permute-start(bf16[2,2,18,8,192]{4,3,2,1,0:T(8,128)(2,1)} %copy-done.17), channel_id=1, source_target_pairs={{0,16},{16,32},{32,48},{48,64},{64,80},{80,96},{96,112},{112,128},... | collective-permute-start | bytes 663560 | tf_op jit(solution)/shard_map/ppermute | solution.py:411
  61.4 11.5 %all-to-all-start.1 = ((bf16[8,64,128]{2,1,0:T(8,128)(2,1)}), bf16[8,64,128]{2,1,0:T(8,128)(2,1)S(1)}, u32[]{:S(2)}, u32[]{:S(2)}) async-start(bf16[8,64,128]{2,1,0:T(8,128)(2,1)} %shard_map.122), calls=%async_computation.1 | async-start | bytes 262144 | tf_op jit(solution)/shard_map/all_to_all | solution.py:498
  73.9 19.8 %all-to-all-start.2 = ((bf16[16,168,128]{2,1,0:T(8,128)(2,1)}), bf16[16,168,128]{2,1,0:T(8,128)(2,1)S(1)}, u32[]{:S(2)}, u32[]{:S(2)}) async-start(bf16[16,168,128]{2,1,0:T(8,128)(2,1)} %get-tuple-element.62), calls=%async_computation.2 | async-start | bytes 1376256 | tf_op jit(solution)/shard_map/all_to_all | solution.py:505
  78.7 10.0 %collective-permute-start.5 = (bf16[2,2,3,24,192]{4,3,2,1,0:T(8,128)(2,1)S(1)}, bf16[2,2,3,24,192]{4,3,2,1,0:T(8,128)(2,1)S(1)}, u32[]{:S(2)}, u32[]{:S(2)}) collective-permute-start(bf16[2,2,3,24,192]{4,3,2,1,0:T(8,128)(2,1)S(1)} %get-tuple-element.63), channel_id=1, source_target_pairs={{0,2},{2,4},{4,6},{6,8},{8,10},{10,12},{12,14},{14,0},{1,3},{3,5},... | collective-permute-start | bytes 331784 | tf_op jit(solution)/shard_map/ppermute | solution.py:411
  93.6 7.5 %collective-permute-start.6 = (bf16[16,168,128]{2,1,0:T(8,128)(2,1)S(1)}, bf16[16,168,128]{2,1,0:T(8,128)(2,1)S(1)}, u32[]{:S(2)}, u32[]{:S(2)}) collective-permute-start(bf16[16,168,128]{2,1,0:T(8,128)(2,1)S(1)} %all-to-all-done.2.mine_ref), channel_id=1, source_target_pairs={{0,1},{1,0},{2,3},{3,2},{4,5},{5,4},{6,7},{7,6},{8,9},{9,8},{10,11... | collective-permute-start | bytes 2064392 | tf_op jit(solution)/shard_map/ppermute | solution.py:411
  (4 other events, 2.6 us)

commit v6 on v4

--- a/solution.py
+++ b/solution.py
@@ -54,8 +54,9 @@
     return ((iota((96, 96), 1) == (n & 15) * 8 + (n >> 4)) & ((n & 15) < AB)).astype(BF16)
 
 
-def strips_kernel(x_ref, y_ref, lon_ref, lat_ref, cor_ref):
-    for k, ref in enumerate((x_ref, y_ref)):
+def strips_kernel(x_ref, y_ref, lon_ref, lat_ref, cor_ref, x_out, y_out):
+    for k, (ref, copy) in enumerate(((x_ref, x_out), (y_ref, y_out))):
+        copy[...] = ref[...]
         lon_ref[k] = ref[:, :, 0:8, :]
         lat_ref[k] = ref[:, 0:3, :, :]
         cor_ref[k] = ref[:, 0:3, 0:8, :]
@@ -225,7 +226,7 @@
     got = interleaved(windows(weights, (grads, outer, gain_acc), save), ext, [(0, 0), (1, 0)])
     for v in range(2):
         for k in range(2):
-            rows_ref[k, v] = got[v, 0][k]
+            rows_ref[k, v] = got[v, 0][k].astype(BF16)
 
 
 def main_kernel(
@@ -258,7 +259,7 @@
     )
     for v in range(TAB):
         for k in range(2):
-            first = rows_in[k, v] if v < 2 else got[v, 0][k]
+            first = rows_in[k, v].astype(F32) if v < 2 else got[v, 0][k]
             ext[k, :, 6 * v + 3 : 6 * v + 9] = (first + got[v, 1][k]).reshape(2, 6, 32, C)
     for k, ref in enumerate((out_ref, ig_ref)):
         ext[k, :, 0:3] = jnp.zeros((2, 3, 32, C), F32)
@@ -442,7 +443,7 @@
 
 
 SUMS = [
-    ((2, 2, 384, C), F32),
+    ((2, 2, 384, C), BF16),
     ((C, 3 * C), F32),
     ((C, C), F32),
     ((C, POINTS), F32),
@@ -454,7 +455,8 @@
     weights = (
         near(regions), near(gain), project_in, near(win_t), project_out, near(wout_t), near(bias),
     )
-    inner = call(inner_kernel, SUMS, (x, y, *weights), [((2, 2, 15, 32, C), F32)], 50)
+    x, y = near(x), near(y)
+    inner = call(inner_kernel, SUMS, (x, y, *weights), [((2, 2, 15, 32, C), F32)], 48)
     return call(
         main_kernel,
         [((2, 18, 24, C), BF16)] * 2 + STRIPS[:2] + [((16, CHUNK, 128), F32), ((16, CHUNK, 128), BF16)],
@@ -471,7 +473,7 @@
             ((32 * T_ROWS, 128), F32),
             ((2, 16, CHUNK, 128), F32),
         ],
-        46,
+        44,
     )
 
 
@@ -479,7 +481,8 @@
     x, y = inputs[0], cotangent[0]
     lat = lax.axis_index("lat").astype(I32).reshape(1)
     me = lax.axis_index("ens").astype(I32).reshape(1)
-    strips = halo(*call(strips_kernel, STRIPS, (x, y), (), 56), -1)
+    *strips, x, y = call(strips_kernel, STRIPS + [((2, 18, 24, C), BF16)] * 2, (x, y), (), 56)
+    strips = halo(*strips, -1)
     bias, win_t, wout_t, gain, regions = run_shadow(lat, bias_table, norm_gain, project_in, project_out, mask_ids)
     out, in_grad, lon_s, lat_s, keep, send = run_main(
         me, x, y, strips, regions, gain, project_in, win_t, project_out, wout_t, bias

time: 93.7 us -> 93.2 us (level)
  transfers between devices with their start and end apart: 10 -> 10, of which waited for: 7 -> 7; matrix products, arithmetic and copies ran while one was open for 0% -> 0% of each run, Pallas kernels for 12% -> 11%
where the time goes in v6:
time: 93.2 us; the launch traced here: 92.7 us
  starting transfers between devices  34.7 us (37%)
  waiting for transfers between devices  30.8 us (33%)
  Pallas kernels  26.6 us (29%)
    pallas_call x9, Pallas kernels, call(): pl.pallas_call(kernel, out_shape=shapes, in_specs=specs, out_specs=tuple(...  26.6 us
    ppermute x7, starting transfers between devices, passed(): return lax.ppermute(x, axes, pairs)  22.6 us
    ppermute x7, waiting for transfers between devices, passed(): return lax.ppermute(x, axes, pairs)  13.2 us
    all_to_all x1, waiting for transfers between devices, local(): part = lax.all_to_all(part, 'lon', 0, 0, tiled=True)  7.95 us
    all_to_all x1, waiting for transfers between devices, local(): mine = lax.all_to_all(part, 'lon', 0, 0, tiled=True)  5.17 us
    all_to_all x1, starting transfers between devices, local(): mine = lax.all_to_all(part, 'lon', 0, 0, tiled=True)  4.97 us
    all_to_all x1, waiting for transfers between devices, local(): part = lax.all_to_all(part, 'lat', 0, 0, tiled=True)  4.5 us
    all_to_all x1, starting transfers between devices, local(): part = lax.all_to_all(part, 'lat', 0, 0, tiled=True)  3.58 us
  transfers between devices with their start and end apart: 10, of which 7 were waited for; matrix products, arithmetic and copies ran while one was open for 0% of the time, Pallas kernels for 11%

profile of v6, /device:TPU:1, one launch (start us, length us, event | category | flops | bytes accessed | tf_op | source)
XLA Modules:
  0.0 92.7 jit_solution(8907804877651270851)
XLA Ops:
  0.6 1.2 %shard_map.118 = (bf16[2,2,18,8,192]{4,3,2,1,0:T(8,128)(2,1)S(1)}, bf16[2,2,3,24,192]{4,3,2,1,0:T(8,128)(2,1)S(1)}, bf16[2,2,3,8,192]{4,3,2,1,0:T(8,128)(2,1)S(1...) custom-call(bf16[2,18,24,192]{3,2,1,0:T(8,128)(2,1)} %bitcast.12, bf16[2,18,24,192]{3,2,1,0:T(8,128)(2,1)} %bitcast.13), custom_call_target="tpu_custom_call" | custom-call | tf_op jit(solution)/shard_map/pallas_call | solution.py:385
  1.9 7.4 %collective-permute-start = (bf16[2,2,18,8,192]{4,3,2,1,0:T(8,128)(2,1)S(1)}, bf16[2,2,18,8,192]{4,3,2,1,0:T(8,128)(2,1)S(1)}, u32[]{:S(2)}, u32[]{:S(2)}) collective-permute-start(bf16[2,2,18,8,192]{4,3,2,1,0:T(8,128)(2,1)S(1)} %get-tuple-element.39), channel_id=1, source_target_pairs={{0,240},{16,0},{32,16},{48,32},{64,48},{80,64},{96,80},{112,96},{1... | collective-permute-start | bytes 663560 | tf_op jit(solution)/shard_map/ppermute | solution.py:411
  9.3 4.9 %collective-permute-start.1 = (bf16[2,2,3,24,192]{4,3,2,1,0:T(8,128)(2,1)S(1)}, bf16[2,2,3,24,192]{4,3,2,1,0:T(8,128)(2,1)S(1)}, u32[]{:S(2)}, u32[]{:S(2)}) collective-permute-start(bf16[2,2,3,24,192]{4,3,2,1,0:T(8,128)(2,1)S(1)} %get-tuple-element.40), channel_id=1, source_target_pairs={{0,14},{2,0},{4,2},{6,4},{8,6},{10,8},{12,10},{14,12},{1,15},{3,1}... | collective-permute-start | bytes 331784 | tf_op jit(solution)/shard_map/ppermute | solution.py:411
  14.9 4.2 %shard_map.119 = (f32[18,144,144]{2,1,0:T(8,128)S(1)}, bf16[576,192]{1,0:T(8,128)(2,1)S(1)}, bf16[192,192]{1,0:T(8,128)(2,1)S(1)}, f32[192,144]{1,0:T(8,128)S(1)}, f32[3,2,1,144]{3,2,1,0:T(1,128)S(1)}) custom-call(s32[1]{0:T(128)} %bitcast.3.lat_ref, f32[6,24,3312]{2,1,0:T(8,128)} %bitcast.11, f32[1,192]{1,0:T(1,128)} %bitcast.15, bf16[192,576]{1,0:T(8,128)(2,1)} %win_ref.5, ...), custom_call_target="tpu_custom_call" | custom-call | tf_op jit(solution)/shard_map/pallas_call | solution.py:385
  19.0 4.8 %shard_map.120 = (bf16[2,2,384,192]{3,2,1,0:T(8,128)(2,1)S(1)}, f32[192,576]{1,0:T(8,128)S(1)}, f32[192,192]{1,0:T(8,128)S(1)}, f32[192,144]{1,0:T(8,128)S(1)}, f32[12,144,144]{2,1,0:T(8,128)S(1)}) custom-call(bf16[2,18,24,192]{3,2,1,0:T(8,128)(2,1)S(1)} %get-tuple-element.37.x_ref, bf16[2,18,24,192]{3,2,1,0:T(8,128)(2,1)S(1)} %get-tuple-element.38.y_ref, ...), custom_call_target="tpu_custom_call" | custom-call | tf_op jit(solution)/shard_map/pallas_call | solution.py:385
  23.9 10.8 %shard_map.121 = (bf16[2,18,24,192]{3,2,1,0:T(8,128)(2,1)S(1)}, bf16[2,18,24,192]{3,2,1,0:T(8,128)(2,1)S(1)}, bf16[2,2,18,8,192]{4,3,2,1,0:T(8,128)(2,1)S(1)}, b...) custom-call(s32[1]{0:T(128)} %bitcast.ens_ref, ...), custom_call_target="tpu_custom_call" | custom-call | tf_op jit(solution)/shard_map/pallas_call | solution.py:385
  34.7 1.6 %collective-permute-start.4 = (bf16[16,64,128]{2,1,0:T(8,128)(2,1)S(1)}, bf16[16,64,128]{2,1,0:T(8,128)(2,1)S(1)}, u32[]{:S(2)}, u32[]{:S(2)}) collective-permute-start(bf16[16,64,128]{2,1,0:T(8,128)(2,1)S(1)} %get-tuple-element.56), channel_id=1, source_target_pairs={{0,1},{1,0},{2,3},{3,2},{4,5},{5,4},{6,7},{7,6},{8,9},{9,8},{10,11... | collective-permute-start | bytes 786440 | tf_op jit(solution)/shard_map/ppermute | solution.py:411
  36.3 1.2 %collective-permute-done.4.got_ref = bf16[16,64,128]{2,1,0:T(8,128)(2,1)S(1)} collective-permute-done((bf16[16,64,128]{2,1,0:T(8,128)(2,1)S(1)}, bf16[16,64,128]{2,1,0:T(8,128)(2,1)S(1)}, u32[]{:S(2)}, u32[]{:S(2)}) %collective-permute-start.4) | collective-permute-done | bytes 262176 | tf_op jit(solution)/shard_map/ppermute | solution.py:411
  37.5 0.8 shard_map.122
  38.2 3.5 %all-to-all-start = ((bf16[16,64,128]{2,1,0:T(8,128)(2,1)}), bf16[16,64,128]{2,1,0:T(8,128)(2,1)S(1)}, u32[]{:S(2)}, u32[]{:S(2)}) async-start(bf16[16,64,128]{2,1,0:T(8,128)(2,1)} %shard_map.122), calls=%async_computation | async-start | bytes 524288 | tf_op jit(solution)/shard_map/all_to_all | solution.py:492
  41.8 1.2 %collective-permute-start.3 = (bf16[2,2,18,8,192]{4,3,2,1,0:T(8,128)(2,1)S(1)}, bf16[2,2,18,8,192]{4,3,2,1,0:T(8,128)(2,1)S(1)}, u32[]{:S(2)}, u32[]{:S(2)}) collective-permute-start(bf16[2,2,18,8,192]{4,3,2,1,0:T(8,128)(2,1)S(1)} %get-tuple-element.54), channel_id=1, source_target_pairs={{0,16},{16,32},{32,48},{48,64},{64,80},{80,96},{96,112},{112,128},... | collective-permute-start | bytes 663560 | tf_op jit(solution)/shard_map/ppermute | solution.py:411
  43.0 7.9 %all-to-all-done.got_ref = bf16[16,64,128]{2,1,0:T(8,128)(2,1)S(1)} async-done(((bf16[16,64,128]{2,1,0:T(8,128)(2,1)}), bf16[16,64,128]{2,1,0:T(8,128)(2,1)S(1)}, u32[]{:S(2)}, u32[]{:S(2)}) %all-to-all-start) | async-done | bytes 262176 | tf_op jit(solution)/shard_map/all_to_all | solution.py:492
  51.7 3.6 %all-to-all-start.1 = ((bf16[8,64,128]{2,1,0:T(8,128)(2,1)}), bf16[8,64,128]{2,1,0:T(8,128)(2,1)S(1)}, u32[]{:S(2)}, u32[]{:S(2)}) async-start(bf16[8,64,128]{2,1,0:T(8,128)(2,1)} %shard_map.123), calls=%async_computation.1 | async-start | bytes 262144 | tf_op jit(solution)/shard_map/all_to_all | solution.py:495
  55.2 2.6 %collective-permute-done.3.lon_ref = bf16[2,2,18,8,192]{4,3,2,1,0:T(8,128)(2,1)S(1)} collective-permute-done((bf16[2,2,18,8,192]{4,3,2,1,0:T(8,128)(2,1)S(1)}, bf16[2,2,18,8,192]{4,3,2,1,0:T(8,128)(2,1)S(1)}, u32[]{:S(2)}, u32[]{:S(2)}) %collective-permute-start.3) | collective-permute-done | bytes 221216 | tf_op jit(solution)/shard_map/ppermute | solution.py:411
  57.8 4.5 %all-to-all-done.1.got_ref = bf16[8,64,128]{2,1,0:T(8,128)(2,1)S(1)} async-done(((bf16[8,64,128]{2,1,0:T(8,128)(2,1)}), bf16[8,64,128]{2,1,0:T(8,128)(2,1)S(1)}, u32[]{:S(2)}, u32[]{:S(2)}) %all-to-all-start.1) | async-done | bytes 131104 | tf_op jit(solution)/shard_map/all_to_all | solution.py:495
  62.3 0.9 %shard_map.124 = (bf16[16,168,128]{2,1,0:T(8,128)(2,1)}, bf16[2,2,3,24,192]{4,3,2,1,0:T(8,128)(2,1)S(1)}) custom-call(bf16[8,64,128]{2,1,0:T(8,128)(2,1)S(1)} %all-to-all-done.1.got_ref, bf16[2,2,18,8,192]{4,3,2,1,0:T(8,128)(2,1)S(1)} %collective-permute-done.3.lon_ref, bf16[2,2,3,24,192]{4,3,2,1,0:T(8,128)(2,1)S(1)} %get-tuple-element.57.lat_ref), custom_call_target="tpu_custom_call" | custom-call | tf_op jit(solution)/shard_map/pallas_call | solution.py:385
  63.2 5.0 %all-to-all-start.2 = ((bf16[16,168,128]{2,1,0:T(8,128)(2,1)}), bf16[16,168,128]{2,1,0:T(8,128)(2,1)S(1)}, u32[]{:S(2)}, u32[]{:S(2)}) async-start(bf16[16,168,128]{2,1,0:T(8,128)(2,1)} %get-tuple-element.58), calls=%async_computation.2 | async-start | bytes 1376256 | tf_op jit(solution)/shard_map/all_to_all | solution.py:502
  68.2 1.4 %collective-permute-start.5 = (bf16[2,2,3,24,192]{4,3,2,1,0:T(8,128)(2,1)S(1)}, bf16[2,2,3,24,192]{4,3,2,1,0:T(8,128)(2,1)S(1)}, u32[]{:S(2)}, u32[]{:S(2)}) collective-permute-start(bf16[2,2,3,24,192]{4,3,2,1,0:T(8,128)(2,1)S(1)} %get-tuple-element.59), channel_id=1, source_target_pairs={{0,2},{2,4},{4,6},{6,8},{8,10},{10,12},{12,14},{14,0},{1,3},{3,5},... | collective-permute-start | bytes 331784 | tf_op jit(solution)/shard_map/ppermute | solution.py:411
  69.6 8.6 %collective-permute-done.5.lat_ref = bf16[2,2,3,24,192]{4,3,2,1,0:T(8,128)(2,1)S(1)} collective-permute-done((bf16[2,2,3,24,192]{4,3,2,1,0:T(8,128)(2,1)S(1)}, bf16[2,2,3,24,192]{4,3,2,1,0:T(8,128)(2,1)S(1)}, u32[]{:S(2)}, u32[]{:S(2)}) %collective-permute-start.5) | collective-permute-done | bytes 110624 | tf_op jit(solution)/shard_map/ppermute | solution.py:411
  78.2 5.2 %all-to-all-done.2.mine_ref = bf16[16,168,128]{2,1,0:T(8,128)(2,1)S(1)} async-done(((bf16[16,168,128]{2,1,0:T(8,128)(2,1)}), bf16[16,168,128]{2,1,0:T(8,128)(2,1)S(1)}, u32[]{:S(2)}, u32[]{:S(2)}) %all-to-all-start.2) | async-done | bytes 688160 | tf_op jit(solution)/shard_map/all_to_all | solution.py:502
  83.4 5.4 %collective-permute-start.6 = (bf16[16,168,128]{2,1,0:T(8,128)(2,1)S(1)}, bf16[16,168,128]{2,1,0:T(8,128)(2,1)S(1)}, u32[]{:S(2)}, u32[]{:S(2)}) collective-permute-start(bf16[16,168,128]{2,1,0:T(8,128)(2,1)S(1)} %all-to-all-done.2.mine_ref), channel_id=1, source_target_pairs={{0,1},{1,0},{2,3},{3,2},{4,5},{5,4},{6,7},{7,6},{8,9},{9,8},{10,11... | collective-permute-start | bytes 2064392 | tf_op jit(solution)/shard_map/ppermute | solution.py:411
  88.8 1.0 %shard_map.125 = (bf16[2,18,24,192]{3,2,1,0:T(8,128)(2,1)}, bf16[2,18,24,192]{3,2,1,0:T(8,128)(2,1)}) custom-call(bf16[2,18,24,192]{3,2,1,0:T(8,128)(2,1)S(1)} %get-tuple-element.52.out_ref, bf16[2,18,24,192]{3,2,1,0:T(8,128)(2,1)S(1)} %get-tuple-element.53.grad_ref, bf16[2,2,18,8,192]{4,3,2,1,0:T(8,128)(2,1)S(1)} %collective-permute-done.3.lon_ref, ...), custom_call_target="tpu_custom_call" | custom-call | tf_op jit(solution)/shard_map/pallas_call | solution.py:385
  89.8 0.8 collective-permute-done.6.other_ref
  90.6 2.2 %shard_map.126 = (f32[192,576]{1,0:T(8,128)}, f32[192,192]{1,0:T(8,128)}, f32[1,192]{1,0:T(1,128)}, f32[6,24,3312]{2,1,0:T(8,128)}) custom-call(s32[1]{0:T(128)} %bitcast.ens_ref, bf16[16,168,128]{2,1,0:T(8,128)(2,1)S(1)} %all-to-all-done.2.mine_ref, bf16[16,168,128]{2,1,0:T(8,128)(2,1)S(1)} %collective-permute-done.6.other_ref), custom_call_target="tpu_custom_call" | custom-call | tf_op jit(solution)/shard_map/pallas_call | solution.py:385
  (7 shorter events, 1.4 us)
Async XLA Ops:
  1.9 22.0 %collective-permute-start = (bf16[2,2,18,8,192]{4,3,2,1,0:T(8,128)(2,1)S(1)}, bf16[2,2,18,8,192]{4,3,2,1,0:T(8,128)(2,1)S(1)}, u32[]{:S(2)}, u32[]{:S(2)}) collective-permute-start(bf16[2,2,18,8,192]{4,3,2,1,0:T(8,128)(2,1)S(1)} %get-tuple-element.39), channel_id=1, source_target_pairs={{0,240},{16,0},{32,16},{48,32},{64,48},{80,64},{96,80},{112,96},{1... | collective-permute-start | bytes 663560 | tf_op jit(solution)/shard_map/ppermute | solution.py:411
  9.3 14.6 %collective-permute-start.1 = (bf16[2,2,3,24,192]{4,3,2,1,0:T(8,128)(2,1)S(1)}, bf16[2,2,3,24,192]{4,3,2,1,0:T(8,128)(2,1)S(1)}, u32[]{:S(2)}, u32[]{:S(2)}) collective-permute-start(bf16[2,2,3,24,192]{4,3,2,1,0:T(8,128)(2,1)S(1)} %get-tuple-element.40), channel_id=1, source_target_pairs={{0,14},{2,0},{4,2},{6,4},{8,6},{10,8},{12,10},{14,12},{1,15},{3,1}... | collective-permute-start | bytes 331784 | tf_op jit(solution)/shard_map/ppermute | solution.py:411
  14.2 9.7 %collective-permute-start.2 = (bf16[2,2,3,8,192]{4,3,2,1,0:T(8,128)(2,1)S(1)}, bf16[2,2,3,8,192]{4,3,2,1,0:T(8,128)(2,1)S(1)}, u32[]{:S(2)}, u32[]{:S(2)}) collective-permute-start(bf16[2,2,3,8,192]{4,3,2,1,0:T(8,128)(2,1)S(1)} %get-tuple-element.41), channel_id=1, source_target_pairs={{0,254},{2,240},{4,242},{6,244},{8,246},{10,248},{12,250},{14,252}... | collective-permute-start | bytes 110600 | tf_op jit(solution)/shard_map/ppermute | solution.py:411
  19.0 4.8 %copy-start = (bf16[192,192]{1,0:T(8,128)(2,1)S(1)}, bf16[192,192]{1,0:T(8,128)(2,1)}, u32[]{:S(2)}) copy-start(bf16[192,192]{1,0:T(8,128)(2,1)} %wout_ref.5) | copy-start | bytes 221188
  34.7 2.8 %collective-permute-start.4 = (bf16[16,64,128]{2,1,0:T(8,128)(2,1)S(1)}, bf16[16,64,128]{2,1,0:T(8,128)(2,1)S(1)}, u32[]{:S(2)}, u32[]{:S(2)}) collective-permute-start(bf16[16,64,128]{2,1,0:T(8,128)(2,1)S(1)} %get-tuple-element.56), channel_id=1, source_target_pairs={{0,1},{1,0},{2,3},{3,2},{4,5},{5,4},{6,7},{7,6},{8,9},{9,8},{10,11... | collective-permute-start | bytes 786440 | tf_op jit(solution)/shard_map/ppermute | solution.py:411
  38.2 12.7 %all-to-all-start = ((bf16[16,64,128]{2,1,0:T(8,128)(2,1)}), bf16[16,64,128]{2,1,0:T(8,128)(2,1)S(1)}, u32[]{:S(2)}, u32[]{:S(2)}) async-start(bf16[16,64,128]{2,1,0:T(8,128)(2,1)} %shard_map.122), calls=%async_computation | async-start | bytes 524288 | tf_op jit(solution)/shard_map/all_to_all | solution.py:492
  41.8 16.0 %collective-permute-start.3 = (bf16[2,2,18,8,192]{4,3,2,1,0:T(8,128)(2,1)S(1)}, bf16[2,2,18,8,192]{4,3,2,1,0:T(8,128)(2,1)S(1)}, u32[]{:S(2)}, u32[]{:S(2)}) collective-permute-start(bf16[2,2,18,8,192]{4,3,2,1,0:T(8,128)(2,1)S(1)} %get-tuple-element.54), channel_id=1, source_target_pairs={{0,16},{16,32},{32,48},{48,64},{64,80},{80,96},{96,112},{112,128},... | collective-permute-start | bytes 663560 | tf_op jit(solution)/shard_map/ppermute | solution.py:411
  51.7 10.6 %all-to-all-start.1 = ((bf16[8,64,128]{2,1,0:T(8,128)(2,1)}), bf16[8,64,128]{2,1,0:T(8,128)(2,1)S(1)}, u32[]{:S(2)}, u32[]{:S(2)}) async-start(bf16[8,64,128]{2,1,0:T(8,128)(2,1)} %shard_map.123), calls=%async_computation.1 | async-start | bytes 262144 | tf_op jit(solution)/shard_map/all_to_all | solution.py:495
  63.2 20.2 %all-to-all-start.2 = ((bf16[16,168,128]{2,1,0:T(8,128)(2,1)}), bf16[16,168,128]{2,1,0:T(8,128)(2,1)S(1)}, u32[]{:S(2)}, u32[]{:S(2)}) async-start(bf16[16,168,128]{2,1,0:T(8,128)(2,1)} %get-tuple-element.58), calls=%async_computation.2 | async-start | bytes 1376256 | tf_op jit(solution)/shard_map/all_to_all | solution.py:502
  68.2 10.0 %collective-permute-start.5 = (bf16[2,2,3,24,192]{4,3,2,1,0:T(8,128)(2,1)S(1)}, bf16[2,2,3,24,192]{4,3,2,1,0:T(8,128)(2,1)S(1)}, u32[]{:S(2)}, u32[]{:S(2)}) collective-permute-start(bf16[2,2,3,24,192]{4,3,2,1,0:T(8,128)(2,1)S(1)} %get-tuple-element.59), channel_id=1, source_target_pairs={{0,2},{2,4},{4,6},{6,8},{8,10},{10,12},{12,14},{14,0},{1,3},{3,5},... | collective-permute-start | bytes 331784 | tf_op jit(solution)/shard_map/ppermute | solution.py:411
  83.4 7.2 %collective-permute-start.6 = (bf16[16,168,128]{2,1,0:T(8,128)(2,1)S(1)}, bf16[16,168,128]{2,1,0:T(8,128)(2,1)S(1)}, u32[]{:S(2)}, u32[]{:S(2)}) collective-permute-start(bf16[16,168,128]{2,1,0:T(8,128)(2,1)S(1)} %all-to-all-done.2.mine_ref), channel_id=1, source_target_pairs={{0,1},{1,0},{2,3},{3,2},{4,5},{5,4},{6,7},{7,6},{8,9},{9,8},{10,11... | collective-permute-start | bytes 2064392 | tf_op jit(solution)/shard_map/ppermute | solution.py:411

commit v7 on v6

--- a/solution.py
+++ b/solution.py
@@ -16,7 +16,7 @@
 TAB = 3
 ENTRIES = AB * AB * SPAN
 LANE_BLOCKS = -(-ENTRIES // 128)
-CHUNK = 64
+CHUNK = 56
 G_ROWS = 40
 T_ROWS = 16
 SHARD = 168

time: 93.2 us -> 92.3 us (level)
  transfers between devices with their start and end apart: 10 -> 10, of which waited for: 7 -> 7; matrix products, arithmetic and copies ran while one was open for 0% -> 0% of each run, Pallas kernels for 11% -> 12%
where the time goes in v7:
time: 92.3 us; the launch traced here: 91.8 us
  starting transfers between devices  34.7 us (38%)
  waiting for transfers between devices  29.9 us (32%)
  Pallas kernels  26.5 us (29%)
    pallas_call x9, Pallas kernels, call(): pl.pallas_call(kernel, out_shape=shapes, in_specs=specs, out_specs=tuple(...  26.5 us
    ppermute x7, starting transfers between devices, passed(): return lax.ppermute(x, axes, pairs)  22.6 us
    ppermute x7, waiting for transfers between devices, passed(): return lax.ppermute(x, axes, pairs)  13.2 us
    all_to_all x1, waiting for transfers between devices, local(): part = lax.all_to_all(part, 'lon', 0, 0, tiled=True)  7.33 us
    all_to_all x1, waiting for transfers between devices, local(): mine = lax.all_to_all(part, 'lon', 0, 0, tiled=True)  5.18 us
    all_to_all x1, starting transfers between devices, local(): mine = lax.all_to_all(part, 'lon', 0, 0, tiled=True)  5.11 us
    all_to_all x1, waiting for transfers between devices, local(): part = lax.all_to_all(part, 'lat', 0, 0, tiled=True)  4.22 us
    all_to_all x1, starting transfers between devices, local(): part = lax.all_to_all(part, 'lon', 0, 0, tiled=True)  3.53 us
  transfers between devices with their start and end apart: 10, of which 7 were waited for; matrix products, arithmetic and copies ran while one was open for 0% of the time, Pallas kernels for 12%

profile of v7, /device:TPU:1, one launch (start us, length us, event | category | flops | bytes accessed | tf_op | source)
XLA Modules:
  0.0 91.8 jit_solution(8973899552106681775)
XLA Ops:
  0.6 1.2 %shard_map.118 = (bf16[2,2,18,8,192]{4,3,2,1,0:T(8,128)(2,1)S(1)}, bf16[2,2,3,24,192]{4,3,2,1,0:T(8,128)(2,1)S(1)}, bf16[2,2,3,8,192]{4,3,2,1,0:T(8,128)(2,1)S(1...) custom-call(bf16[2,18,24,192]{3,2,1,0:T(8,128)(2,1)} %bitcast.12, bf16[2,18,24,192]{3,2,1,0:T(8,128)(2,1)} %bitcast.13), custom_call_target="tpu_custom_call" | custom-call | tf_op jit(solution)/shard_map/pallas_call | solution.py:385
  1.9 7.4 %collective-permute-start = (bf16[2,2,18,8,192]{4,3,2,1,0:T(8,128)(2,1)S(1)}, bf16[2,2,18,8,192]{4,3,2,1,0:T(8,128)(2,1)S(1)}, u32[]{:S(2)}, u32[]{:S(2)}) collective-permute-start(bf16[2,2,18,8,192]{4,3,2,1,0:T(8,128)(2,1)S(1)} %get-tuple-element.39), channel_id=1, source_target_pairs={{0,240},{16,0},{32,16},{48,32},{64,48},{80,64},{96,80},{112,96},{1... | collective-permute-start | bytes 663560 | tf_op jit(solution)/shard_map/ppermute | solution.py:411
  9.3 4.9 %collective-permute-start.1 = (bf16[2,2,3,24,192]{4,3,2,1,0:T(8,128)(2,1)S(1)}, bf16[2,2,3,24,192]{4,3,2,1,0:T(8,128)(2,1)S(1)}, u32[]{:S(2)}, u32[]{:S(2)}) collective-permute-start(bf16[2,2,3,24,192]{4,3,2,1,0:T(8,128)(2,1)S(1)} %get-tuple-element.40), channel_id=1, source_target_pairs={{0,14},{2,0},{4,2},{6,4},{8,6},{10,8},{12,10},{14,12},{1,15},{3,1}... | collective-permute-start | bytes 331784 | tf_op jit(solution)/shard_map/ppermute | solution.py:411
  14.9 4.2 %shard_map.119 = (f32[18,144,144]{2,1,0:T(8,128)S(1)}, bf16[576,192]{1,0:T(8,128)(2,1)S(1)}, bf16[192,192]{1,0:T(8,128)(2,1)S(1)}, f32[192,144]{1,0:T(8,128)S(1)}, f32[3,2,1,144]{3,2,1,0:T(1,128)S(1)}) custom-call(s32[1]{0:T(128)} %bitcast.3.lat_ref, f32[6,24,3312]{2,1,0:T(8,128)} %bitcast.11, f32[1,192]{1,0:T(1,128)} %bitcast.15, bf16[192,576]{1,0:T(8,128)(2,1)} %win_ref.5, ...), custom_call_target="tpu_custom_call" | custom-call | tf_op jit(solution)/shard_map/pallas_call | solution.py:385
  19.0 4.8 %shard_map.120 = (bf16[2,2,384,192]{3,2,1,0:T(8,128)(2,1)S(1)}, f32[192,576]{1,0:T(8,128)S(1)}, f32[192,192]{1,0:T(8,128)S(1)}, f32[192,144]{1,0:T(8,128)S(1)}, f32[12,144,144]{2,1,0:T(8,128)S(1)}) custom-call(bf16[2,18,24,192]{3,2,1,0:T(8,128)(2,1)S(1)} %get-tuple-element.37.x_ref, bf16[2,18,24,192]{3,2,1,0:T(8,128)(2,1)S(1)} %get-tuple-element.38.y_ref, ...), custom_call_target="tpu_custom_call" | custom-call | tf_op jit(solution)/shard_map/pallas_call | solution.py:385
  23.9 10.8 %shard_map.121 = (bf16[2,18,24,192]{3,2,1,0:T(8,128)(2,1)S(1)}, bf16[2,18,24,192]{3,2,1,0:T(8,128)(2,1)S(1)}, bf16[2,2,18,8,192]{4,3,2,1,0:T(8,128)(2,1)S(1)}, b...) custom-call(s32[1]{0:T(128)} %bitcast.ens_ref, ...), custom_call_target="tpu_custom_call" | custom-call | tf_op jit(solution)/shard_map/pallas_call | solution.py:385
  34.7 1.6 %collective-permute-start.4 = (bf16[16,56,128]{2,1,0:T(8,128)(2,1)S(1)}, bf16[16,56,128]{2,1,0:T(8,128)(2,1)S(1)}, u32[]{:S(2)}, u32[]{:S(2)}) collective-permute-start(bf16[16,56,128]{2,1,0:T(8,128)(2,1)S(1)} %get-tuple-element.56), channel_id=1, source_target_pairs={{0,1},{1,0},{2,3},{3,2},{4,5},{5,4},{6,7},{7,6},{8,9},{9,8},{10,11... | collective-permute-start | bytes 688136 | tf_op jit(solution)/shard_map/ppermute | solution.py:411
  36.3 1.1 %collective-permute-done.4.got_ref = bf16[16,56,128]{2,1,0:T(8,128)(2,1)S(1)} collective-permute-done((bf16[16,56,128]{2,1,0:T(8,128)(2,1)S(1)}, bf16[16,56,128]{2,1,0:T(8,128)(2,1)S(1)}, u32[]{:S(2)}, u32[]{:S(2)}) %collective-permute-start.4) | collective-permute-done | bytes 229408 | tf_op jit(solution)/shard_map/ppermute | solution.py:411
  37.4 0.7 shard_map.122
  38.1 3.5 %all-to-all-start = ((bf16[16,56,128]{2,1,0:T(8,128)(2,1)}), bf16[16,56,128]{2,1,0:T(8,128)(2,1)S(1)}, u32[]{:S(2)}, u32[]{:S(2)}) async-start(bf16[16,56,128]{2,1,0:T(8,128)(2,1)} %shard_map.122), calls=%async_computation | async-start | bytes 458752 | tf_op jit(solution)/shard_map/all_to_all | solution.py:492
  41.7 1.2 %collective-permute-start.3 = (bf16[2,2,18,8,192]{4,3,2,1,0:T(8,128)(2,1)S(1)}, bf16[2,2,18,8,192]{4,3,2,1,0:T(8,128)(2,1)S(1)}, u32[]{:S(2)}, u32[]{:S(2)}) collective-permute-start(bf16[2,2,18,8,192]{4,3,2,1,0:T(8,128)(2,1)S(1)} %get-tuple-element.54), channel_id=1, source_target_pairs={{0,16},{16,32},{32,48},{48,64},{64,80},{80,96},{96,112},{112,128},... | collective-permute-start | bytes 663560 | tf_op jit(solution)/shard_map/ppermute | solution.py:411
  42.9 7.3 %all-to-all-done.got_ref = bf16[16,56,128]{2,1,0:T(8,128)(2,1)S(1)} async-done(((bf16[16,56,128]{2,1,0:T(8,128)(2,1)}), bf16[16,56,128]{2,1,0:T(8,128)(2,1)S(1)}, u32[]{:S(2)}, u32[]{:S(2)}) %all-to-all-start) | async-done | bytes 229408 | tf_op jit(solution)/shard_map/all_to_all | solution.py:492
  50.9 3.4 %all-to-all-start.1 = ((bf16[8,56,128]{2,1,0:T(8,128)(2,1)}), bf16[8,56,128]{2,1,0:T(8,128)(2,1)S(1)}, u32[]{:S(2)}, u32[]{:S(2)}) async-start(bf16[8,56,128]{2,1,0:T(8,128)(2,1)} %shard_map.123), calls=%async_computation.1 | async-start | bytes 229376 | tf_op jit(solution)/shard_map/all_to_all | solution.py:495
  54.3 2.7 %collective-permute-done.3.lon_ref = bf16[2,2,18,8,192]{4,3,2,1,0:T(8,128)(2,1)S(1)} collective-permute-done((bf16[2,2,18,8,192]{4,3,2,1,0:T(8,128)(2,1)S(1)}, bf16[2,2,18,8,192]{4,3,2,1,0:T(8,128)(2,1)S(1)}, u32[]{:S(2)}, u32[]{:S(2)}) %collective-permute-start.3) | collective-permute-done | bytes 221216 | tf_op jit(solution)/shard_map/ppermute | solution.py:411
  57.0 4.2 %all-to-all-done.1.got_ref = bf16[8,56,128]{2,1,0:T(8,128)(2,1)S(1)} async-done(((bf16[8,56,128]{2,1,0:T(8,128)(2,1)}), bf16[8,56,128]{2,1,0:T(8,128)(2,1)S(1)}, u32[]{:S(2)}, u32[]{:S(2)}) %all-to-all-start.1) | async-done | bytes 114720 | tf_op jit(solution)/shard_map/all_to_all | solution.py:495
  61.2 0.9 %shard_map.124 = (bf16[16,168,128]{2,1,0:T(8,128)(2,1)}, bf16[2,2,3,24,192]{4,3,2,1,0:T(8,128)(2,1)S(1)}) custom-call(bf16[8,56,128]{2,1,0:T(8,128)(2,1)S(1)} %all-to-all-done.1.got_ref, bf16[2,2,18,8,192]{4,3,2,1,0:T(8,128)(2,1)S(1)} %collective-permute-done.3.lon_ref, bf16[2,2,3,24,192]{4,3,2,1,0:T(8,128)(2,1)S(1)} %get-tuple-element.57.lat_ref), custom_call_target="tpu_custom_call" | custom-call | tf_op jit(solution)/shard_map/pallas_call | solution.py:385
  62.2 5.1 %all-to-all-start.2 = ((bf16[16,168,128]{2,1,0:T(8,128)(2,1)}), bf16[16,168,128]{2,1,0:T(8,128)(2,1)S(1)}, u32[]{:S(2)}, u32[]{:S(2)}) async-start(bf16[16,168,128]{2,1,0:T(8,128)(2,1)} %get-tuple-element.58), calls=%async_computation.2 | async-start | bytes 1376256 | tf_op jit(solution)/shard_map/all_to_all | solution.py:502
  67.3 1.4 %collective-permute-start.5 = (bf16[2,2,3,24,192]{4,3,2,1,0:T(8,128)(2,1)S(1)}, bf16[2,2,3,24,192]{4,3,2,1,0:T(8,128)(2,1)S(1)}, u32[]{:S(2)}, u32[]{:S(2)}) collective-permute-start(bf16[2,2,3,24,192]{4,3,2,1,0:T(8,128)(2,1)S(1)} %get-tuple-element.59), channel_id=1, source_target_pairs={{0,2},{2,4},{4,6},{6,8},{8,10},{10,12},{12,14},{14,0},{1,3},{3,5},... | collective-permute-start | bytes 331784 | tf_op jit(solution)/shard_map/ppermute | solution.py:411
  68.7 8.6 %collective-permute-done.5.lat_ref = bf16[2,2,3,24,192]{4,3,2,1,0:T(8,128)(2,1)S(1)} collective-permute-done((bf16[2,2,3,24,192]{4,3,2,1,0:T(8,128)(2,1)S(1)}, bf16[2,2,3,24,192]{4,3,2,1,0:T(8,128)(2,1)S(1)}, u32[]{:S(2)}, u32[]{:S(2)}) %collective-permute-start.5) | collective-permute-done | bytes 110624 | tf_op jit(solution)/shard_map/ppermute | solution.py:411
  77.3 5.2 %all-to-all-done.2.mine_ref = bf16[16,168,128]{2,1,0:T(8,128)(2,1)S(1)} async-done(((bf16[16,168,128]{2,1,0:T(8,128)(2,1)}), bf16[16,168,128]{2,1,0:T(8,128)(2,1)S(1)}, u32[]{:S(2)}, u32[]{:S(2)}) %all-to-all-start.2) | async-done | bytes 688160 | tf_op jit(solution)/shard_map/all_to_all | solution.py:502
  82.5 5.4 %collective-permute-start.6 = (bf16[16,168,128]{2,1,0:T(8,128)(2,1)S(1)}, bf16[16,168,128]{2,1,0:T(8,128)(2,1)S(1)}, u32[]{:S(2)}, u32[]{:S(2)}) collective-permute-start(bf16[16,168,128]{2,1,0:T(8,128)(2,1)S(1)} %all-to-all-done.2.mine_ref), channel_id=1, source_target_pairs={{0,1},{1,0},{2,3},{3,2},{4,5},{5,4},{6,7},{7,6},{8,9},{9,8},{10,11... | collective-permute-start | bytes 2064392 | tf_op jit(solution)/shard_map/ppermute | solution.py:411
  87.9 1.0 %shard_map.125 = (bf16[2,18,24,192]{3,2,1,0:T(8,128)(2,1)}, bf16[2,18,24,192]{3,2,1,0:T(8,128)(2,1)}) custom-call(bf16[2,18,24,192]{3,2,1,0:T(8,128)(2,1)S(1)} %get-tuple-element.52.out_ref, bf16[2,18,24,192]{3,2,1,0:T(8,128)(2,1)S(1)} %get-tuple-element.53.grad_ref, bf16[2,2,18,8,192]{4,3,2,1,0:T(8,128)(2,1)S(1)} %collective-permute-done.3.lon_ref, ...), custom_call_target="tpu_custom_call" | custom-call | tf_op jit(solution)/shard_map/pallas_call | solution.py:385
  88.8 0.8 collective-permute-done.6.other_ref
  89.6 2.2 %shard_map.126 = (f32[192,576]{1,0:T(8,128)}, f32[192,192]{1,0:T(8,128)}, f32[1,192]{1,0:T(1,128)}, f32[6,24,3312]{2,1,0:T(8,128)}) custom-call(s32[1]{0:T(128)} %bitcast.ens_ref, bf16[16,168,128]{2,1,0:T(8,128)(2,1)S(1)} %all-to-all-done.2.mine_ref, bf16[16,168,128]{2,1,0:T(8,128)(2,1)S(1)} %collective-permute-done.6.other_ref), custom_call_target="tpu_custom_call" | custom-call | tf_op jit(solution)/shard_map/pallas_call | solution.py:385
  (7 shorter events, 1.4 us)
Async XLA Ops:
  1.9 22.0 %collective-permute-start = (bf16[2,2,18,8,192]{4,3,2,1,0:T(8,128)(2,1)S(1)}, bf16[2,2,18,8,192]{4,3,2,1,0:T(8,128)(2,1)S(1)}, u32[]{:S(2)}, u32[]{:S(2)}) collective-permute-start(bf16[2,2,18,8,192]{4,3,2,1,0:T(8,128)(2,1)S(1)} %get-tuple-element.39), channel_id=1, source_target_pairs={{0,240},{16,0},{32,16},{48,32},{64,48},{80,64},{96,80},{112,96},{1... | collective-permute-start | bytes 663560 | tf_op jit(solution)/shard_map/ppermute | solution.py:411
  9.3 14.6 %collective-permute-start.1 = (bf16[2,2,3,24,192]{4,3,2,1,0:T(8,128)(2,1)S(1)}, bf16[2,2,3,24,192]{4,3,2,1,0:T(8,128)(2,1)S(1)}, u32[]{:S(2)}, u32[]{:S(2)}) collective-permute-start(bf16[2,2,3,24,192]{4,3,2,1,0:T(8,128)(2,1)S(1)} %get-tuple-element.40), channel_id=1, source_target_pairs={{0,14},{2,0},{4,2},{6,4},{8,6},{10,8},{12,10},{14,12},{1,15},{3,1}... | collective-permute-start | bytes 331784 | tf_op jit(solution)/shard_map/ppermute | solution.py:411
  14.2 9.7 %collective-permute-start.2 = (bf16[2,2,3,8,192]{4,3,2,1,0:T(8,128)(2,1)S(1)}, bf16[2,2,3,8,192]{4,3,2,1,0:T(8,128)(2,1)S(1)}, u32[]{:S(2)}, u32[]{:S(2)}) collective-permute-start(bf16[2,2,3,8,192]{4,3,2,1,0:T(8,128)(2,1)S(1)} %get-tuple-element.41), channel_id=1, source_target_pairs={{0,254},{2,240},{4,242},{6,244},{8,246},{10,248},{12,250},{14,252}... | collective-permute-start | bytes 110600 | tf_op jit(solution)/shard_map/ppermute | solution.py:411
  19.0 4.8 %copy-start = (bf16[192,192]{1,0:T(8,128)(2,1)S(1)}, bf16[192,192]{1,0:T(8,128)(2,1)}, u32[]{:S(2)}) copy-start(bf16[192,192]{1,0:T(8,128)(2,1)} %wout_ref.5) | copy-start | bytes 221188
  34.7 2.7 %collective-permute-start.4 = (bf16[16,56,128]{2,1,0:T(8,128)(2,1)S(1)}, bf16[16,56,128]{2,1,0:T(8,128)(2,1)S(1)}, u32[]{:S(2)}, u32[]{:S(2)}) collective-permute-start(bf16[16,56,128]{2,1,0:T(8,128)(2,1)S(1)} %get-tuple-element.56), channel_id=1, source_target_pairs={{0,1},{1,0},{2,3},{3,2},{4,5},{5,4},{6,7},{7,6},{8,9},{9,8},{10,11... | collective-permute-start | bytes 688136 | tf_op jit(solution)/shard_map/ppermute | solution.py:411
  38.1 12.1 %all-to-all-start = ((bf16[16,56,128]{2,1,0:T(8,128)(2,1)}), bf16[16,56,128]{2,1,0:T(8,128)(2,1)S(1)}, u32[]{:S(2)}, u32[]{:S(2)}) async-start(bf16[16,56,128]{2,1,0:T(8,128)(2,1)} %shard_map.122), calls=%async_computation | async-start | bytes 458752 | tf_op jit(solution)/shard_map/all_to_all | solution.py:492
  41.7 15.3 %collective-permute-start.3 = (bf16[2,2,18,8,192]{4,3,2,1,0:T(8,128)(2,1)S(1)}, bf16[2,2,18,8,192]{4,3,2,1,0:T(8,128)(2,1)S(1)}, u32[]{:S(2)}, u32[]{:S(2)}) collective-permute-start(bf16[2,2,18,8,192]{4,3,2,1,0:T(8,128)(2,1)S(1)} %get-tuple-element.54), channel_id=1, source_target_pairs={{0,16},{16,32},{32,48},{48,64},{64,80},{80,96},{96,112},{112,128},... | collective-permute-start | bytes 663560 | tf_op jit(solution)/shard_map/ppermute | solution.py:411
  50.9 10.3 %all-to-all-start.1 = ((bf16[8,56,128]{2,1,0:T(8,128)(2,1)}), bf16[8,56,128]{2,1,0:T(8,128)(2,1)S(1)}, u32[]{:S(2)}, u32[]{:S(2)}) async-start(bf16[8,56,128]{2,1,0:T(8,128)(2,1)} %shard_map.123), calls=%async_computation.1 | async-start | bytes 229376 | tf_op jit(solution)/shard_map/all_to_all | solution.py:495
  62.2 20.3 %all-to-all-start.2 = ((bf16[16,168,128]{2,1,0:T(8,128)(2,1)}), bf16[16,168,128]{2,1,0:T(8,128)(2,1)S(1)}, u32[]{:S(2)}, u32[]{:S(2)}) async-start(bf16[16,168,128]{2,1,0:T(8,128)(2,1)} %get-tuple-element.58), calls=%async_computation.2 | async-start | bytes 1376256 | tf_op jit(solution)/shard_map/all_to_all | solution.py:502
  67.3 10.0 %collective-permute-start.5 = (bf16[2,2,3,24,192]{4,3,2,1,0:T(8,128)(2,1)S(1)}, bf16[2,2,3,24,192]{4,3,2,1,0:T(8,128)(2,1)S(1)}, u32[]{:S(2)}, u32[]{:S(2)}) collective-permute-start(bf16[2,2,3,24,192]{4,3,2,1,0:T(8,128)(2,1)S(1)} %get-tuple-element.59), channel_id=1, source_target_pairs={{0,2},{2,4},{4,6},{6,8},{8,10},{10,12},{12,14},{14,0},{1,3},{3,5},... | collective-permute-start | bytes 331784 | tf_op jit(solution)/shard_map/ppermute | solution.py:411
  82.5 7.2 %collective-permute-start.6 = (bf16[16,168,128]{2,1,0:T(8,128)(2,1)S(1)}, bf16[16,168,128]{2,1,0:T(8,128)(2,1)S(1)}, u32[]{:S(2)}, u32[]{:S(2)}) collective-permute-start(bf16[16,168,128]{2,1,0:T(8,128)(2,1)S(1)} %all-to-all-done.2.mine_ref), channel_id=1, source_target_pairs={{0,1},{1,0},{2,3},{3,2},{4,5},{5,4},{6,7},{7,6},{8,9},{9,8},{10,11... | collective-permute-start | bytes 2064392 | tf_op jit(solution)/shard_map/ppermute | solution.py:411
